TPU v7x, 32 devices: a whole 2x2x4 slice. The times are simulated.
32 devices in a mesh: shard: 8 (over z, y), tensor: 4 (over x, core).
Axes of the slice: x: 2, y: 2, z: 4, core: 2. Of those that a mesh axis runs over, the one named last changes fastest.
Arguments:
- gradient: float32 [384, 4, 3456], P('shard', 'tensor'), may hold values from -6 to 6
- weight: float32 [384, 4, 3456], P('shard', 'tensor'), may hold values from -0.3125 to 0.3125
- first_moment: float32 [384, 4, 3456], P('shard', 'tensor'), may hold values from -6 to 6
- second_moment: float32 [384, 4, 3456], P('shard', 'tensor'), may hold values from 0.3 to 3
- left_basis: float32 [384, 4, 960], P('shard', 'tensor')
- left_gram: float32 [384, 4, 960], P('shard', 'tensor'), as said below
- owner_table: int32 [2, 5], replicated, may hold values from 0 to 7, as said below
- bias_gradient: float32 [11520], P(('shard', 'tensor')), may hold values from -6 to 6
- bias_weight: float32 [11520], P(('shard', 'tensor')), may hold values from -3 to 3
- bias_first: float32 [11520], P(('shard', 'tensor')), may hold values from -6 to 6
- bias_second: float32 [11520], P(('shard', 'tensor')), may hold values from 0.3 to 3
Outputs:
- new_weight: float32 [384, 4, 3456], P('shard', 'tensor')
- new_first: float32 [384, 4, 3456], P('shard', 'tensor')
- new_second: float32 [384, 4, 3456], P('shard', 'tensor')
- owned_basis: float32 [8, 2, 384, 384], P('shard', None, None, 'tensor')
- owned_gram: float32 [8, 2, 384, 384], P('shard', None, None, 'tensor')
- bias_updated: float32 [11520], P(('shard', 'tensor'))
- bias_first_new: float32 [11520], P(('shard', 'tensor'))
- bias_second_new: float32 [11520], P(('shard', 'tensor'))
Inputs may be any that keep to these rules, and one draw needn't show every extreme that they name: `owner_table`: every owner group that owns a matrix owns exactly 2, with at most 8 column tiles together, and some group has exactly 8; group 0 and the last group own matrices. `left_gram`: each matrix is symmetric.
All inputs are finite; a program needn't handle non-finite values.
Results may differ from a plain program's by a relative error of at most 0.0001.
Values sent between devices are 32-bit elements; how exact they have to be, the bound alone decides.
No kernel may reach another device: no remote copies, remote signals or barrier semaphores. Data moves between devices by JAX's collectives and lax.ppermute only.
A program may use at most 128 MiB of HBM per device.

v0:
```python
import functools

import jax
import jax.numpy as jnp
import numpy as np
from jax import lax
from jax.experimental import pallas as pl
from jax.experimental.pallas import tpu as pltpu
from jax.sharding import PartitionSpec as P

MCAP = 2
STEP = 10
NS_STEPS = 5
TYPE_TILES = (3, 1, 4, 4, 6)
LANES = 128
F32 = jnp.float32
BF16 = jnp.bfloat16
CORR_ONE = 1.0 - 0.9**STEP
CORR_TWO = 1.0 - 0.95**STEP


def adam_direction(moment_hat, second_new):
    return moment_hat / CORR_ONE / (jnp.sqrt(second_new / CORR_TWO) + 1e-08)


def place_columns(layer_total, shards, columns):
    sizes = [tiles * columns for tiles in TYPE_TILES] * layer_total
    starts = np.concatenate([[0], np.cumsum(sizes)]).tolist()
    share = starts[-1] // shards
    assert share * shards == starts[-1]
    small = [i for i, size in enumerate(sizes) if size <= share]
    groups = [[] for _ in range(shards)]
    room = [share] * shards
    if len(small) <= shards:
        for group, i in enumerate(small):
            groups[group].append((i, starts[i], sizes[i]))
            room[group] -= sizes[i]
        rest = [i for i in range(len(sizes)) if i not in small]
    else:
        rest = list(range(len(sizes)))
    group = 0
    for i in rest:
        at, left = starts[i], sizes[i]
        while left:
            while not room[group]:
                group += 1
            take = min(left, room[group])
            groups[group].append((i, at, take))
            room[group] -= take
            at += take
            left -= take
    return groups, share


def block_form(rows, width):
    full, rest = divmod(width, LANES)
    padded = -(-rows // 8) * 8
    halved = 0 < rest <= LANES // 2 and rows % 16 == 0
    total = full * padded + (0 if not rest else rows // 2 if halved else padded)
    return full, rest, padded, halved, total


def store_block(ref, index, base, value, rows, width):
    full, rest, padded, halved, _ = block_form(rows, width)
    for j in range(full):
        at = base + j * padded
        ref[index, at : at + rows, :] = value[:, j * LANES : (j + 1) * LANES]
    if rest:
        at = base + full * padded
        tail = value[:, full * LANES : width]
        if halved:
            half = rows // 2
            ref[index, at : at + half, 0:rest] = tail[:half]
            ref[index, at : at + half, LANES // 2 : LANES // 2 + rest] = tail[half:]
        else:
            ref[index, at : at + rows, 0:rest] = tail


def load_pieces(ref, index, base, rows, width):
    full, rest, padded, halved, _ = block_form(rows, width)
    pieces = []
    for j in range(full):
        at = base + j * padded
        pieces.append(ref[index, at : at + rows, :])
    if rest:
        at = base + full * padded
        if halved:
            half = rows // 2
            block = ref[index, at : at + half, :]
            pieces.append(
                jnp.concatenate(
                    [block[:, 0:rest], block[:, LANES // 2 : LANES // 2 + rest]], axis=0
                )
            )
        else:
            pieces.append(ref[index, at : at + rows, 0:rest])
    return pieces


def load_block(ref, index, base, rows, width):
    pieces = load_pieces(ref, index, base, rows, width)
    return pieces[0] if len(pieces) == 1 else jnp.concatenate(pieces, axis=1)


def unpack_columns(ref, base, out_ref, shards, rows, width):
    if width % LANES:
        tail = width // LANES * LANES
        out_ref[:, tail:] = jnp.zeros((out_ref.shape[0], LANES), F32)
    for source in range(shards):
        for j, piece in enumerate(load_pieces(ref, source, base, rows, width)):
            lanes = piece.shape[1]
            out_ref[source * rows : (source + 1) * rows, j * LANES : j * LANES + lanes] = piece


def pack_columns(value_ref, ref, base, shards, rows, width):
    for dest in range(shards):
        block = value_ref[dest * rows : (dest + 1) * rows, 0:width]
        store_block(ref, dest, base, block, rows, width)


def parts_of(value):
    high = value.astype(BF16)
    return high, (value - high.astype(F32)).astype(BF16)


def product(left, right, contract=(1, 0)):
    dims = (((contract[0],), (contract[1],)), ((), ()))
    dot = functools.partial(lax.dot_general, dimension_numbers=dims, preferred_element_type=F32)
    return dot(left[0], right[0]) + (dot(left[0], right[1]) + dot(left[1], right[0]))


def call(kernel, outs, args, specs=None, out_specs=None, scratch=(), aliases=None, grid=()):
    single = isinstance(outs, tuple)
    shapes = [outs] if single else list(outs)
    shapes = [s if isinstance(s, jax.ShapeDtypeStruct) else jax.ShapeDtypeStruct(s, F32) for s in shapes]
    vmem = pl.BlockSpec(memory_space=pltpu.VMEM)
    specs = specs or [None] * len(args)
    result = pl.pallas_call(
        kernel,
        out_shape=shapes,
        grid=grid,
        in_specs=[s or vmem for s in specs],
        out_specs=out_specs or [vmem] * len(shapes),
        scratch_shapes=list(scratch),
        input_output_aliases=aliases or {},
        compiler_params=pltpu.CompilerParams(vmem_limit_bytes=40 * 2**20),
    )(*args)
    return result[0] if single else result


SMEM = pl.BlockSpec(memory_space=pltpu.SMEM)
ANY = pl.BlockSpec(memory_space=pl.ANY)


def body(
    gradient,
    weight,
    first_moment,
    second_moment,
    left_basis,
    left_gram,
    owner_table,
    bias_gradient,
    bias_weight,
    bias_first,
    bias_second,
):
    shards = lax.axis_size("shard")
    ranks = lax.axis_size("tensor")
    assert ranks == 4 and MCAP == 2
    layer_total = owner_table.shape[0]
    matrix_total = 5 * layer_total
    rows = gradient.shape[0]
    line = gradient.shape[2]
    columns = line // (sum(TYPE_TILES) * layer_total)
    width = rows * shards
    assert columns * ranks == width and columns <= LANES
    groups, share = place_columns(layer_total, shards, columns)
    slots = max(len(group) for group in groups)
    wide = -(-share // LANES) * LANES
    strip = slots * columns
    owned = MCAP * columns
    tile_rows = block_form(rows, share)[4]
    strip_rows = block_form(rows, strip)[4]
    owned_rows = block_form(rows, owned)[4]
    slot_matrix = [[piece[0] for piece in group] for group in groups]
    edges = np.full((shards, slots + 1), share, np.int32)
    for group, pieces in enumerate(groups):
        edges[group, 0] = 0
        edges[group, 1 : len(pieces) + 1] = np.cumsum([piece[2] for piece in pieces])

    my_group = lax.axis_index("shard")
    my_rank = lax.axis_index("tensor").astype(jnp.int32)
    my_edges = jnp.asarray(edges)[my_group]
    rank_arg = my_rank.reshape(1)
    owners = owner_table.reshape(-1)
    core_pairs = [(r, r ^ 1) for r in range(ranks)]
    chip_pairs = [(r, r ^ 2) for r in range(ranks)]

    def over_core(value):
        return lax.ppermute(value, "tensor", core_pairs)

    def over_chip(value):
        return lax.ppermute(value, "tensor", chip_pairs)

    def exchange(value):
        return lax.all_to_all(value, "shard", split_axis=0, concat_axis=0, tiled=True)

    together = lax.optimization_barrier


    line_tiles = line // LANES
    assert line_tiles * LANES == line
    dense = (rows * line_tiles, LANES)
    line_scratch = pltpu.VMEM((rows, line), F32)

    def open_line(ref, line_ref):
        for j in range(line_tiles):
            line_ref[:, j * LANES : (j + 1) * LANES] = ref[pl.ds(j, rows, stride=line_tiles), :]

    def close_line(line_ref, ref):
        for j in range(line_tiles):
            ref[pl.ds(j, rows, stride=line_tiles), :] = line_ref[:, j * LANES : (j + 1) * LANES]

    def gather_line(ref, group):
        pieces = [ref[:, at : at + length] for _, at, length in groups[group]]
        return pieces[0] if len(pieces) == 1 else jnp.concatenate(pieces, axis=1)

    def send_tiles(ref, line_ref, out_ref, base):
        open_line(ref, line_ref)
        for group in range(shards):
            store_block(out_ref, group, base, gather_line(line_ref, group), rows, share)

    def fill_owned_table(owner_ref, table_ref, count_ref):
        for group in range(shards):
            count_ref[group] = 0
            for m in range(MCAP):
                table_ref[group * MCAP + m] = -1

        def take(i, carry):
            owner = owner_ref[i]
            rank = count_ref[owner]
            table_ref[owner * MCAP + rank] = i
            count_ref[owner] = rank + 1
            return carry

        lax.fori_loop(0, matrix_total, take, 0)

    def send_owned(stage_ref, table_ref, out_ref, base):
        for group in range(shards):
            held = []
            for m in range(MCAP):
                matrix = table_ref[group * MCAP + m]
                block = stage_ref[jnp.maximum(matrix, 0)]
                held.append(jnp.where(matrix >= 0, block, 0.0))
            store_block(out_ref, group, base, jnp.concatenate(held, axis=1), rows, owned)

    table_scratch = [pltpu.SMEM((shards * MCAP,), jnp.int32), pltpu.SMEM((shards,), jnp.int32)]
    stage_scratch = pltpu.VMEM((matrix_total, rows, columns), F32)

    def slot_masks(edges_ref):
        lane = lax.broadcasted_iota(jnp.int32, (1, wide), 1)
        return [(lane >= edges_ref[k]) & (lane < edges_ref[k + 1]) for k in range(slots)]


    def pack_gradient(grad_ref, basis_ref, out_ref, line_ref):
        send_tiles(grad_ref, line_ref, out_ref, strip_rows)
        for group in range(shards):
            held = [
                basis_ref[:, matrix * columns : (matrix + 1) * columns]
                for matrix in slot_matrix[group]
            ]
            held += [jnp.zeros((rows, columns), F32)] * (slots - len(held))
            store_block(out_ref, group, 0, jnp.concatenate(held, axis=1), rows, strip)

    grad_dense = gradient.reshape(dense)
    basis_line = left_basis.reshape(rows, matrix_total * columns)
    send_one = call(
        pack_gradient,
        (shards, strip_rows + tile_rows, LANES),
        (grad_dense, basis_line),
        scratch=[line_scratch],
    )
    came_one = exchange(send_one)


    def pack_second(
        owner_ref, second_ref, basis_ref, out_ref, table_ref, count_ref, stage_ref, line_ref
    ):
        fill_owned_table(owner_ref, table_ref, count_ref)
        for matrix in range(matrix_total):
            stage_ref[matrix] = basis_ref[:, matrix * columns : (matrix + 1) * columns]
        send_tiles(second_ref, line_ref, out_ref, owned_rows)
        send_owned(stage_ref, table_ref, out_ref, 0)

    send_two = call(
        pack_second,
        (shards, owned_rows + tile_rows, LANES),
        (owners, second_moment.reshape(dense), basis_line),
        specs=[SMEM, None, None],
        scratch=table_scratch + [stage_scratch, line_scratch],
    )
    came_one, send_two = together((came_one, send_two))
    came_two = exchange(send_two)


    def gram_partials(edges_ref, came_ref, grad_ref, strips_ref, gram_ref, turned_ref):
        unpack_columns(came_ref, strip_rows, grad_ref, shards, rows, share)
        for source in range(shards):
            strips_ref[source] = came_ref[source, 0:strip_rows, :]
        turned_ref[...] = jnp.zeros_like(turned_ref)
        for rank in range(ranks):
            turned_ref[rank * LANES : rank * LANES + columns, :] = grad_ref[
                rank * columns : (rank + 1) * columns, :
            ]
        right = parts_of(turned_ref[...])
        grams = []
        for mask in slot_masks(edges_ref):
            left = parts_of(jnp.where(mask, grad_ref[...], 0.0))
            grams.append(product(left, right, (1, 1)))
        for rank in range(ranks):
            for group in range(shards):
                at = slice(group * rows, (group + 1) * rows)
                held = [g[at, rank * LANES : rank * LANES + columns] for g in grams]
                store_block(
                    gram_ref.at[rank],
                    group,
                    0,
                    jnp.concatenate(held, axis=1),
                    rows,
                    strip,
                )

    strip_shape = (shards, strip_rows, LANES)
    grad_full, strips_own, gram_parts = call(
        gram_partials,
        [(width, wide), strip_shape, (ranks,) + strip_shape],
        (my_edges, came_one),
        specs=[SMEM, None],
        scratch=[pltpu.VMEM((ranks * LANES, wide), F32)],
    )

    parts = gram_parts.reshape((2, 2) + strip_shape)
    my_chip, my_core = my_rank // 2, my_rank % 2
    for_core = lax.dynamic_index_in_dim(parts, 1 - my_core, 1, False)
    kept = lax.dynamic_index_in_dim(parts, my_core, 1, False) + over_core(for_core)
    for_chip = lax.dynamic_index_in_dim(kept, 1 - my_chip, 0, False)
    gram_strips = lax.dynamic_index_in_dim(kept, my_chip, 0, False) + over_chip(for_chip)

    strips_chip = over_chip(strips_own)
    pair = over_core(jnp.stack([strips_own, strips_chip]))


    def pack_first(first_ref, grad_ref, out_ref, new_ref, line_ref):
        send_tiles(first_ref, line_ref, out_ref, strip_rows)
        new_ref[...] = 0.9 * first_ref[...] + 0.1 * grad_ref[...]

    send_three, first_out = call(
        pack_first,
        [(shards, strip_rows + tile_rows, LANES), dense],
        (first_moment.reshape(dense), grad_dense),
        scratch=[line_scratch],
    )

    def add_strips(base_ref, strips_ref, out_ref):
        del base_ref
        out_ref[...] = strips_ref[...]

    def fill_head(kernel, base, head_rows, args, specs, scratch=()):
        return call(
            kernel,
            base.shape,
            (base,) + args,
            specs=[ANY] + specs,
            out_specs=[pl.BlockSpec((shards, head_rows, LANES), lambda i: (0, 0, 0))],
            grid=(1,),
            scratch=scratch,
            aliases={0: 0},
        )

    send_three = fill_head(add_strips, send_three, strip_rows, (gram_strips,), [None])
    came_two, send_three = together((came_two, send_three))
    came_three = exchange(send_three)


    half_shape = jax.ShapeDtypeStruct((slots, width, width), BF16)

    def rotate_gradient(
        rank_ref,
        edges_ref,
        own_ref,
        chip_ref,
        pair_ref,
        grad_ref,
        came_ref,
        high_ref,
        low_ref,
        high_turned_ref,
        low_turned_ref,
        second_ref,
        basis_ref,
    ):
        rank = rank_ref[0]
        for group in range(shards):
            blocks = [
                load_block(ref, group, 0, rows, strip)
                for ref in (own_ref, pair_ref.at[0], chip_ref, pair_ref.at[1])
            ]
            at = slice(group * rows, (group + 1) * rows)
            for k in range(slots):
                cut = [block[:, k * columns : (k + 1) * columns] for block in blocks]
                low = [jnp.where(rank % 2 == 0, cut[0 + h], cut[1 + h]) for h in (0, 2)]
                odd = [jnp.where(rank % 2 == 0, cut[1 + h], cut[0 + h]) for h in (0, 2)]
                first = rank < 2
                ordered = [
                    jnp.where(first, low[0], low[1]),
                    jnp.where(first, odd[0], odd[1]),
                    jnp.where(first, low[1], low[0]),
                    jnp.where(first, odd[1], odd[0]),
                ]
                basis_ref[k, at, :] = jnp.concatenate(ordered, axis=1)
        unpack_columns(came_ref, owned_rows, second_ref, shards, rows, share)
        grad = parts_of(grad_ref[...])
        hat = jnp.zeros((width, wide), F32)
        for k, mask in enumerate(slot_masks(edges_ref)):
            basis = basis_ref[k]
            high_ref[k], low_ref[k] = parts_of(basis)
            turned = parts_of(basis.T)
            high_turned_ref[k], low_turned_ref[k] = turned
            hat = jnp.where(mask, product(turned, grad), hat)
        second_ref[...] = 0.95 * second_ref[...] + 0.05 * hat * hat

    high, low, high_turned, low_turned, second_full = call(
        rotate_gradient,
        [half_shape] * 4 + [(width, wide)],
        (rank_arg, my_edges, strips_own, strips_chip, pair, grad_full, came_two),
        specs=[SMEM, SMEM] + [None] * 5,
        scratch=[pltpu.VMEM((slots, width, width), F32)],
    )


    def new_grams(owner_ref, came_ref, gram_ref, out_ref, table_ref, count_ref, stage_ref):
        fill_owned_table(owner_ref, table_ref, count_ref)
        total = [None] * matrix_total
        for group in range(shards):
            block = load_block(came_ref, group, 0, rows, strip)
            for k, matrix in enumerate(slot_matrix[group]):
                part = block[:, k * columns : (k + 1) * columns]
                total[matrix] = part if total[matrix] is None else total[matrix] + part
        for matrix in range(matrix_total):
            gram = gram_ref[:, matrix * columns : (matrix + 1) * columns]
            stage_ref[matrix] = 0.95 * gram + 0.05 * total[matrix]
        send_owned(stage_ref, table_ref, out_ref, 0)

    send_four = call(
        new_grams,
        (shards, owned_rows, LANES),
        (owners, came_three, left_gram.reshape(rows, matrix_total * columns)),
        specs=[SMEM, None, None],
        scratch=table_scratch + [stage_scratch],
    )
    came_three, send_four = together((came_three, send_four))
    came_four = exchange(send_four)


    def directions(
        edges_ref,
        came_ref,
        grad_ref,
        second_ref,
        high_ref,
        low_ref,
        high_turned_ref,
        low_turned_ref,
        send_ref,
        moment_ref,
    ):
        unpack_columns(came_ref, strip_rows, moment_ref, shards, rows, share)
        masks = slot_masks(edges_ref)
        moment = parts_of(0.9 * moment_ref[...] + 0.1 * grad_ref[...])
        hat = jnp.zeros((width, wide), F32)
        for k, mask in enumerate(masks):
            hat = jnp.where(mask, product((high_turned_ref[k], low_turned_ref[k]), moment), hat)
        step = parts_of(adam_direction(hat, second_ref[...]))
        turned = jnp.zeros((width, wide), F32)
        for k, mask in enumerate(masks):
            turned = jnp.where(mask, product((high_ref[k], low_ref[k]), step), turned)
        moment_ref[...] = turned
        pack_columns(moment_ref, send_ref, 0, shards, rows, share)
        pack_columns(second_ref, send_ref, tile_rows, shards, rows, share)

    send_five = call(
        directions,
        (shards, 2 * tile_rows, LANES),
        (my_edges, came_three, grad_full, second_full, high, low, high_turned, low_turned),
        specs=[SMEM] + [None] * 7,
        scratch=[pltpu.VMEM((width, wide), F32)],
    )
    came_four, send_five = together((came_four, send_five))
    came_five = exchange(send_five)


    def split_owned(rank_ref, came_ref, strips_ref, mine_ref, other_ref, whole_ref):
        odd = rank_ref[0] % 2 == 1
        for source in range(shards):
            at = slice(source * rows, (source + 1) * rows)
            block = load_block(came_ref, source, 0, rows, owned)
            zero, one = block[:, 0:columns], block[:, columns:owned]
            whole_ref[0, at, 0:columns] = zero
            whole_ref[1, at, 0:columns] = one
            mine_ref[at, 0:columns] = jnp.where(odd, one, zero)
            other_ref[at, 0:columns] = jnp.where(odd, zero, one)
        for m in range(MCAP):
            strips_ref[m] = whole_ref[m].T[0:columns]

    def join_half(rank_ref, mine_ref, other_ref, half_ref):
        odd = rank_ref[0] % 2 == 1
        for group in range(shards):
            at = slice(group * rows, (group + 1) * rows)
            mine, other = mine_ref[at, 0:columns], other_ref[at, 0:columns]
            both = [jnp.where(odd, other, mine), jnp.where(odd, mine, other)]
            store_block(half_ref, group, 0, jnp.concatenate(both, axis=1), rows, owned)

    def collect(came):
        strips, mine, other = call(
            split_owned,
            [(MCAP, columns, width), (width, LANES), (width, LANES)],
            (rank_arg, came),
            specs=[SMEM, None],
            scratch=[pltpu.VMEM((MCAP, width, LANES), F32)],
        )
        half = call(
            join_half,
            (shards, owned_rows, LANES),
            (rank_arg, mine, over_core(other)),
            specs=[SMEM, None, None],
        )
        return strips, half, over_chip(half)

    _, basis_half, basis_far = collect(came_two)
    gram_out, gram_half, gram_far = collect(came_four)

    def refresh(
        rank_ref,
        basis_half_ref,
        basis_far_ref,
        gram_half_ref,
        gram_far_ref,
        mine_ref,
        other_ref,
        basis_ref,
        gram_ref,
    ):
        rank = rank_ref[0]
        first = rank < 2
        for out, half_ref, far_ref in (
            (basis_ref, basis_half_ref, basis_far_ref),
            (gram_ref, gram_half_ref, gram_far_ref),
        ):
            for group in range(shards):
                half = load_block(half_ref, group, 0, rows, owned)
                far = load_block(far_ref, group, 0, rows, owned)
                both = [jnp.where(first, half, far), jnp.where(first, far, half)]
                out[group * rows : (group + 1) * rows, :] = jnp.concatenate(both, axis=1)
        power = product(parts_of(basis_ref[...].T), parts_of(gram_ref[...]))
        frame = power / jnp.sqrt(jnp.sum(power * power) + 1e-06)
        for _ in range(NS_STEPS):
            pieces = parts_of(frame)
            square = product(pieces, pieces, (1, 1))
            frame = 1.5 * frame - 0.5 * product(parts_of(square), pieces)
        strips = [frame[r * columns : (r + 1) * columns] for r in range(ranks)]
        low = jnp.where(first, strips[0], strips[2])
        odd = jnp.where(first, strips[1], strips[3])
        even_core = rank % 2 == 0
        mine_ref[...] = jnp.where(even_core, low, odd)
        other_ref[...] = jnp.where(even_core, odd, low)

    frame_mine, frame_other = call(
        refresh,
        [(columns, width), (columns, width)],
        (rank_arg, basis_half, basis_far, gram_half, gram_far),
        specs=[SMEM] + [None] * 4,
        scratch=[pltpu.VMEM((width, width), F32)] * 2,
    )
    frame_came = over_core(frame_other)
    pair_out = jnp.where(
        my_core == 0,
        jnp.stack([frame_mine, frame_came]),
        jnp.stack([frame_came, frame_mine]),
    )
    came_five, pair_out, gram_out, first_out = together((came_five, pair_out, gram_out, first_out))


    def line_from(came_ref, base, line_ref):
        for group in range(shards):
            block = load_block(came_ref, group, base, rows, share)
            offset = 0
            for _, at, length in groups[group]:
                line_ref[:, at : at + length] = block[:, offset : offset + length]
                offset += length

    def take_back(came_ref, weight_ref, weight_out_ref, second_out_ref, line_ref):
        line_from(came_ref, 0, line_ref)
        close_line(line_ref, weight_out_ref)
        old = weight_ref[...]
        weight_out_ref[...] = old - 0.01 * (weight_out_ref[...] + 0.1 * old)
        line_from(came_ref, tile_rows, line_ref)
        close_line(line_ref, second_out_ref)

    weight_out, second_out = call(
        take_back, [dense, dense], (came_five, weight.reshape(dense)), scratch=[line_scratch]
    )

    bias_first_new = 0.9 * bias_first + 0.1 * bias_gradient
    bias_second_new = 0.95 * bias_second + 0.05 * bias_gradient * bias_gradient
    bias_updated = bias_weight - 0.01 * adam_direction(bias_first_new, bias_second_new)
    flat = (rows, 1, line)
    return (
        weight_out.reshape(flat),
        first_out.reshape(flat),
        second_out.reshape(flat),
        pair_out.transpose(0, 2, 1)[None],
        gram_out.transpose(0, 2, 1)[None],
        bias_updated,
        bias_first_new,
        bias_second_new,
    )


def solution(mesh):
    tiles = P("shard", "tensor", None)
    bias = P(("shard", "tensor"))
    owned = P("shard", None, None, "tensor")
    in_specs = (tiles,) * 6 + (P(),) + (bias,) * 4
    out_specs = (tiles,) * 3 + (owned,) * 2 + (bias,) * 3
    return jax.shard_map(body, mesh=mesh, in_specs=in_specs, out_specs=out_specs, check_vma=False)
```

profile of v0, /device:TPU:0, one launch (start us, length us, event | category | flops | bytes accessed | tf_op | source)
XLA Modules:
  0.0 148.2 jit_solution(157425097383761737)
XLA Ops:
  0.6 1.0 copy.29
  1.6 1.1 copy-done
  2.7 1.9 %shard_map.179 = f32[8,240,128]{2,1,0:T(8,128)} custom-call(f32[1296,128]{1,0:T(8,128)S(1)} %bitcast.35, f32[48,960]{1,0:T(8,128)S(1)} %bitcast.37), custom_call_target="tpu_custom_call" | custom-call | tf_op jit(solution)/shard_map/pallas_call | solution.py:138
  4.5 7.4 %all-to-all-start = ((f32[8,240,128]{2,1,0:T(8,128)}), f32[8,240,128]{2,1,0:T(8,128)S(1)}, u32[]{:S(2)}, u32[]{:S(2)}) async-start(f32[8,240,128]{2,1,0:T(8,128)} %shard_map.179), calls=%async_computation | async-start | bytes 1966080 | tf_op jit(solution)/shard_map/all_to_all | solution.py:207
  12.1 2.7 %shard_map.180 = f32[8,240,128]{2,1,0:T(8,128)} custom-call(s32[10]{0:T(128)S(1)} %reshape.54.owner_ref, f32[1296,128]{1,0:T(8,128)S(1)} %bitcast.45, f32[48,960]{1,0:T(8,128)S(1)} %bitcast.38), custom_call_target="tpu_custom_call" | custom-call | tf_op jit(solution)/shard_map/pallas_call | solution.py:138
  14.7 21.6 %all-to-all-done.came_ref = f32[8,240,128]{2,1,0:T(8,128)S(1)} async-done(((f32[8,240,128]{2,1,0:T(8,128)}), f32[8,240,128]{2,1,0:T(8,128)S(1)}, u32[]{:S(2)}, u32[]{:S(2)}) %all-to-all-start) | async-done | bytes 983072 | tf_op jit(solution)/shard_map/all_to_all | solution.py:207
  36.4 3.6 %all-to-all-start.1 = ((f32[8,240,128]{2,1,0:T(8,128)}), f32[8,240,128]{2,1,0:T(8,128)S(1)}, u32[]{:S(2)}, u32[]{:S(2)}) async-start(f32[8,240,128]{2,1,0:T(8,128)} %shard_map.180), calls=%async_computation.1 | async-start | bytes 1966080 | tf_op jit(solution)/shard_map/all_to_all | solution.py:207
  39.9 0.7 fusion.1.edges_ref
  40.6 2.3 %shard_map.182 = (f32[384,512]{1,0:T(8,128)S(1)}, f32[8,72,128]{2,1,0:T(8,128)S(1)}, f32[4,8,72,128]{3,2,1,0:T(8,128)S(1)}) custom-call(s32[3]{0:T(128)S(1)} %fusion.1.edges_ref, f32[8,240,128]{2,1,0:T(8,128)S(1)} %all-to-all-done.came_ref), custom_call_target="tpu_custom_call" | custom-call | tf_op jit(solution)/shard_map/pallas_call | solution.py:138
  43.0 1.0 copy-done.4
  44.1 2.1 %collective-permute-done = f32[2,8,72,128]{3,2,1,0:T(8,128)} collective-permute-done((f32[2,8,72,128]{3,2,1,0:T(8,128)S(1)}, f32[2,8,72,128]{3,2,1,0:T(8,128)}, u32[]{:S(2)}, u32[]{:S(2)}) %collective-permute-start) | collective-permute-done | bytes 589856 | tf_op jit(solution)/shard_map/ppermute | solution.py:201
  46.2 1.3 bitcast_add_fusion
  47.5 0.7 dynamic-slice_bitcast_fusion.1
  48.3 1.5 %collective-permute-start.1 = (f32[8,72,128]{2,1,0:T(8,128)}, f32[8,72,128]{2,1,0:T(8,128)}, u32[]{:S(2)}, u32[]{:S(2)}) collective-permute-start(f32[8,72,128]{2,1,0:T(8,128)} %dynamic-slice_bitcast_fusion.1), channel_id=1, source_target_pairs={{0,2},{1,3},{2,0},{3,1},{4,6},{5,7},{6,4},{7,5},{8,10},{9,11},{10,... | collective-permute-start | bytes 884744 | tf_op jit(solution)/shard_map/ppermute | solution.py:204
  49.8 1.1 copy-done.7
  50.9 1.6 %shard_map.181 = (f32[8,240,128]{2,1,0:T(8,128)}, f32[1296,128]{1,0:T(8,128)}) custom-call(f32[1296,128]{1,0:T(8,128)S(1)} %bitcast.44, f32[1296,128]{1,0:T(8,128)S(1)} %bitcast.36), custom_call_target="tpu_custom_call" | custom-call | tf_op jit(solution)/shard_map/pallas_call | solution.py:138
  52.5 5.1 %collective-permute-done.1 = f32[8,72,128]{2,1,0:T(8,128)} collective-permute-done((f32[8,72,128]{2,1,0:T(8,128)}, f32[8,72,128]{2,1,0:T(8,128)}, u32[]{:S(2)}, u32[]{:S(2)}) %collective-permute-start.1) | collective-permute-done | bytes 294944 | tf_op jit(solution)/shard_map/ppermute | solution.py:204
  57.6 1.0 bitcast_add_fusion.1.strips_ref
  58.6 0.7 shard_map.183
  59.4 5.1 %all-to-all-done.1.came_ref = f32[8,240,128]{2,1,0:T(8,128)S(1)} async-done(((f32[8,240,128]{2,1,0:T(8,128)}), f32[8,240,128]{2,1,0:T(8,128)S(1)}, u32[]{:S(2)}, u32[]{:S(2)}) %all-to-all-start.1) | async-done | bytes 983072 | tf_op jit(solution)/shard_map/all_to_all | solution.py:207
  64.5 3.6 %all-to-all-start.2 = ((f32[8,240,128]{2,1,0:T(8,128)}), f32[8,240,128]{2,1,0:T(8,128)S(1)}, u32[]{:S(2)}, u32[]{:S(2)}) async-start(f32[8,240,128]{2,1,0:T(8,128)} %shard_map.183), calls=%async_computation.2 | async-start | bytes 1966080 | tf_op jit(solution)/shard_map/all_to_all | solution.py:207
  68.1 1.5 %collective-permute-start.2 = (f32[8,72,128]{2,1,0:T(8,128)S(1)}, f32[8,72,128]{2,1,0:T(8,128)S(1)}, u32[]{:S(2)}, u32[]{:S(2)}) collective-permute-start(f32[8,72,128]{2,1,0:T(8,128)S(1)} %get-tuple-element.47.own_ref), channel_id=1, source_target_pairs={{0,2},{1,3},{2,0},{3,1},{4,6},{5,7},{6,4},{7,5},{8,10},{9,11},{10,... | collective-permute-start | bytes 884744 | tf_op jit(solution)/shard_map/ppermute | solution.py:204
  69.6 7.1 %collective-permute-done.2.chip_ref = f32[8,72,128]{2,1,0:T(8,128)S(1)} collective-permute-done((f32[8,72,128]{2,1,0:T(8,128)S(1)}, f32[8,72,128]{2,1,0:T(8,128)S(1)}, u32[]{:S(2)}, u32[]{:S(2)}) %collective-permute-start.2) | collective-permute-done | bytes 294944 | tf_op jit(solution)/shard_map/ppermute | solution.py:204
  76.8 0.9 pad_maximum_fusion
  77.6 1.0 copy.28
  78.6 14.0 %all-to-all-done.2.came_ref = f32[8,240,128]{2,1,0:T(8,128)S(1)} async-done(((f32[8,240,128]{2,1,0:T(8,128)}), f32[8,240,128]{2,1,0:T(8,128)S(1)}, u32[]{:S(2)}, u32[]{:S(2)}) %all-to-all-start.2) | async-done | bytes 983072 | tf_op jit(solution)/shard_map/all_to_all | solution.py:207
  92.6 1.9 %shard_map.184 = f32[8,72,128]{2,1,0:T(8,128)} custom-call(s32[10]{0:T(128)S(1)} %reshape.54.owner_ref, f32[8,240,128]{2,1,0:T(8,128)S(1)} %all-to-all-done.2.came_ref, f32[48,960]{1,0:T(8,128)S(1)} %bitcast.43), custom_call_target="tpu_custom_call" | custom-call | tf_op jit(solution)/shard_map/pallas_call | solution.py:138
  94.5 3.6 %all-to-all-start.3 = ((f32[8,72,128]{2,1,0:T(8,128)}), f32[8,72,128]{2,1,0:T(8,128)S(1)}, u32[]{:S(2)}, u32[]{:S(2)}) async-start(f32[8,72,128]{2,1,0:T(8,128)} %shard_map.184), calls=%async_computation.3 | async-start | bytes 589824 | tf_op jit(solution)/shard_map/all_to_all | solution.py:207
  98.2 1.0 copy-done.6
  99.1 3.1 %shard_map.185 = (bf16[2,384,384]{2,1,0:T(8,128)(2,1)S(1)}, bf16[2,384,384]{2,1,0:T(8,128)(2,1)S(1)}, bf16[2,384,384]{2,1,0:T(8,128)(2,1)S(1)}, bf16[2,384,384]{2,1,0:T(8,128)(2,1)S(1)}, f32[384,512]{1,0:T(8,128)S(1)}) custom-call(s32[1]{0:T(128)} %bitcast.9.rank_ref, s32[3]{0:T(128)S(1)} %fusion.1.edges_ref, f32[8,72,128]{2,1,0:T(8,128)S(1)} %get-tuple-element.47.own_ref, ...), custom_call_target="tpu_custom_call" | custom-call | tf_op jit(solution)/shard_map/pallas_call | solution.py:138
  102.3 4.8 %shard_map.186 = f32[8,336,128]{2,1,0:T(8,128)} custom-call(s32[3]{0:T(128)S(1)} %fusion.1.edges_ref, f32[8,240,128]{2,1,0:T(8,128)S(1)} %all-to-all-done.2.came_ref, f32[384,512]{1,0:T(8,128)S(1)} %get-tuple-element.46.grad_ref, f32[384,512]{1,0:T(8,128)S(1)} %get-tuple-element.49.second_ref, bf16[2,384,384]{2,1,0:T(8,128)(2,1)S(1)} %get-tuple-element.50.high_ref, ...), custom_call_target="tpu_custom_call" | custom-call | tf_op jit(solution)/shard_map/pallas_call | solution.py:138
  107.1 0.9 all-to-all-done.3.came_ref
  107.9 0.7 copy-done.2
  108.6 5.1 %all-to-all-start.4 = ((f32[8,336,128]{2,1,0:T(8,128)}), f32[8,336,128]{2,1,0:T(8,128)S(1)}, u32[]{:S(2)}, u32[]{:S(2)}) async-start(f32[8,336,128]{2,1,0:T(8,128)} %shard_map.186), calls=%async_computation.4 | async-start | bytes 2752512 | tf_op jit(solution)/shard_map/all_to_all | solution.py:207
  113.8 1.9 %shard_map.187 = (f32[2,96,384]{2,1,0:T(8,128)}, f32[384,128]{1,0:T(8,128)S(1)}, f32[384,128]{1,0:T(8,128)S(1)}) custom-call(s32[1]{0:T(128)} %bitcast.9.rank_ref, f32[8,240,128]{2,1,0:T(8,128)S(1)} %all-to-all-done.1.came_ref), custom_call_target="tpu_custom_call" | custom-call | tf_op jit(solution)/shard_map/pallas_call | solution.py:138
  115.7 1.9 %shard_map.189 = (f32[2,96,384]{2,1,0:T(8,128)}, f32[384,128]{1,0:T(8,128)S(1)}, f32[384,128]{1,0:T(8,128)S(1)}) custom-call(s32[1]{0:T(128)} %bitcast.9.rank_ref, f32[8,72,128]{2,1,0:T(8,128)S(1)} %copy-done.3), custom_call_target="tpu_custom_call" | custom-call | tf_op jit(solution)/shard_map/pallas_call | solution.py:138
  117.6 0.5 collective-permute-start.6
  118.2 0.2 shard_map.188.basis_half_ref
  118.3 1.6 %collective-permute-start.5 = (f32[8,72,128]{2,1,0:T(8,128)S(1)}, f32[8,72,128]{2,1,0:T(8,128)S(1)}, u32[]{:S(2)}, u32[]{:S(2)}) collective-permute-start(f32[8,72,128]{2,1,0:T(8,128)S(1)} %shard_map.188.basis_half_ref), channel_id=1, source_target_pairs={{0,2},{1,3},{2,0},{3,1},{4,6},{5,7},{6,4},{7,5},{8,10},{9,11},{10,... | collective-permute-start | bytes 884744 | tf_op jit(solution)/shard_map/ppermute | solution.py:204
  120.1 0.9 collective-permute-start.7
  121.0 7.3 %collective-permute-done.5.basis_far_ref = f32[8,72,128]{2,1,0:T(8,128)S(1)} collective-permute-done((f32[8,72,128]{2,1,0:T(8,128)S(1)}, f32[8,72,128]{2,1,0:T(8,128)S(1)}, u32[]{:S(2)}, u32[]{:S(2)}) %collective-permute-start.5) | collective-permute-done | bytes 294944 | tf_op jit(solution)/shard_map/ppermute | solution.py:204
  128.3 5.4 %collective-permute-done.7.gram_far_ref = f32[8,72,128]{2,1,0:T(8,128)S(1)} collective-permute-done((f32[8,72,128]{2,1,0:T(8,128)S(1)}, f32[8,72,128]{2,1,0:T(8,128)S(1)}, u32[]{:S(2)}, u32[]{:S(2)}) %collective-permute-start.7) | collective-permute-done | bytes 294944 | tf_op jit(solution)/shard_map/ppermute | solution.py:204
  133.7 8.6 %shard_map.191 = (f32[96,384]{1,0:T(8,128)S(1)}, f32[96,384]{1,0:T(8,128)S(1)}) custom-call(s32[1]{0:T(128)} %bitcast.9.rank_ref, f32[8,72,128]{2,1,0:T(8,128)S(1)} %shard_map.188.basis_half_ref, f32[8,72,128]{2,1,0:T(8,128)S(1)} %collective-permute-done.5.basis_far_ref, f32[8,72,128]{2,1,0:T(8,128)S(1)} %shard_map.190.gram_half_ref, ...), custom_call_target="tpu_custom_call" | custom-call | tf_op jit(solution)/shard_map/pallas_call | solution.py:138
  142.3 0.6 multiply_subtract_fusion
  142.9 0.7 collective-permute-done.8
  143.6 0.7 maximum_select_fusion
  144.4 1.8 %all-to-all-done.4.came_ref = f32[8,336,128]{2,1,0:T(8,128)S(1)} async-done(((f32[8,336,128]{2,1,0:T(8,128)}), f32[8,336,128]{2,1,0:T(8,128)S(1)}, u32[]{:S(2)}, u32[]{:S(2)}) %all-to-all-start.4) | async-done | bytes 1376288 | tf_op jit(solution)/shard_map/all_to_all | solution.py:207
  146.2 2.1 %shard_map.192 = (f32[1296,128]{1,0:T(8,128)}, f32[1296,128]{1,0:T(8,128)}) custom-call(f32[8,336,128]{2,1,0:T(8,128)S(1)} %all-to-all-done.4.came_ref, f32[1296,128]{1,0:T(8,128)S(1)} %bitcast.46), custom_call_target="tpu_custom_call" | custom-call | tf_op jit(solution)/shard_map/pallas_call | solution.py:138
  (35 shorter events, 0.5 us)
Async XLA Ops:
  1.6 1.1 copy-start
  4.5 7.4 %copy-start.14 = (s32[2,5]{1,0:T(2,128)S(1)}, s32[2,5]{1,0:T(2,128)}, u32[]{:S(2)}) copy-start(s32[2,5]{1,0:T(2,128)} %param.18) | copy-start | bytes 124
  4.5 7.5 %copy-start.8 = (f32[48,1,3456]{2,1,0:T(1,128)S(1)}, f32[48,1,3456]{2,1,0:T(1,128)}, u32[]{:S(2)}) copy-start(f32[48,1,3456]{2,1,0:T(1,128)} %param.15) | copy-start | bytes 1990660
  4.5 31.8 %all-to-all-start = ((f32[8,240,128]{2,1,0:T(8,128)}), f32[8,240,128]{2,1,0:T(8,128)S(1)}, u32[]{:S(2)}, u32[]{:S(2)}) async-start(f32[8,240,128]{2,1,0:T(8,128)} %shard_map.179), calls=%async_computation | async-start | bytes 1966080 | tf_op jit(solution)/shard_map/all_to_all | solution.py:207
  36.4 28.1 %all-to-all-start.1 = ((f32[8,240,128]{2,1,0:T(8,128)}), f32[8,240,128]{2,1,0:T(8,128)S(1)}, u32[]{:S(2)}, u32[]{:S(2)}) async-start(f32[8,240,128]{2,1,0:T(8,128)} %shard_map.180), calls=%async_computation.1 | async-start | bytes 1966080 | tf_op jit(solution)/shard_map/all_to_all | solution.py:207
  42.9 1.0 copy-start.4
  44.0 2.2 %collective-permute-start = (f32[2,8,72,128]{3,2,1,0:T(8,128)S(1)}, f32[2,8,72,128]{3,2,1,0:T(8,128)}, u32[]{:S(2)}, u32[]{:S(2)}) collective-permute-start(f32[2,8,72,128]{3,2,1,0:T(8,128)S(1)} %dynamic-slice_bitcast_fusion), channel_id=1, source_target_pairs={{0,1},{1,0},{2,3},{3,2},{4,5},{5,4},{6,7},{7,6},{8,9},{9,8},{10,11... | collective-permute-start | bytes 1769480 | tf_op jit(solution)/shard_map/ppermute | solution.py:201
  44.1 5.7 %copy-start.1 = (f32[48,1,3456]{2,1,0:T(1,128)S(1)}, f32[48,1,3456]{2,1,0:T(1,128)}, u32[]{:S(2)}) copy-start(f32[48,1,3456]{2,1,0:T(1,128)} %param.12) | copy-start | bytes 1990660
  48.3 9.4 %collective-permute-start.1 = (f32[8,72,128]{2,1,0:T(8,128)}, f32[8,72,128]{2,1,0:T(8,128)}, u32[]{:S(2)}, u32[]{:S(2)}) collective-permute-start(f32[8,72,128]{2,1,0:T(8,128)} %dynamic-slice_bitcast_fusion.1), channel_id=1, source_target_pairs={{0,2},{1,3},{2,0},{3,1},{4,6},{5,7},{6,4},{7,5},{8,10},{9,11},{10,... | collective-permute-start | bytes 884744 | tf_op jit(solution)/shard_map/ppermute | solution.py:204
  49.8 1.1 copy-start.7
  64.5 28.2 %all-to-all-start.2 = ((f32[8,240,128]{2,1,0:T(8,128)}), f32[8,240,128]{2,1,0:T(8,128)S(1)}, u32[]{:S(2)}, u32[]{:S(2)}) async-start(f32[8,240,128]{2,1,0:T(8,128)} %shard_map.183), calls=%async_computation.2 | async-start | bytes 1966080 | tf_op jit(solution)/shard_map/all_to_all | solution.py:207
  68.1 8.6 %collective-permute-start.2 = (f32[8,72,128]{2,1,0:T(8,128)S(1)}, f32[8,72,128]{2,1,0:T(8,128)S(1)}, u32[]{:S(2)}, u32[]{:S(2)}) collective-permute-start(f32[8,72,128]{2,1,0:T(8,128)S(1)} %get-tuple-element.47.own_ref), channel_id=1, source_target_pairs={{0,2},{1,3},{2,0},{3,1},{4,6},{5,7},{6,4},{7,5},{8,10},{9,11},{10,... | collective-permute-start | bytes 884744 | tf_op jit(solution)/shard_map/ppermute | solution.py:204
  76.7 17.8 %copy-start.5 = (f32[8,72,128]{2,1,0:T(8,128)}, f32[8,72,128]{2,1,0:T(8,128)S(1)}, u32[]{:S(2)}) copy-start(f32[8,72,128]{2,1,0:T(8,128)S(1)} %collective-permute-done.2.chip_ref) | copy-start | bytes 884740
  77.6 20.5 %collective-permute-start.3 = (f32[2,8,72,128]{3,2,1,0:T(8,128)}, f32[2,8,72,128]{3,2,1,0:T(8,128)}, u32[]{:S(2)}, u32[]{:S(2)}) collective-permute-start(f32[2,8,72,128]{3,2,1,0:T(8,128)} %pad_maximum_fusion), channel_id=1, source_target_pairs={{0,1},{1,0},{2,3},{3,2},{4,5},{5,4},{6,7},{7,6},{8,9},{9,8},{10,11... | collective-permute-start | bytes 1769480 | tf_op jit(solution)/shard_map/ppermute | solution.py:201
  94.5 13.4 %all-to-all-start.3 = ((f32[8,72,128]{2,1,0:T(8,128)}), f32[8,72,128]{2,1,0:T(8,128)S(1)}, u32[]{:S(2)}, u32[]{:S(2)}) async-start(f32[8,72,128]{2,1,0:T(8,128)} %shard_map.184), calls=%async_computation.3 | async-start | bytes 589824 | tf_op jit(solution)/shard_map/all_to_all | solution.py:207
  98.2 1.0 copy-start.6
  107.9 0.7 copy-start.2
  108.6 37.5 %all-to-all-start.4 = ((f32[8,336,128]{2,1,0:T(8,128)}), f32[8,336,128]{2,1,0:T(8,128)S(1)}, u32[]{:S(2)}, u32[]{:S(2)}) async-start(f32[8,336,128]{2,1,0:T(8,128)} %shard_map.186), calls=%async_computation.4 | async-start | bytes 2752512 | tf_op jit(solution)/shard_map/all_to_all | solution.py:207
  113.8 1.9 %copy-start.3 = (f32[8,72,128]{2,1,0:T(8,128)S(1)}, f32[8,72,128]{2,1,0:T(8,128)}, u32[]{:S(2)}) copy-start(f32[8,72,128]{2,1,0:T(8,128)} %copy-done.2) | copy-start | bytes 884740
  115.7 2.4 %collective-permute-start.4 = (f32[384,128]{1,0:T(8,128)S(1)}, f32[384,128]{1,0:T(8,128)S(1)}, u32[]{:S(2)}, u32[]{:S(2)}) collective-permute-start(f32[384,128]{1,0:T(8,128)S(1)} %get-tuple-element.56), channel_id=1, source_target_pairs={{0,1},{1,0},{2,3},{3,2},{4,5},{5,4},{6,7},{7,6},{8,9},{9,8},{10,11... | collective-permute-start | bytes 589832 | tf_op jit(solution)/shard_map/ppermute | solution.py:201
  117.6 2.3 %collective-permute-start.6 = (f32[384,128]{1,0:T(8,128)S(1)}, f32[384,128]{1,0:T(8,128)S(1)}, u32[]{:S(2)}, u32[]{:S(2)}) collective-permute-start(f32[384,128]{1,0:T(8,128)S(1)} %get-tuple-element.59), channel_id=1, source_target_pairs={{0,1},{1,0},{2,3},{3,2},{4,5},{5,4},{6,7},{7,6},{8,9},{9,8},{10,11... | collective-permute-start | bytes 589832 | tf_op jit(solution)/shard_map/ppermute | solution.py:201
  118.1 24.2 %copy-start.10 = (f32[360]{0:T(512)S(1)}, f32[360]{0:T(512)}, u32[]{:S(2)}) copy-start(f32[360]{0:T(512)} %param.20) | copy-start | bytes 4324
  118.1 24.2 %copy-start.11 = (f32[360]{0:T(512)S(1)}, f32[360]{0:T(512)}, u32[]{:S(2)}) copy-start(f32[360]{0:T(512)} %param.19) | copy-start | bytes 4324
  118.1 24.2 %copy-start.12 = (f32[360]{0:T(512)S(1)}, f32[360]{0:T(512)}, u32[]{:S(2)}) copy-start(f32[360]{0:T(512)} %param.21) | copy-start | bytes 4324
  118.2 24.2 %copy-start.13 = (f32[360]{0:T(512)S(1)}, f32[360]{0:T(512)}, u32[]{:S(2)}) copy-start(f32[360]{0:T(512)} %param.22) | copy-start | bytes 4324
  118.3 9.9 %collective-permute-start.5 = (f32[8,72,128]{2,1,0:T(8,128)S(1)}, f32[8,72,128]{2,1,0:T(8,128)S(1)}, u32[]{:S(2)}, u32[]{:S(2)}) collective-permute-start(f32[8,72,128]{2,1,0:T(8,128)S(1)} %shard_map.188.basis_half_ref), channel_id=1, source_target_pairs={{0,2},{1,3},{2,0},{3,1},{4,6},{5,7},{6,4},{7,5},{8,10},{9,11},{10,... | collective-permute-start | bytes 884744 | tf_op jit(solution)/shard_map/ppermute | solution.py:204
  119.9 26.3 %copy-start.9 = (f32[48,1,3456]{2,1,0:T(1,128)S(1)}, f32[48,1,3456]{2,1,0:T(1,128)}, u32[]{:S(2)}) copy-start(f32[48,1,3456]{2,1,0:T(1,128)} %param.13) | copy-start | bytes 1990660
  120.1 13.6 %collective-permute-start.7 = (f32[8,72,128]{2,1,0:T(8,128)S(1)}, f32[8,72,128]{2,1,0:T(8,128)S(1)}, u32[]{:S(2)}, u32[]{:S(2)}) collective-permute-start(f32[8,72,128]{2,1,0:T(8,128)S(1)} %shard_map.190.gram_half_ref), channel_id=1, source_target_pairs={{0,2},{1,3},{2,0},{3,1},{4,6},{5,7},{6,4},{7,5},{8,10},{9,11},{10,... | collective-permute-start | bytes 884744 | tf_op jit(solution)/shard_map/ppermute | solution.py:204
  142.2 1.4 collective-permute-start.8
where the time goes:
time: 149 us; the launch traced here: 148 us
  waiting for transfers between devices  71.1 us (48%)
  Pallas kernels  33.8 us (23%)
  starting transfers between devices  29.5 us (20%)
  local copies, waits for them, and re-layouts  8.4 us (6%)
  other arithmetic  4.53 us (3%)
    all_to_all x5, waiting for transfers between devices, exchange(): lax.all_to_all(value, 'shard', split_axis=0, concat_axis=0, tiled=True)  43.4 us
    pallas_call x14, Pallas kernels, call(): pl.pallas_call(kernel, out_shape=shapes, grid=grid, in_specs=[s or vmem f...  33.8 us
    ppermute x4, waiting for transfers between devices, over_chip(): return lax.ppermute(value, 'tensor', chip_pairs)  25 us
    all_to_all x5, starting transfers between devices, exchange(): lax.all_to_all(value, 'shard', split_axis=0, concat_axis=0, tiled=True)  23.4 us
    unnamed x32, local copies, waits for them, and re-layouts  6.84 us
    ppermute x4, starting transfers between devices, over_chip(): return lax.ppermute(value, 'tensor', chip_pairs)  5.47 us
  transfers between devices with their start and end apart: 14, of which 11 were waited for; matrix products, arithmetic and copies ran while one was open for 5% of the time, Pallas kernels for 20%

commit v1 on v0

--- a/solution.py
+++ b/solution.py
@@ -143,13 +143,14 @@
         out_specs=out_specs or [vmem] * len(shapes),
         scratch_shapes=list(scratch),
         input_output_aliases=aliases or {},
-        compiler_params=pltpu.CompilerParams(vmem_limit_bytes=40 * 2**20),
+        compiler_params=pltpu.CompilerParams(vmem_limit_bytes=32 * 2**20),
     )(*args)
     return result[0] if single else result
 
 
 SMEM = pl.BlockSpec(memory_space=pltpu.SMEM)
 ANY = pl.BlockSpec(memory_space=pl.ANY)
+HBM = pl.BlockSpec(memory_space=pltpu.HBM)
 
 
 def body(
@@ -255,7 +256,7 @@
                 held.append(jnp.where(matrix >= 0, block, 0.0))
             store_block(out_ref, group, base, jnp.concatenate(held, axis=1), rows, owned)
 
-    table_scratch = [pltpu.SMEM((shards * MCAP,), jnp.int32), pltpu.SMEM((shards,), jnp.int32)]
+    count_scratch = pltpu.SMEM((shards,), jnp.int32)
     stage_scratch = pltpu.VMEM((matrix_total, rows, columns), F32)
 
     def slot_masks(edges_ref):
@@ -263,23 +264,49 @@
         return [(lane >= edges_ref[k]) & (lane < edges_ref[k + 1]) for k in range(slots)]
 
 
-    def pack_gradient(grad_ref, basis_ref, out_ref, line_ref):
-        send_tiles(grad_ref, line_ref, out_ref, strip_rows)
-        for group in range(shards):
-            held = [
-                basis_ref[:, matrix * columns : (matrix + 1) * columns]
-                for matrix in slot_matrix[group]
-            ]
-            held += [jnp.zeros((rows, columns), F32)] * (slots - len(held))
-            store_block(out_ref, group, 0, jnp.concatenate(held, axis=1), rows, strip)
+    def pack_gradient(grad_ref, out_ref, line_ref, dense_ref, send_ref, in_sems, out_sems):
+        parts = 2 if rows % 16 == 0 else 1
+        part_rows = rows // parts
+        size = part_rows * line_tiles
+        fetches = [
+            pltpu.make_async_copy(
+                grad_ref.at[pl.ds(p * size, size)], dense_ref.at[pl.ds(p * size, size)], in_sems.at[p]
+            )
+            for p in range(parts)
+        ]
+        for fetch in fetches:
+            fetch.start()
+        for p, fetch in enumerate(fetches):
+            fetch.wait()
+            for j in range(line_tiles):
+                line_ref[p * part_rows : (p + 1) * part_rows, j * LANES : (j + 1) * LANES] = dense_ref[
+                    pl.ds(p * size + j, part_rows, stride=line_tiles), :
+                ]
+        puts = []
+        for group in range(shards):
+            store_block(send_ref, group, 0, gather_line(line_ref, group), rows, share)
+            puts.append(
+                pltpu.make_async_copy(send_ref.at[group], out_ref.at[group], out_sems.at[group])
+            )
+            puts[-1].start()
+        for put in puts:
+            put.wait()
 
     grad_dense = gradient.reshape(dense)
     basis_line = left_basis.reshape(rows, matrix_total * columns)
     send_one = call(
         pack_gradient,
-        (shards, strip_rows + tile_rows, LANES),
-        (grad_dense, basis_line),
-        scratch=[line_scratch],
+        (shards, tile_rows, LANES),
+        (pltpu.with_memory_space_constraint(grad_dense, pltpu.HBM),),
+        specs=[HBM],
+        out_specs=[HBM],
+        scratch=[
+            line_scratch,
+            pltpu.VMEM(dense, F32),
+            pltpu.VMEM((shards, tile_rows, LANES), F32),
+            pltpu.SemaphoreType.DMA((2,)),
+            pltpu.SemaphoreType.DMA((shards,)),
+        ],
     )
     came_one = exchange(send_one)
 
@@ -290,24 +317,31 @@
         fill_owned_table(owner_ref, table_ref, count_ref)
         for matrix in range(matrix_total):
             stage_ref[matrix] = basis_ref[:, matrix * columns : (matrix + 1) * columns]
-        send_tiles(second_ref, line_ref, out_ref, owned_rows)
+        send_tiles(second_ref, line_ref, out_ref, head_rows)
         send_owned(stage_ref, table_ref, out_ref, 0)
-
-    send_two = call(
+        for group in range(shards):
+            held = [stage_ref[matrix] for matrix in slot_matrix[group]]
+            held += [jnp.zeros((rows, columns), F32)] * (slots - len(held))
+            store_block(out_ref, group, owned_rows, jnp.concatenate(held, axis=1), rows, strip)
+
+    head_rows = owned_rows + strip_rows
+    send_two, owned_table = call(
         pack_second,
-        (shards, owned_rows + tile_rows, LANES),
+        [
+            (shards, head_rows + tile_rows, LANES),
+            jax.ShapeDtypeStruct((shards * MCAP,), jnp.int32),
+        ],
         (owners, second_moment.reshape(dense), basis_line),
         specs=[SMEM, None, None],
-        scratch=table_scratch + [stage_scratch, line_scratch],
+        out_specs=[pl.BlockSpec(memory_space=pltpu.VMEM), SMEM],
+        scratch=[count_scratch, stage_scratch, line_scratch],
     )
     came_one, send_two = together((came_one, send_two))
     came_two = exchange(send_two)
 
 
-    def gram_partials(edges_ref, came_ref, grad_ref, strips_ref, gram_ref, turned_ref):
-        unpack_columns(came_ref, strip_rows, grad_ref, shards, rows, share)
-        for source in range(shards):
-            strips_ref[source] = came_ref[source, 0:strip_rows, :]
+    def gram_partials(edges_ref, came_ref, grad_ref, gram_ref, turned_ref):
+        unpack_columns(came_ref, 0, grad_ref, shards, rows, share)
         turned_ref[...] = jnp.zeros_like(turned_ref)
         for rank in range(ranks):
             turned_ref[rank * LANES : rank * LANES + columns, :] = grad_ref[
@@ -332,9 +366,9 @@
                 )
 
     strip_shape = (shards, strip_rows, LANES)
-    grad_full, strips_own, gram_parts = call(
+    grad_full, gram_parts = call(
         gram_partials,
-        [(width, wide), strip_shape, (ranks,) + strip_shape],
+        [(width, wide), (ranks,) + strip_shape],
         (my_edges, came_one),
         specs=[SMEM, None],
         scratch=[pltpu.VMEM((ranks * LANES, wide), F32)],
@@ -346,9 +380,6 @@
     kept = lax.dynamic_index_in_dim(parts, my_core, 1, False) + over_core(for_core)
     for_chip = lax.dynamic_index_in_dim(kept, 1 - my_chip, 0, False)
     gram_strips = lax.dynamic_index_in_dim(kept, my_chip, 0, False) + over_chip(for_chip)
-
-    strips_chip = over_chip(strips_own)
-    pair = over_core(jnp.stack([strips_own, strips_chip]))
 
 
     def pack_first(first_ref, grad_ref, out_ref, new_ref, line_ref):
@@ -383,7 +414,10 @@
     came_three = exchange(send_three)
 
 
-    half_shape = jax.ShapeDtypeStruct((slots, width, width), BF16)
+    strips_own = came_two[:, owned_rows:head_rows]
+    strips_chip = over_chip(strips_own)
+    pair = over_core(jnp.stack([strips_own, strips_chip]))
+
 
     def rotate_gradient(
         rank_ref,
@@ -393,12 +427,8 @@
         pair_ref,
         grad_ref,
         came_ref,
-        high_ref,
-        low_ref,
-        high_turned_ref,
-        low_turned_ref,
+        basis_ref,
         second_ref,
-        basis_ref,
     ):
         rank = rank_ref[0]
         for group in range(shards):
@@ -419,85 +449,19 @@
                     jnp.where(first, odd[1], odd[0]),
                 ]
                 basis_ref[k, at, :] = jnp.concatenate(ordered, axis=1)
-        unpack_columns(came_ref, owned_rows, second_ref, shards, rows, share)
+        unpack_columns(came_ref, head_rows, second_ref, shards, rows, share)
         grad = parts_of(grad_ref[...])
         hat = jnp.zeros((width, wide), F32)
         for k, mask in enumerate(slot_masks(edges_ref)):
-            basis = basis_ref[k]
-            high_ref[k], low_ref[k] = parts_of(basis)
-            turned = parts_of(basis.T)
-            high_turned_ref[k], low_turned_ref[k] = turned
-            hat = jnp.where(mask, product(turned, grad), hat)
+            hat = jnp.where(mask, product(parts_of(basis_ref[k].T), grad), hat)
         second_ref[...] = 0.95 * second_ref[...] + 0.05 * hat * hat
 
-    high, low, high_turned, low_turned, second_full = call(
+    basis_full, second_full = call(
         rotate_gradient,
-        [half_shape] * 4 + [(width, wide)],
+        [(slots, width, width), (width, wide)],
         (rank_arg, my_edges, strips_own, strips_chip, pair, grad_full, came_two),
         specs=[SMEM, SMEM] + [None] * 5,
-        scratch=[pltpu.VMEM((slots, width, width), F32)],
-    )
-
-
-    def new_grams(owner_ref, came_ref, gram_ref, out_ref, table_ref, count_ref, stage_ref):
-        fill_owned_table(owner_ref, table_ref, count_ref)
-        total = [None] * matrix_total
-        for group in range(shards):
-            block = load_block(came_ref, group, 0, rows, strip)
-            for k, matrix in enumerate(slot_matrix[group]):
-                part = block[:, k * columns : (k + 1) * columns]
-                total[matrix] = part if total[matrix] is None else total[matrix] + part
-        for matrix in range(matrix_total):
-            gram = gram_ref[:, matrix * columns : (matrix + 1) * columns]
-            stage_ref[matrix] = 0.95 * gram + 0.05 * total[matrix]
-        send_owned(stage_ref, table_ref, out_ref, 0)
-
-    send_four = call(
-        new_grams,
-        (shards, owned_rows, LANES),
-        (owners, came_three, left_gram.reshape(rows, matrix_total * columns)),
-        specs=[SMEM, None, None],
-        scratch=table_scratch + [stage_scratch],
-    )
-    came_three, send_four = together((came_three, send_four))
-    came_four = exchange(send_four)
-
-
-    def directions(
-        edges_ref,
-        came_ref,
-        grad_ref,
-        second_ref,
-        high_ref,
-        low_ref,
-        high_turned_ref,
-        low_turned_ref,
-        send_ref,
-        moment_ref,
-    ):
-        unpack_columns(came_ref, strip_rows, moment_ref, shards, rows, share)
-        masks = slot_masks(edges_ref)
-        moment = parts_of(0.9 * moment_ref[...] + 0.1 * grad_ref[...])
-        hat = jnp.zeros((width, wide), F32)
-        for k, mask in enumerate(masks):
-            hat = jnp.where(mask, product((high_turned_ref[k], low_turned_ref[k]), moment), hat)
-        step = parts_of(adam_direction(hat, second_ref[...]))
-        turned = jnp.zeros((width, wide), F32)
-        for k, mask in enumerate(masks):
-            turned = jnp.where(mask, product((high_ref[k], low_ref[k]), step), turned)
-        moment_ref[...] = turned
-        pack_columns(moment_ref, send_ref, 0, shards, rows, share)
-        pack_columns(second_ref, send_ref, tile_rows, shards, rows, share)
-
-    send_five = call(
-        directions,
-        (shards, 2 * tile_rows, LANES),
-        (my_edges, came_three, grad_full, second_full, high, low, high_turned, low_turned),
-        specs=[SMEM] + [None] * 7,
-        scratch=[pltpu.VMEM((width, wide), F32)],
-    )
-    came_four, send_five = together((came_four, send_five))
-    came_five = exchange(send_five)
+    )
 
 
     def split_owned(rank_ref, came_ref, strips_ref, mine_ref, other_ref, whole_ref):
@@ -538,6 +502,67 @@
         return strips, half, over_chip(half)
 
     _, basis_half, basis_far = collect(came_two)
+
+
+    def new_grams(table_ref, came_ref, gram_ref, out_ref, stage_ref):
+        total = [None] * matrix_total
+        for group in range(shards):
+            block = load_block(came_ref, group, 0, rows, strip)
+            for k, matrix in enumerate(slot_matrix[group]):
+                part = block[:, k * columns : (k + 1) * columns]
+                total[matrix] = part if total[matrix] is None else total[matrix] + part
+        for matrix in range(matrix_total):
+            gram = gram_ref[:, matrix * columns : (matrix + 1) * columns]
+            stage_ref[matrix] = 0.95 * gram + 0.05 * total[matrix]
+        send_owned(stage_ref, table_ref, out_ref, 0)
+
+    send_four = call(
+        new_grams,
+        (shards, owned_rows, LANES),
+        (owned_table, came_three, left_gram.reshape(rows, matrix_total * columns)),
+        specs=[SMEM, None, None],
+        scratch=[stage_scratch],
+    )
+    came_three, send_four, second_full, basis_half, basis_far = together(
+        (came_three, send_four, second_full, basis_half, basis_far)
+    )
+    came_four = exchange(send_four)
+
+
+    def directions(
+        edges_ref,
+        came_ref,
+        grad_ref,
+        second_ref,
+        basis_ref,
+        send_ref,
+        moment_ref,
+    ):
+        unpack_columns(came_ref, strip_rows, moment_ref, shards, rows, share)
+        masks = slot_masks(edges_ref)
+        moment = parts_of(0.9 * moment_ref[...] + 0.1 * grad_ref[...])
+        hat = jnp.zeros((width, wide), F32)
+        for k, mask in enumerate(masks):
+            hat = jnp.where(mask, product(parts_of(basis_ref[k].T), moment), hat)
+        step = parts_of(adam_direction(hat, second_ref[...]))
+        turned = jnp.zeros((width, wide), F32)
+        for k, mask in enumerate(masks):
+            turned = jnp.where(mask, product(parts_of(basis_ref[k]), step), turned)
+        moment_ref[...] = turned
+        pack_columns(moment_ref, send_ref, 0, shards, rows, share)
+        pack_columns(second_ref, send_ref, tile_rows, shards, rows, share)
+
+    send_five = call(
+        directions,
+        (shards, 2 * tile_rows, LANES),
+        (my_edges, came_three, grad_full, second_full, basis_full),
+        specs=[SMEM] + [None] * 4,
+        scratch=[pltpu.VMEM((width, wide), F32)],
+    )
+    came_four, send_five = together((came_four, send_five))
+    came_five = exchange(send_five)
+
+
     gram_out, gram_half, gram_far = collect(came_four)
 
     def refresh(
@@ -546,11 +571,16 @@
         basis_far_ref,
         gram_half_ref,
         gram_far_ref,
+        weight_ref,
         mine_ref,
         other_ref,
+        weight_out_ref,
         basis_ref,
         gram_ref,
+        sem,
     ):
+        fetch = pltpu.make_async_copy(weight_ref, weight_out_ref, sem)
+        fetch.start()
         rank = rank_ref[0]
         first = rank < 2
         for out, half_ref, far_ref in (
@@ -574,13 +604,15 @@
         even_core = rank % 2 == 0
         mine_ref[...] = jnp.where(even_core, low, odd)
         other_ref[...] = jnp.where(even_core, odd, low)
-
-    frame_mine, frame_other = call(
+        fetch.wait()
+
+    weight_dense = pltpu.with_memory_space_constraint(weight.reshape(dense), pltpu.HBM)
+    frame_mine, frame_other, weight_near = call(
         refresh,
-        [(columns, width), (columns, width)],
-        (rank_arg, basis_half, basis_far, gram_half, gram_far),
-        specs=[SMEM] + [None] * 4,
-        scratch=[pltpu.VMEM((width, width), F32)] * 2,
+        [(columns, width), (columns, width), dense],
+        (rank_arg, basis_half, basis_far, gram_half, gram_far, weight_dense),
+        specs=[SMEM] + [None] * 4 + [HBM],
+        scratch=[pltpu.VMEM((width, width), F32)] * 2 + [pltpu.SemaphoreType.DMA(())],
     )
     frame_came = over_core(frame_other)
     pair_out = jnp.where(
@@ -608,7 +640,7 @@
         close_line(line_ref, second_out_ref)
 
     weight_out, second_out = call(
-        take_back, [dense, dense], (came_five, weight.reshape(dense)), scratch=[line_scratch]
+        take_back, [dense, dense], (came_five, weight_near), scratch=[line_scratch]
     )
 
     bias_first_new = 0.9 * bias_first + 0.1 * bias_gradient

time: 149 us -> 145 us (0.973)
  waiting for transfers between devices: 71.1 us -> 66.5 us
    ppermute x4, waiting for transfers between devices: 25 us -> 20.9 us  [over_chip(): return lax.ppermute(value, 'tensor', chip_pairs)]
    all_to_all x5, waiting for transfers between devices: 43.4 us -> 40 us  [exchange(): lax.all_to_all(value, 'shard', split_axis=0, concat_axis=0, tiled=True)]
    ppermute x5, waiting for transfers between devices: 2.8 us -> 5.56 us  [over_core(): return lax.ppermute(value, 'tensor', core_pairs)]
    unnamed x32 -> x36, local copies, waits for them, and re-layouts: 6.84 us -> 7.4 us
  transfers between devices with their start and end apart: 14 -> 14, of which waited for: 11 -> 12; matrix products, arithmetic and copies ran while one was open for 5% -> 4% of each run, Pallas kernels for 20% -> 21%
where the time goes in v1:
time: 145 us; the launch traced here: 144 us
  waiting for transfers between devices  66.5 us (46%)
  Pallas kernels  34.5 us (24%)
  starting transfers between devices  28.8 us (20%)
  local copies, waits for them, and re-layouts  9.8 us (7%)
  other arithmetic  3.76 us (3%)
    all_to_all x5, waiting for transfers between devices, exchange(): lax.all_to_all(value, 'shard', split_axis=0, concat_axis=0, tiled=True)  40 us
    pallas_call x14, Pallas kernels, call(): pl.pallas_call(kernel, out_shape=shapes, grid=grid, in_specs=[s or vmem f...  34.5 us
    all_to_all x5, starting transfers between devices, exchange(): lax.all_to_all(value, 'shard', split_axis=0, concat_axis=0, tiled=True)  22 us
    ppermute x4, waiting for transfers between devices, over_chip(): return lax.ppermute(value, 'tensor', chip_pairs)  20.9 us
    unnamed x36, local copies, waits for them, and re-layouts  7.4 us
    ppermute x4, starting transfers between devices, over_chip(): return lax.ppermute(value, 'tensor', chip_pairs)  6.17 us
    ppermute x5, waiting for transfers between devices, over_core(): return lax.ppermute(value, 'tensor', core_pairs)  5.56 us
  transfers between devices with their start and end apart: 14, of which 12 were waited for; matrix products, arithmetic and copies ran while one was open for 4% of the time, Pallas kernels for 21%

profile of v1, /device:TPU:0, one launch (start us, length us, event | category | flops | bytes accessed | tf_op | source)
XLA Modules:
  0.0 144.3 jit_solution(657770126251430777)
XLA Ops:
  0.7 2.4 %shard_map.179 = f32[8,168,128]{2,1,0:T(8,128)} custom-call(f32[1296,128]{1,0:T(8,128)} %bitcast.36), custom_call_target="tpu_custom_call" | custom-call | tf_op jit(solution)/shard_map/pallas_call | solution.py:138
  3.0 7.3 %all-to-all-start = ((f32[8,168,128]{2,1,0:T(8,128)}), f32[8,168,128]{2,1,0:T(8,128)S(1)}, u32[]{:S(2)}, u32[]{:S(2)}) async-start(f32[8,168,128]{2,1,0:T(8,128)} %shard_map.179), calls=%async_computation | async-start | bytes 1376256 | tf_op jit(solution)/shard_map/all_to_all | solution.py:208
  10.5 3.4 %shard_map.180 = (f32[8,312,128]{2,1,0:T(8,128)}, s32[16]{0:T(128)S(1)}) custom-call(s32[10]{0:T(128)S(1)} %reshape.53.owner_ref, f32[1296,128]{1,0:T(8,128)S(1)} %bitcast.43, f32[48,960]{1,0:T(8,128)S(1)} %bitcast.41), custom_call_target="tpu_custom_call" | custom-call | tf_op jit(solution)/shard_map/pallas_call | solution.py:138
  13.9 14.4 %all-to-all-done.came_ref = f32[8,168,128]{2,1,0:T(8,128)S(1)} async-done(((f32[8,168,128]{2,1,0:T(8,128)}), f32[8,168,128]{2,1,0:T(8,128)S(1)}, u32[]{:S(2)}, u32[]{:S(2)}) %all-to-all-start) | async-done | bytes 688160 | tf_op jit(solution)/shard_map/all_to_all | solution.py:208
  28.3 3.6 %all-to-all-start.1 = ((f32[8,312,128]{2,1,0:T(8,128)}), f32[8,312,128]{2,1,0:T(8,128)S(1)}, u32[]{:S(2)}, u32[]{:S(2)}) async-start(f32[8,312,128]{2,1,0:T(8,128)} %get-tuple-element.42), calls=%async_computation.1 | async-start | bytes 2555904 | tf_op jit(solution)/shard_map/all_to_all | solution.py:208
  32.0 0.7 fusion.1.edges_ref
  32.7 2.3 %shard_map.182 = (f32[384,512]{1,0:T(8,128)S(1)}, f32[4,8,72,128]{3,2,1,0:T(8,128)S(1)}) custom-call(s32[3]{0:T(128)S(1)} %fusion.1.edges_ref, f32[8,168,128]{2,1,0:T(8,128)S(1)} %all-to-all-done.came_ref), custom_call_target="tpu_custom_call" | custom-call | tf_op jit(solution)/shard_map/pallas_call | solution.py:138
  35.0 1.0 copy-done.2
  36.0 0.9 dynamic-slice_bitcast_fusion
  36.9 2.3 %collective-permute-done = f32[2,8,72,128]{3,2,1,0:T(8,128)} collective-permute-done((f32[2,8,72,128]{3,2,1,0:T(8,128)}, f32[2,8,72,128]{3,2,1,0:T(8,128)}, u32[]{:S(2)}, u32[]{:S(2)}) %collective-permute-start) | collective-permute-done | bytes 589856 | tf_op jit(solution)/shard_map/ppermute | solution.py:202
  39.2 1.3 bitcast_add_fusion
  40.6 0.8 copy-done.9
  41.4 0.7 dynamic-slice_bitcast_fusion.1
  42.1 1.5 %collective-permute-start.1 = (f32[8,72,128]{2,1,0:T(8,128)}, f32[8,72,128]{2,1,0:T(8,128)}, u32[]{:S(2)}, u32[]{:S(2)}) collective-permute-start(f32[8,72,128]{2,1,0:T(8,128)} %dynamic-slice_bitcast_fusion.1), channel_id=1, source_target_pairs={{0,2},{1,3},{2,0},{3,1},{4,6},{5,7},{6,4},{7,5},{8,10},{9,11},{10,... | collective-permute-start | bytes 884744 | tf_op jit(solution)/shard_map/ppermute | solution.py:205
  43.6 1.6 %shard_map.181 = (f32[8,240,128]{2,1,0:T(8,128)}, f32[1296,128]{1,0:T(8,128)}) custom-call(f32[1296,128]{1,0:T(8,128)S(1)} %bitcast.44, f32[1296,128]{1,0:T(8,128)S(1)} %bitcast.37), custom_call_target="tpu_custom_call" | custom-call | tf_op jit(solution)/shard_map/pallas_call | solution.py:138
  45.2 6.2 %collective-permute-done.1 = f32[8,72,128]{2,1,0:T(8,128)} collective-permute-done((f32[8,72,128]{2,1,0:T(8,128)}, f32[8,72,128]{2,1,0:T(8,128)}, u32[]{:S(2)}, u32[]{:S(2)}) %collective-permute-start.1) | collective-permute-done | bytes 294944 | tf_op jit(solution)/shard_map/ppermute | solution.py:205
  51.5 1.1 bitcast_add_fusion.1.strips_ref
  52.6 0.8 shard_map.183
  53.3 9.5 %all-to-all-done.1.came_ref = f32[8,312,128]{2,1,0:T(8,128)S(1)} async-done(((f32[8,312,128]{2,1,0:T(8,128)}), f32[8,312,128]{2,1,0:T(8,128)S(1)}, u32[]{:S(2)}, u32[]{:S(2)}) %all-to-all-start.1) | async-done | bytes 1277984 | tf_op jit(solution)/shard_map/all_to_all | solution.py:208
  62.8 3.6 %all-to-all-start.2 = ((f32[8,240,128]{2,1,0:T(8,128)}), f32[8,240,128]{2,1,0:T(8,128)S(1)}, u32[]{:S(2)}, u32[]{:S(2)}) async-start(f32[8,240,128]{2,1,0:T(8,128)} %shard_map.183), calls=%async_computation.2 | async-start | bytes 1966080 | tf_op jit(solution)/shard_map/all_to_all | solution.py:208
  66.5 1.6 %collective-permute-start.2 = (f32[8,72,128]{2,1,0:T(8,128)S(1)}, f32[8,72,128]{2,1,0:T(8,128)S(1)}, u32[]{:S(2)}, u32[]{:S(2)}) collective-permute-start(f32[8,72,128]{2,1,0:T(8,128)S(1)} %get-tuple-element.86.own_ref), channel_id=1, source_target_pairs={{0,2},{1,3},{2,0},{3,1},{4,6},{5,7},{6,4},{7,5},{8,10},{9,11},{10,... | collective-permute-start | bytes 884744 | tf_op jit(solution)/shard_map/ppermute | solution.py:205
  68.1 7.2 %collective-permute-done.2.chip_ref = f32[8,72,128]{2,1,0:T(8,128)S(1)} collective-permute-done((f32[8,72,128]{2,1,0:T(8,128)S(1)}, f32[8,72,128]{2,1,0:T(8,128)S(1)}, u32[]{:S(2)}, u32[]{:S(2)}) %collective-permute-start.2) | collective-permute-done | bytes 294944 | tf_op jit(solution)/shard_map/ppermute | solution.py:205
  75.4 1.9 %shard_map.186 = (f32[2,96,384]{2,1,0:T(8,128)}, f32[384,128]{1,0:T(8,128)S(1)}, f32[384,128]{1,0:T(8,128)S(1)}) custom-call(s32[1]{0:T(128)} %bitcast.9.rank_ref, f32[8,312,128]{2,1,0:T(8,128)S(1)} %all-to-all-done.1.came_ref), custom_call_target="tpu_custom_call" | custom-call | tf_op jit(solution)/shard_map/pallas_call | solution.py:138
  77.3 0.5 collective-permute-start.4
  77.8 1.1 collective-permute-done.4.other_ref
  79.0 1.6 %collective-permute-start.5 = (f32[8,72,128]{2,1,0:T(8,128)S(1)}, f32[8,72,128]{2,1,0:T(8,128)}, u32[]{:S(2)}, u32[]{:S(2)}) collective-permute-start(f32[8,72,128]{2,1,0:T(8,128)S(1)} %shard_map.187.basis_half_ref), channel_id=1, source_target_pairs={{0,2},{1,3},{2,0},{3,1},{4,6},{5,7},{6,4},{7,5},{8,10},{9,11},{10,... | collective-permute-start | bytes 884744 | tf_op jit(solution)/shard_map/ppermute | solution.py:205
  80.6 2.6 %shard_map.185 = (f32[2,384,384]{2,1,0:T(8,128)S(1)}, f32[384,512]{1,0:T(8,128)S(1)}) custom-call(s32[1]{0:T(128)} %bitcast.9.rank_ref, s32[3]{0:T(128)S(1)} %fusion.1.edges_ref, f32[8,72,128]{2,1,0:T(8,128)S(1)} %get-tuple-element.86.own_ref, f32[8,72,128]{2,1,0:T(8,128)S(1)} %collective-permute-done.2.chip_ref, ...), custom_call_target="tpu_custom_call" | custom-call | tf_op jit(solution)/shard_map/pallas_call | solution.py:138
  83.3 1.0 copy-done.3
  84.3 0.9 copy-done.5
  85.2 5.9 %all-to-all-done.2.came_ref = f32[8,240,128]{2,1,0:T(8,128)S(1)} async-done(((f32[8,240,128]{2,1,0:T(8,128)}), f32[8,240,128]{2,1,0:T(8,128)S(1)}, u32[]{:S(2)}, u32[]{:S(2)}) %all-to-all-start.2) | async-done | bytes 983072 | tf_op jit(solution)/shard_map/all_to_all | solution.py:208
  91.0 1.7 %shard_map.184 = f32[8,72,128]{2,1,0:T(8,128)} custom-call(s32[16]{0:T(128)S(1)} %get-tuple-element.47.table_ref, f32[8,240,128]{2,1,0:T(8,128)S(1)} %all-to-all-done.2.came_ref, f32[48,960]{1,0:T(8,128)S(1)} %bitcast.42), custom_call_target="tpu_custom_call" | custom-call | tf_op jit(solution)/shard_map/pallas_call | solution.py:138
  92.8 3.6 %all-to-all-start.3 = ((f32[8,72,128]{2,1,0:T(8,128)}), f32[8,72,128]{2,1,0:T(8,128)S(1)}, u32[]{:S(2)}, u32[]{:S(2)}) async-start(f32[8,72,128]{2,1,0:T(8,128)} %shard_map.184), calls=%async_computation.3 | async-start | bytes 589824 | tf_op jit(solution)/shard_map/all_to_all | solution.py:208
  96.4 1.3 copy-done.4
  97.7 1.1 copy-done.6
  98.8 3.9 %shard_map.188 = f32[8,336,128]{2,1,0:T(8,128)S(1)} custom-call(s32[3]{0:T(128)S(1)} %fusion.1.edges_ref, f32[8,240,128]{2,1,0:T(8,128)S(1)} %all-to-all-done.2.came_ref, f32[384,512]{1,0:T(8,128)S(1)} %get-tuple-element.49.grad_ref, f32[384,512]{1,0:T(8,128)S(1)} %copy-done.6, f32[2,384,384]{2,1,0:T(8,128)S(1)} %copy-done.4), custom_call_target="tpu_custom_call" | custom-call | tf_op jit(solution)/shard_map/pallas_call | solution.py:138
  102.7 1.1 copy-done
  103.8 2.3 %all-to-all-done.3.came_ref = f32[8,72,128]{2,1,0:T(8,128)S(1)} async-done(((f32[8,72,128]{2,1,0:T(8,128)}), f32[8,72,128]{2,1,0:T(8,128)S(1)}, u32[]{:S(2)}, u32[]{:S(2)}) %all-to-all-start.3) | async-done | bytes 294944 | tf_op jit(solution)/shard_map/all_to_all | solution.py:208
  106.1 3.8 %all-to-all-start.4 = ((f32[8,336,128]{2,1,0:T(8,128)}), f32[8,336,128]{2,1,0:T(8,128)S(1)}, u32[]{:S(2)}, u32[]{:S(2)}) async-start(f32[8,336,128]{2,1,0:T(8,128)} %copy-done), calls=%async_computation.4 | async-start | bytes 2752512 | tf_op jit(solution)/shard_map/all_to_all | solution.py:208
  109.9 1.9 %shard_map.189 = (f32[2,96,384]{2,1,0:T(8,128)}, f32[384,128]{1,0:T(8,128)S(1)}, f32[384,128]{1,0:T(8,128)S(1)}) custom-call(s32[1]{0:T(128)} %bitcast.9.rank_ref, f32[8,72,128]{2,1,0:T(8,128)S(1)} %all-to-all-done.3.came_ref), custom_call_target="tpu_custom_call" | custom-call | tf_op jit(solution)/shard_map/pallas_call | solution.py:138
  111.9 1.4 collective-permute-done.6.other_ref
  113.5 1.6 %collective-permute-start.7 = (f32[8,72,128]{2,1,0:T(8,128)S(1)}, f32[8,72,128]{2,1,0:T(8,128)S(1)}, u32[]{:S(2)}, u32[]{:S(2)}) collective-permute-start(f32[8,72,128]{2,1,0:T(8,128)S(1)} %shard_map.190.gram_half_ref), channel_id=1, source_target_pairs={{0,2},{1,3},{2,0},{3,1},{4,6},{5,7},{6,4},{7,5},{8,10},{9,11},{10,... | collective-permute-start | bytes 884744 | tf_op jit(solution)/shard_map/ppermute | solution.py:205
  115.1 7.6 %collective-permute-done.7.gram_far_ref = f32[8,72,128]{2,1,0:T(8,128)S(1)} collective-permute-done((f32[8,72,128]{2,1,0:T(8,128)S(1)}, f32[8,72,128]{2,1,0:T(8,128)S(1)}, u32[]{:S(2)}, u32[]{:S(2)}) %collective-permute-start.7) | collective-permute-done | bytes 294944 | tf_op jit(solution)/shard_map/ppermute | solution.py:205
  122.6 9.5 %shard_map.191 = (f32[96,384]{1,0:T(8,128)S(1)}, f32[96,384]{1,0:T(8,128)S(1)}, f32[1296,128]{1,0:T(8,128)S(1)}) custom-call(s32[1]{0:T(128)} %bitcast.9.rank_ref, f32[8,72,128]{2,1,0:T(8,128)S(1)} %shard_map.187.basis_half_ref, f32[8,72,128]{2,1,0:T(8,128)} %collective-permute-done.5.basis_far_ref, f32[8,72,128]{2,1,0:T(8,128)S(1)} %shard_map.190.gram_half_ref, ...), custom_call_target="tpu_custom_call" | custom-call | tf_op jit(solution)/shard_map/pallas_call | solution.py:138
  132.3 0.6 multiply_subtract_fusion
  132.9 0.7 collective-permute-done.8
  133.6 0.7 maximum_select_fusion
  134.3 7.9 %all-to-all-done.4.came_ref = f32[8,336,128]{2,1,0:T(8,128)S(1)} async-done(((f32[8,336,128]{2,1,0:T(8,128)}), f32[8,336,128]{2,1,0:T(8,128)S(1)}, u32[]{:S(2)}, u32[]{:S(2)}) %all-to-all-start.4) | async-done | bytes 1376288 | tf_op jit(solution)/shard_map/all_to_all | solution.py:208
  142.3 2.1 %shard_map.192 = (f32[1296,128]{1,0:T(8,128)}, f32[1296,128]{1,0:T(8,128)}) custom-call(f32[8,336,128]{2,1,0:T(8,128)S(1)} %all-to-all-done.4.came_ref, f32[1296,128]{1,0:T(8,128)S(1)} %get-tuple-element.68.weight_ref), custom_call_target="tpu_custom_call" | custom-call | tf_op jit(solution)/shard_map/pallas_call | solution.py:138
  (40 shorter events, 0.8 us)
Async XLA Ops:
  0.6 9.7 %copy-start.16 = (s32[2,5]{1,0:T(2,128)S(1)}, s32[2,5]{1,0:T(2,128)}, u32[]{:S(2)}) copy-start(s32[2,5]{1,0:T(2,128)} %param.18) | copy-start | bytes 124
  0.6 9.8 %copy-start.10 = (f32[48,1,960]{2,1,0:T(1,128)S(1)}, f32[48,1,960]{2,1,0:T(1,128)}, u32[]{:S(2)}) copy-start(f32[48,1,960]{2,1,0:T(1,128)} %param.16) | copy-start | bytes 552964
  0.7 9.8 %copy-start.7 = (f32[48,1,3456]{2,1,0:T(1,128)S(1)}, f32[48,1,3456]{2,1,0:T(1,128)}, u32[]{:S(2)}) copy-start(f32[48,1,3456]{2,1,0:T(1,128)} %param.15) | copy-start | bytes 1990660
  3.0 25.3 %all-to-all-start = ((f32[8,168,128]{2,1,0:T(8,128)}), f32[8,168,128]{2,1,0:T(8,128)S(1)}, u32[]{:S(2)}, u32[]{:S(2)}) async-start(f32[8,168,128]{2,1,0:T(8,128)} %shard_map.179), calls=%async_computation | async-start | bytes 1376256 | tf_op jit(solution)/shard_map/all_to_all | solution.py:208
  28.3 34.5 %all-to-all-start.1 = ((f32[8,312,128]{2,1,0:T(8,128)}), f32[8,312,128]{2,1,0:T(8,128)S(1)}, u32[]{:S(2)}, u32[]{:S(2)}) async-start(f32[8,312,128]{2,1,0:T(8,128)} %get-tuple-element.42), calls=%async_computation.1 | async-start | bytes 2555904 | tf_op jit(solution)/shard_map/all_to_all | solution.py:208
  35.0 1.0 copy-start.2
  36.9 6.7 %copy-start.1 = (f32[48,1,3456]{2,1,0:T(1,128)S(1)}, f32[48,1,3456]{2,1,0:T(1,128)}, u32[]{:S(2)}) copy-start(f32[48,1,3456]{2,1,0:T(1,128)} %param.12) | copy-start | bytes 1990660
  36.9 6.7 %copy-start.8 = (f32[48,1,3456]{2,1,0:T(1,128)S(1)}, f32[48,1,3456]{2,1,0:T(1,128)}, u32[]{:S(2)}) copy-start(f32[48,1,3456]{2,1,0:T(1,128)} %param.14) | copy-start | bytes 1990660
  36.9 2.3 %collective-permute-start = (f32[2,8,72,128]{3,2,1,0:T(8,128)}, f32[2,8,72,128]{3,2,1,0:T(8,128)}, u32[]{:S(2)}, u32[]{:S(2)}) collective-permute-start(f32[2,8,72,128]{3,2,1,0:T(8,128)} %dynamic-slice_bitcast_fusion), channel_id=1, source_target_pairs={{0,1},{1,0},{2,3},{3,2},{4,5},{5,4},{6,7},{7,6},{8,9},{9,8},{10,11... | collective-permute-start | bytes 1769480 | tf_op jit(solution)/shard_map/ppermute | solution.py:202
  40.6 0.8 copy-start.9
  42.1 9.4 %collective-permute-start.1 = (f32[8,72,128]{2,1,0:T(8,128)}, f32[8,72,128]{2,1,0:T(8,128)}, u32[]{:S(2)}, u32[]{:S(2)}) collective-permute-start(f32[8,72,128]{2,1,0:T(8,128)} %dynamic-slice_bitcast_fusion.1), channel_id=1, source_target_pairs={{0,2},{1,3},{2,0},{3,1},{4,6},{5,7},{6,4},{7,5},{8,10},{9,11},{10,... | collective-permute-start | bytes 884744 | tf_op jit(solution)/shard_map/ppermute | solution.py:205
  62.8 28.2 %all-to-all-start.2 = ((f32[8,240,128]{2,1,0:T(8,128)}), f32[8,240,128]{2,1,0:T(8,128)S(1)}, u32[]{:S(2)}, u32[]{:S(2)}) async-start(f32[8,240,128]{2,1,0:T(8,128)} %shard_map.183), calls=%async_computation.2 | async-start | bytes 1966080 | tf_op jit(solution)/shard_map/all_to_all | solution.py:208
  66.5 8.7 %collective-permute-start.2 = (f32[8,72,128]{2,1,0:T(8,128)S(1)}, f32[8,72,128]{2,1,0:T(8,128)S(1)}, u32[]{:S(2)}, u32[]{:S(2)}) collective-permute-start(f32[8,72,128]{2,1,0:T(8,128)S(1)} %get-tuple-element.86.own_ref), channel_id=1, source_target_pairs={{0,2},{1,3},{2,0},{3,1},{4,6},{5,7},{6,4},{7,5},{8,10},{9,11},{10,... | collective-permute-start | bytes 884744 | tf_op jit(solution)/shard_map/ppermute | solution.py:205
  75.3 5.3 %copy-start.11 = (f32[48,1,960]{2,1,0:T(1,128)S(1)}, f32[48,1,960]{2,1,0:T(1,128)}, u32[]{:S(2)}) copy-start(f32[48,1,960]{2,1,0:T(1,128)} %param.17) | copy-start | bytes 552964
  75.3 5.4 %collective-permute-start.3 = (f32[2,8,72,128]{3,2,1,0:T(8,128)S(1)}, f32[2,8,72,128]{3,2,1,0:T(8,128)S(1)}, u32[]{:S(2)}, u32[]{:S(2)}) collective-permute-start(f32[2,8,72,128]{3,2,1,0:T(8,128)S(1)} %pad_maximum_fusion), channel_id=1, source_target_pairs={{0,1},{1,0},{2,3},{3,2},{4,5},{5,4},{6,7},{7,6},{8,9},{9,8},{10,11... | collective-permute-start | bytes 1769480 | tf_op jit(solution)/shard_map/ppermute | solution.py:202
  77.3 1.6 %collective-permute-start.4 = (f32[384,128]{1,0:T(8,128)S(1)}, f32[384,128]{1,0:T(8,128)S(1)}, u32[]{:S(2)}, u32[]{:S(2)}) collective-permute-start(f32[384,128]{1,0:T(8,128)S(1)} %get-tuple-element.52), channel_id=1, source_target_pairs={{0,1},{1,0},{2,3},{3,2},{4,5},{5,4},{6,7},{7,6},{8,9},{9,8},{10,11... | collective-permute-start | bytes 589832 | tf_op jit(solution)/shard_map/ppermute | solution.py:202
  79.0 13.7 %collective-permute-start.5 = (f32[8,72,128]{2,1,0:T(8,128)S(1)}, f32[8,72,128]{2,1,0:T(8,128)}, u32[]{:S(2)}, u32[]{:S(2)}) collective-permute-start(f32[8,72,128]{2,1,0:T(8,128)S(1)} %shard_map.187.basis_half_ref), channel_id=1, source_target_pairs={{0,2},{1,3},{2,0},{3,1},{4,6},{5,7},{6,4},{7,5},{8,10},{9,11},{10,... | collective-permute-start | bytes 884744 | tf_op jit(solution)/shard_map/ppermute | solution.py:205
  83.2 1.0 copy-start.3
  84.3 0.9 copy-start.5
  92.8 13.4 %all-to-all-start.3 = ((f32[8,72,128]{2,1,0:T(8,128)}), f32[8,72,128]{2,1,0:T(8,128)S(1)}, u32[]{:S(2)}, u32[]{:S(2)}) async-start(f32[8,72,128]{2,1,0:T(8,128)} %shard_map.184), calls=%async_computation.3 | async-start | bytes 589824 | tf_op jit(solution)/shard_map/all_to_all | solution.py:208
  96.4 1.3 copy-start.4
  97.7 1.1 copy-start.6
  102.7 1.1 copy-start
  106.1 36.1 %all-to-all-start.4 = ((f32[8,336,128]{2,1,0:T(8,128)}), f32[8,336,128]{2,1,0:T(8,128)S(1)}, u32[]{:S(2)}, u32[]{:S(2)}) async-start(f32[8,336,128]{2,1,0:T(8,128)} %copy-done), calls=%async_computation.4 | async-start | bytes 2752512 | tf_op jit(solution)/shard_map/all_to_all | solution.py:208
  111.8 20.4 %copy-start.12 = (f32[360]{0:T(512)S(1)}, f32[360]{0:T(512)}, u32[]{:S(2)}) copy-start(f32[360]{0:T(512)} %param.20) | copy-start | bytes 4324
  111.8 20.4 %copy-start.13 = (f32[360]{0:T(512)S(1)}, f32[360]{0:T(512)}, u32[]{:S(2)}) copy-start(f32[360]{0:T(512)} %param.19) | copy-start | bytes 4324
  111.8 20.4 %copy-start.14 = (f32[360]{0:T(512)S(1)}, f32[360]{0:T(512)}, u32[]{:S(2)}) copy-start(f32[360]{0:T(512)} %param.21) | copy-start | bytes 4324
  111.8 20.4 %copy-start.15 = (f32[360]{0:T(512)S(1)}, f32[360]{0:T(512)}, u32[]{:S(2)}) copy-start(f32[360]{0:T(512)} %param.22) | copy-start | bytes 4324
  111.8 1.5 %collective-permute-start.6 = (f32[384,128]{1,0:T(8,128)S(1)}, f32[384,128]{1,0:T(8,128)S(1)}, u32[]{:S(2)}, u32[]{:S(2)}) collective-permute-start(f32[384,128]{1,0:T(8,128)S(1)} %get-tuple-element.62), channel_id=1, source_target_pairs={{0,1},{1,0},{2,3},{3,2},{4,5},{5,4},{6,7},{7,6},{8,9},{9,8},{10,11... | collective-permute-start | bytes 589832 | tf_op jit(solution)/shard_map/ppermute | solution.py:202
  113.5 9.1 %collective-permute-start.7 = (f32[8,72,128]{2,1,0:T(8,128)S(1)}, f32[8,72,128]{2,1,0:T(8,128)S(1)}, u32[]{:S(2)}, u32[]{:S(2)}) collective-permute-start(f32[8,72,128]{2,1,0:T(8,128)S(1)} %shard_map.190.gram_half_ref), channel_id=1, source_target_pairs={{0,2},{1,3},{2,0},{3,1},{4,6},{5,7},{6,4},{7,5},{8,10},{9,11},{10,... | collective-permute-start | bytes 884744 | tf_op jit(solution)/shard_map/ppermute | solution.py:205
  132.2 1.4 collective-permute-start.8

commit v2 on v0

--- a/solution.py
+++ b/solution.py
@@ -143,13 +143,14 @@
         out_specs=out_specs or [vmem] * len(shapes),
         scratch_shapes=list(scratch),
         input_output_aliases=aliases or {},
-        compiler_params=pltpu.CompilerParams(vmem_limit_bytes=40 * 2**20),
+        compiler_params=pltpu.CompilerParams(vmem_limit_bytes=32 * 2**20),
     )(*args)
     return result[0] if single else result
 
 
 SMEM = pl.BlockSpec(memory_space=pltpu.SMEM)
 ANY = pl.BlockSpec(memory_space=pl.ANY)
+HBM = pl.BlockSpec(memory_space=pltpu.HBM)
 
 
 def body(
@@ -255,7 +256,7 @@
                 held.append(jnp.where(matrix >= 0, block, 0.0))
             store_block(out_ref, group, base, jnp.concatenate(held, axis=1), rows, owned)
 
-    table_scratch = [pltpu.SMEM((shards * MCAP,), jnp.int32), pltpu.SMEM((shards,), jnp.int32)]
+    count_scratch = pltpu.SMEM((shards,), jnp.int32)
     stage_scratch = pltpu.VMEM((matrix_total, rows, columns), F32)
 
     def slot_masks(edges_ref):
@@ -263,8 +264,9 @@
         return [(lane >= edges_ref[k]) & (lane < edges_ref[k + 1]) for k in range(slots)]
 
 
-    def pack_gradient(grad_ref, basis_ref, out_ref, line_ref):
-        send_tiles(grad_ref, line_ref, out_ref, strip_rows)
+    def pack_gradient(grad_ref, basis_ref, out_ref, line_ref, dense_ref, sem):
+        fetch = pltpu.make_async_copy(grad_ref, dense_ref, sem)
+        fetch.start()
         for group in range(shards):
             held = [
                 basis_ref[:, matrix * columns : (matrix + 1) * columns]
@@ -272,33 +274,75 @@
             ]
             held += [jnp.zeros((rows, columns), F32)] * (slots - len(held))
             store_block(out_ref, group, 0, jnp.concatenate(held, axis=1), rows, strip)
+        fetch.wait()
+        send_tiles(dense_ref, line_ref, out_ref, strip_rows)
 
     grad_dense = gradient.reshape(dense)
     basis_line = left_basis.reshape(rows, matrix_total * columns)
     send_one = call(
         pack_gradient,
         (shards, strip_rows + tile_rows, LANES),
-        (grad_dense, basis_line),
-        scratch=[line_scratch],
+        (pltpu.with_memory_space_constraint(grad_dense, pltpu.HBM), basis_line),
+        specs=[HBM, None],
+        scratch=[line_scratch, pltpu.VMEM(dense, F32), pltpu.SemaphoreType.DMA(())],
     )
     came_one = exchange(send_one)
 
 
-    def pack_second(
-        owner_ref, second_ref, basis_ref, out_ref, table_ref, count_ref, stage_ref, line_ref
+    half_groups = shards // 2
+    half_total = matrix_total // 2
+    assert half_groups * 2 == shards and shards & (shards - 1) == 0
+    assert all(
+        (matrix >= half_total) == (group >= half_groups)
+        for group in range(shards)
+        for matrix in slot_matrix[group]
+    )
+    group_arg = my_group.astype(jnp.int32).reshape(1)
+    slot_table = np.full((shards, slots), -1, np.int32)
+    for group in range(shards):
+        slot_table[group, : len(slot_matrix[group])] = slot_matrix[group]
+    slot_table = jnp.asarray(slot_table.reshape(-1))
+
+
+    def pack_moments(
+        owner_ref,
+        second_ref,
+        first_ref,
+        grad_ref,
+        basis_ref,
+        out_ref,
+        new_ref,
+        table_ref,
+        count_ref,
+        stage_ref,
+        line_ref,
     ):
         fill_owned_table(owner_ref, table_ref, count_ref)
         for matrix in range(matrix_total):
             stage_ref[matrix] = basis_ref[:, matrix * columns : (matrix + 1) * columns]
+        send_owned(stage_ref, table_ref, out_ref, 0)
         send_tiles(second_ref, line_ref, out_ref, owned_rows)
-        send_owned(stage_ref, table_ref, out_ref, 0)
-
-    send_two = call(
-        pack_second,
-        (shards, owned_rows + tile_rows, LANES),
-        (owners, second_moment.reshape(dense), basis_line),
-        specs=[SMEM, None, None],
-        scratch=table_scratch + [stage_scratch, line_scratch],
+        send_tiles(first_ref, line_ref, out_ref, owned_rows + tile_rows)
+        new_ref[...] = 0.9 * first_ref[...] + 0.1 * grad_ref[...]
+
+    vmem = pl.BlockSpec(memory_space=pltpu.VMEM)
+    send_two, first_out, owned_table = call(
+        pack_moments,
+        [
+            (shards, owned_rows + 2 * tile_rows, LANES),
+            dense,
+            jax.ShapeDtypeStruct((shards * MCAP,), jnp.int32),
+        ],
+        (
+            owners,
+            second_moment.reshape(dense),
+            first_moment.reshape(dense),
+            grad_dense,
+            basis_line,
+        ),
+        specs=[SMEM, None, None, None, None],
+        out_specs=[vmem, vmem, SMEM],
+        scratch=[count_scratch, stage_scratch, line_scratch],
     )
     came_one, send_two = together((came_one, send_two))
     came_two = exchange(send_two)
@@ -345,45 +389,123 @@
     for_core = lax.dynamic_index_in_dim(parts, 1 - my_core, 1, False)
     kept = lax.dynamic_index_in_dim(parts, my_core, 1, False) + over_core(for_core)
     for_chip = lax.dynamic_index_in_dim(kept, 1 - my_chip, 0, False)
-    gram_strips = lax.dynamic_index_in_dim(kept, my_chip, 0, False) + over_chip(for_chip)
-
+    came_chip = over_chip(for_chip)
+
+
+    def sum_strips(group_ref, chip_ref, kept_ref, came_ref, *out_refs):
+        place = group_ref[0] % half_groups
+        for k, out_ref in enumerate(out_refs):
+            for j in range(2):
+                at = (place ^ k) + j * half_groups
+                out_ref[j] = kept_ref[chip_ref[0], at] + came_ref[at]
+
+    gram_blocks = call(
+        sum_strips,
+        [(2, strip_rows, LANES)] * half_groups,
+        (group_arg, my_chip.astype(jnp.int32).reshape(1), kept, came_chip),
+        specs=[SMEM, SMEM, None, None],
+    )
+    gram_blocks = [gram_blocks[0]] + [
+        lax.ppermute(gram_blocks[k], "shard", [(s, s ^ k) for s in range(shards)])
+        for k in range(1, half_groups)
+    ]
+
+
+    *gram_blocks, strips_own = together((*gram_blocks, strips_own))
     strips_chip = over_chip(strips_own)
+
+
+    def split_owned(rank_ref, came_ref, *refs):
+        spread = len(refs) == 4
+        mine_ref, other_ref = refs[-3:-1] if spread else refs
+        odd = rank_ref[0] % 2 == 1
+        for block_at in range(shards):
+            at = slice(block_at * rows, (block_at + 1) * rows)
+            if spread:
+                place, base = block_at % half_groups, block_at // half_groups * owned_rows
+                block = load_block(came_ref, place, base, rows, owned) + load_block(
+                    came_ref, half_groups + place, base, rows, owned
+                )
+            else:
+                block = load_block(came_ref, block_at, 0, rows, owned)
+            strips = [block[:, m * columns : (m + 1) * columns] for m in range(MCAP)]
+            mine_ref[at, 0:columns] = jnp.where(odd, strips[1], strips[0])
+            other_ref[at, 0:columns] = jnp.where(odd, strips[0], strips[1])
+            if spread:
+                for m in range(MCAP):
+                    refs[-1][m, at, 0:columns] = strips[m]
+        if spread:
+            for m in range(MCAP):
+                refs[0][m] = refs[-1][m].T[0:columns]
+
+    def join_half(rank_ref, mine_ref, other_ref, half_ref):
+        odd = rank_ref[0] % 2 == 1
+        for group in range(shards):
+            at = slice(group * rows, (group + 1) * rows)
+            mine, other = mine_ref[at, 0:columns], other_ref[at, 0:columns]
+            both = [jnp.where(odd, other, mine), jnp.where(odd, mine, other)]
+            store_block(half_ref, group, 0, jnp.concatenate(both, axis=1), rows, owned)
+
+    def collect(came, spread):
+        *strips, mine, other = call(
+            split_owned,
+            [(MCAP, columns, width)] * spread + [(width, LANES), (width, LANES)],
+            (rank_arg, came),
+            specs=[SMEM, None],
+            scratch=[pltpu.VMEM((MCAP, width, LANES), F32)] * spread,
+        )
+        half = call(
+            join_half,
+            (shards, owned_rows, LANES),
+            (rank_arg, mine, over_core(other)),
+            specs=[SMEM, None, None],
+        )
+        return *strips, half, over_chip(half)
+
+
+    def new_grams(group_ref, table_ref, slot_ref, gram_ref, *refs):
+        came, (out_ref, stage_ref) = refs[:half_groups], refs[half_groups:]
+        group = group_ref[0]
+        half = group // half_groups
+        for matrix in range(matrix_total):
+            old = 0.95 * gram_ref[:, matrix * columns : (matrix + 1) * columns]
+            stage_ref[0, matrix] = jnp.where(half == 0, old, 0.0)
+            stage_ref[1, matrix] = jnp.where(half == 0, 0.0, old)
+        for k, came_ref in enumerate(came):
+            for j in range(2):
+                block = load_block(came_ref, j, 0, rows, strip)
+                for m in range(slots):
+                    matrix = slot_ref[(group ^ k) * slots + m]
+                    at = jnp.where(matrix >= 0, matrix, matrix_total)
+                    part = block[:, m * columns : (m + 1) * columns]
+                    stage_ref[j, at] = stage_ref[j, at] + 0.05 * part
+        for dest in range(shards):
+            for j in range(2):
+                held = []
+                for m in range(MCAP):
+                    matrix = table_ref[dest * MCAP + m]
+                    block = stage_ref[j, jnp.maximum(matrix, 0)]
+                    held.append(jnp.where(matrix >= 0, block, 0.0))
+                block = jnp.concatenate(held, axis=1)
+                store_block(out_ref, dest, j * owned_rows, block, rows, owned)
+
+    send_four = call(
+        new_grams,
+        (shards, 2 * owned_rows, LANES),
+        (
+            group_arg,
+            owned_table,
+            slot_table,
+            left_gram.reshape(rows, matrix_total * columns),
+            *gram_blocks,
+        ),
+        specs=[SMEM, SMEM, SMEM] + [None] * (1 + half_groups),
+        scratch=[pltpu.VMEM((2, matrix_total + 1, rows, columns), F32)],
+    )
+    came_two, send_four, strips_chip = together((came_two, send_four, strips_chip))
+    came_four = exchange(send_four)
     pair = over_core(jnp.stack([strips_own, strips_chip]))
 
-
-    def pack_first(first_ref, grad_ref, out_ref, new_ref, line_ref):
-        send_tiles(first_ref, line_ref, out_ref, strip_rows)
-        new_ref[...] = 0.9 * first_ref[...] + 0.1 * grad_ref[...]
-
-    send_three, first_out = call(
-        pack_first,
-        [(shards, strip_rows + tile_rows, LANES), dense],
-        (first_moment.reshape(dense), grad_dense),
-        scratch=[line_scratch],
-    )
-
-    def add_strips(base_ref, strips_ref, out_ref):
-        del base_ref
-        out_ref[...] = strips_ref[...]
-
-    def fill_head(kernel, base, head_rows, args, specs, scratch=()):
-        return call(
-            kernel,
-            base.shape,
-            (base,) + args,
-            specs=[ANY] + specs,
-            out_specs=[pl.BlockSpec((shards, head_rows, LANES), lambda i: (0, 0, 0))],
-            grid=(1,),
-            scratch=scratch,
-            aliases={0: 0},
-        )
-
-    send_three = fill_head(add_strips, send_three, strip_rows, (gram_strips,), [None])
-    came_two, send_three = together((came_two, send_three))
-    came_three = exchange(send_three)
-
-
-    half_shape = jax.ShapeDtypeStruct((slots, width, width), BF16)
 
     def rotate_gradient(
         rank_ref,
@@ -392,13 +514,8 @@
         chip_ref,
         pair_ref,
         grad_ref,
-        came_ref,
-        high_ref,
-        low_ref,
-        high_turned_ref,
-        low_turned_ref,
-        second_ref,
         basis_ref,
+        hat_ref,
     ):
         rank = rank_ref[0]
         for group in range(shards):
@@ -419,72 +536,44 @@
                     jnp.where(first, odd[1], odd[0]),
                 ]
                 basis_ref[k, at, :] = jnp.concatenate(ordered, axis=1)
-        unpack_columns(came_ref, owned_rows, second_ref, shards, rows, share)
         grad = parts_of(grad_ref[...])
         hat = jnp.zeros((width, wide), F32)
         for k, mask in enumerate(slot_masks(edges_ref)):
-            basis = basis_ref[k]
-            high_ref[k], low_ref[k] = parts_of(basis)
-            turned = parts_of(basis.T)
-            high_turned_ref[k], low_turned_ref[k] = turned
-            hat = jnp.where(mask, product(turned, grad), hat)
-        second_ref[...] = 0.95 * second_ref[...] + 0.05 * hat * hat
-
-    high, low, high_turned, low_turned, second_full = call(
+            hat = jnp.where(mask, product(parts_of(basis_ref[k].T), grad), hat)
+        hat_ref[...] = hat
+
+    basis_full, hat_full = call(
         rotate_gradient,
-        [half_shape] * 4 + [(width, wide)],
-        (rank_arg, my_edges, strips_own, strips_chip, pair, grad_full, came_two),
-        specs=[SMEM, SMEM] + [None] * 5,
-        scratch=[pltpu.VMEM((slots, width, width), F32)],
-    )
-
-
-    def new_grams(owner_ref, came_ref, gram_ref, out_ref, table_ref, count_ref, stage_ref):
-        fill_owned_table(owner_ref, table_ref, count_ref)
-        total = [None] * matrix_total
-        for group in range(shards):
-            block = load_block(came_ref, group, 0, rows, strip)
-            for k, matrix in enumerate(slot_matrix[group]):
-                part = block[:, k * columns : (k + 1) * columns]
-                total[matrix] = part if total[matrix] is None else total[matrix] + part
-        for matrix in range(matrix_total):
-            gram = gram_ref[:, matrix * columns : (matrix + 1) * columns]
-            stage_ref[matrix] = 0.95 * gram + 0.05 * total[matrix]
-        send_owned(stage_ref, table_ref, out_ref, 0)
-
-    send_four = call(
-        new_grams,
-        (shards, owned_rows, LANES),
-        (owners, came_three, left_gram.reshape(rows, matrix_total * columns)),
-        specs=[SMEM, None, None],
-        scratch=table_scratch + [stage_scratch],
-    )
-    came_three, send_four = together((came_three, send_four))
-    came_four = exchange(send_four)
+        [(slots, width, width), (width, wide)],
+        (rank_arg, my_edges, strips_own, strips_chip, pair, grad_full),
+        specs=[SMEM, SMEM] + [None] * 4,
+    )
+
+    basis_half, basis_far = collect(came_two, 0)
 
 
     def directions(
         edges_ref,
         came_ref,
         grad_ref,
-        second_ref,
-        high_ref,
-        low_ref,
-        high_turned_ref,
-        low_turned_ref,
+        hat_ref,
+        basis_ref,
         send_ref,
         moment_ref,
+        second_ref,
     ):
-        unpack_columns(came_ref, strip_rows, moment_ref, shards, rows, share)
+        unpack_columns(came_ref, owned_rows, second_ref, shards, rows, share)
+        second_ref[...] = 0.95 * second_ref[...] + 0.05 * hat_ref[...] * hat_ref[...]
+        unpack_columns(came_ref, owned_rows + tile_rows, moment_ref, shards, rows, share)
         masks = slot_masks(edges_ref)
         moment = parts_of(0.9 * moment_ref[...] + 0.1 * grad_ref[...])
         hat = jnp.zeros((width, wide), F32)
         for k, mask in enumerate(masks):
-            hat = jnp.where(mask, product((high_turned_ref[k], low_turned_ref[k]), moment), hat)
+            hat = jnp.where(mask, product(parts_of(basis_ref[k].T), moment), hat)
         step = parts_of(adam_direction(hat, second_ref[...]))
         turned = jnp.zeros((width, wide), F32)
         for k, mask in enumerate(masks):
-            turned = jnp.where(mask, product((high_ref[k], low_ref[k]), step), turned)
+            turned = jnp.where(mask, product(parts_of(basis_ref[k]), step), turned)
         moment_ref[...] = turned
         pack_columns(moment_ref, send_ref, 0, shards, rows, share)
         pack_columns(second_ref, send_ref, tile_rows, shards, rows, share)
@@ -492,53 +581,15 @@
     send_five = call(
         directions,
         (shards, 2 * tile_rows, LANES),
-        (my_edges, came_three, grad_full, second_full, high, low, high_turned, low_turned),
-        specs=[SMEM] + [None] * 7,
-        scratch=[pltpu.VMEM((width, wide), F32)],
+        (my_edges, came_two, grad_full, hat_full, basis_full),
+        specs=[SMEM] + [None] * 4,
+        scratch=[pltpu.VMEM((width, wide), F32)] * 2,
     )
     came_four, send_five = together((came_four, send_five))
     came_five = exchange(send_five)
 
 
-    def split_owned(rank_ref, came_ref, strips_ref, mine_ref, other_ref, whole_ref):
-        odd = rank_ref[0] % 2 == 1
-        for source in range(shards):
-            at = slice(source * rows, (source + 1) * rows)
-            block = load_block(came_ref, source, 0, rows, owned)
-            zero, one = block[:, 0:columns], block[:, columns:owned]
-            whole_ref[0, at, 0:columns] = zero
-            whole_ref[1, at, 0:columns] = one
-            mine_ref[at, 0:columns] = jnp.where(odd, one, zero)
-            other_ref[at, 0:columns] = jnp.where(odd, zero, one)
-        for m in range(MCAP):
-            strips_ref[m] = whole_ref[m].T[0:columns]
-
-    def join_half(rank_ref, mine_ref, other_ref, half_ref):
-        odd = rank_ref[0] % 2 == 1
-        for group in range(shards):
-            at = slice(group * rows, (group + 1) * rows)
-            mine, other = mine_ref[at, 0:columns], other_ref[at, 0:columns]
-            both = [jnp.where(odd, other, mine), jnp.where(odd, mine, other)]
-            store_block(half_ref, group, 0, jnp.concatenate(both, axis=1), rows, owned)
-
-    def collect(came):
-        strips, mine, other = call(
-            split_owned,
-            [(MCAP, columns, width), (width, LANES), (width, LANES)],
-            (rank_arg, came),
-            specs=[SMEM, None],
-            scratch=[pltpu.VMEM((MCAP, width, LANES), F32)],
-        )
-        half = call(
-            join_half,
-            (shards, owned_rows, LANES),
-            (rank_arg, mine, over_core(other)),
-            specs=[SMEM, None, None],
-        )
-        return strips, half, over_chip(half)
-
-    _, basis_half, basis_far = collect(came_two)
-    gram_out, gram_half, gram_far = collect(came_four)
+    gram_out, gram_half, gram_far = collect(came_four, 1)
 
     def refresh(
         rank_ref,
@@ -546,11 +597,16 @@
         basis_far_ref,
         gram_half_ref,
         gram_far_ref,
+        weight_ref,
         mine_ref,
         other_ref,
+        weight_out_ref,
         basis_ref,
         gram_ref,
+        sem,
     ):
+        fetch = pltpu.make_async_copy(weight_ref, weight_out_ref, sem)
+        fetch.start()
         rank = rank_ref[0]
         first = rank < 2
         for out, half_ref, far_ref in (
@@ -574,13 +630,15 @@
         even_core = rank % 2 == 0
         mine_ref[...] = jnp.where(even_core, low, odd)
         other_ref[...] = jnp.where(even_core, odd, low)
-
-    frame_mine, frame_other = call(
+        fetch.wait()
+
+    weight_dense = pltpu.with_memory_space_constraint(weight.reshape(dense), pltpu.HBM)
+    frame_mine, frame_other, weight_near = call(
         refresh,
-        [(columns, width), (columns, width)],
-        (rank_arg, basis_half, basis_far, gram_half, gram_far),
-        specs=[SMEM] + [None] * 4,
-        scratch=[pltpu.VMEM((width, width), F32)] * 2,
+        [(columns, width), (columns, width), dense],
+        (rank_arg, basis_half, basis_far, gram_half, gram_far, weight_dense),
+        specs=[SMEM] + [None] * 4 + [HBM],
+        scratch=[pltpu.VMEM((width, width), F32)] * 2 + [pltpu.SemaphoreType.DMA(())],
     )
     frame_came = over_core(frame_other)
     pair_out = jnp.where(
@@ -608,7 +666,7 @@
         close_line(line_ref, second_out_ref)
 
     weight_out, second_out = call(
-        take_back, [dense, dense], (came_five, weight.reshape(dense)), scratch=[line_scratch]
+        take_back, [dense, dense], (came_five, weight_near), scratch=[line_scratch]
     )
 
     bias_first_new = 0.9 * bias_first + 0.1 * bias_gradient

time: 149 us -> 139 us (0.933)
  waiting for transfers between devices: 71.1 us -> 60.3 us
  local copies, waits for them, and re-layouts: 8.4 us -> 12.7 us
  Pallas kernels: 33.8 us -> 30.7 us
    all_to_all x5 -> x4, waiting for transfers between devices: 43.4 us -> 21.8 us  [exchange(): lax.all_to_all(value, 'shard', split_axis=0, concat_axis=0, tiled=True)]
    ppermute x0 -> x3, waiting for transfers between devices: none -> 10.4 us  [body(): lax.ppermute(gram_blocks[k], 'shard', [(s, s ^ k) for s in range(shards)])]
    unnamed x32 -> x46, local copies, waits for them, and re-layouts: 6.84 us -> 11.8 us
    ppermute x0 -> x3, starting transfers between devices: none -> 3.57 us  [body(): lax.ppermute(gram_blocks[k], 'shard', [(s, s ^ k) for s in range(shards)])]
    pallas_call x14 -> x13, Pallas kernels: 33.8 us -> 30.7 us  [call(): pl.pallas_call(kernel, out_shape=shapes, grid=grid, in_specs=[s or vmem f...]
    all_to_all x5 -> x4, starting transfers between devices: 23.4 us -> 20.5 us  [exchange(): lax.all_to_all(value, 'shard', split_axis=0, concat_axis=0, tiled=True)]
    ppermute x5, waiting for transfers between devices: 2.8 us -> 4.78 us  [over_core(): return lax.ppermute(value, 'tensor', core_pairs)]
    ppermute x4, waiting for transfers between devices: 25 us -> 23.3 us  [over_chip(): return lax.ppermute(value, 'tensor', chip_pairs)]
  transfers between devices with their start and end apart: 14 -> 16, of which waited for: 11 -> 13; matrix products, arithmetic and copies ran while one was open for 5% -> 3% of each run, Pallas kernels for 20% -> 19%
where the time goes in v2:
time: 139 us
  waiting for transfers between devices  60.3 us (43%)
  Pallas kernels  30.7 us (22%)
  starting transfers between devices  30.2 us (22%)
  local copies, waits for them, and re-layouts  12.7 us (9%)
  other arithmetic  3.64 us (3%)
    pallas_call x13, Pallas kernels, call(): pl.pallas_call(kernel, out_shape=shapes, grid=grid, in_specs=[s or vmem f...  30.7 us
    ppermute x4, waiting for transfers between devices, over_chip(): return lax.ppermute(value, 'tensor', chip_pairs)  23.3 us
    all_to_all x4, waiting for transfers between devices, exchange(): lax.all_to_all(value, 'shard', split_axis=0, concat_axis=0, tiled=True)  21.8 us
    all_to_all x4, starting transfers between devices, exchange(): lax.all_to_all(value, 'shard', split_axis=0, concat_axis=0, tiled=True)  20.5 us
    unnamed x46, local copies, waits for them, and re-layouts  11.8 us
    ppermute x3, waiting for transfers between devices, body(): lax.ppermute(gram_blocks[k], 'shard', [(s, s ^ k) for s in range(shards)])  10.4 us
    ppermute x4, starting transfers between devices, over_chip(): return lax.ppermute(value, 'tensor', chip_pairs)  5.6 us
    ppermute x5, waiting for transfers between devices, over_core(): return lax.ppermute(value, 'tensor', core_pairs)  4.78 us
  transfers between devices with their start and end apart: 16, of which 13 were waited for; matrix products, arithmetic and copies ran while one was open for 3% of the time, Pallas kernels for 19%

profile of v2, /device:TPU:0, one launch (start us, length us, event | category | flops | bytes accessed | tf_op | source)
XLA Modules:
  0.0 138.5 jit_solution(6297824339295483450)
XLA Ops:
  0.6 1.0 copy.33
  1.6 2.6 %shard_map.188 = f32[8,240,128]{2,1,0:T(8,128)} custom-call(f32[1296,128]{1,0:T(8,128)} %bitcast.39, f32[48,960]{1,0:T(8,128)S(1)} %bitcast.41), custom_call_target="tpu_custom_call" | custom-call | tf_op jit(solution)/shard_map/pallas_call | solution.py:138
  4.3 7.4 %all-to-all-start = ((f32[8,240,128]{2,1,0:T(8,128)}), f32[8,240,128]{2,1,0:T(8,128)S(1)}, u32[]{:S(2)}, u32[]{:S(2)}) async-start(f32[8,240,128]{2,1,0:T(8,128)} %shard_map.188), calls=%async_computation | async-start | bytes 1966080 | tf_op jit(solution)/shard_map/all_to_all | solution.py:208
  11.8 0.9 copy-done.6
  12.7 1.1 copy-done.13
  13.8 1.1 copy-done.14
  14.9 3.4 %shard_map.189 = (f32[8,408,128]{2,1,0:T(8,128)S(1)}, f32[1296,128]{1,0:T(8,128)}, s32[16]{0:T(128)S(1)}) custom-call(s32[10]{0:T(128)S(1)} %reshape.60.owner_ref, f32[1296,128]{1,0:T(8,128)S(1)} %bitcast.47, f32[1296,128]{1,0:T(8,128)S(1)} %bitcast.48, f32[1296,128]{1,0:T(8,128)S(1)} %bitcast.40, f32[48,960]{1,0:T(8,128)S(1)} %bitcast.42), custom_call_target="tpu_custom_call" | custom-call | tf_op jit(solution)/shard_map/pallas_call | solution.py:138
  18.3 1.2 copy-done.7
  19.5 16.6 %all-to-all-done.came_ref = f32[8,240,128]{2,1,0:T(8,128)S(1)} async-done(((f32[8,240,128]{2,1,0:T(8,128)}), f32[8,240,128]{2,1,0:T(8,128)S(1)}, u32[]{:S(2)}, u32[]{:S(2)}) %all-to-all-start) | async-done | bytes 983072 | tf_op jit(solution)/shard_map/all_to_all | solution.py:208
  36.1 3.6 %all-to-all-start.1 = ((f32[8,408,128]{2,1,0:T(8,128)}), f32[8,408,128]{2,1,0:T(8,128)S(1)}, u32[]{:S(2)}, u32[]{:S(2)}) async-start(f32[8,408,128]{2,1,0:T(8,128)} %copy-done.7), calls=%async_computation.1 | async-start | bytes 3342336 | tf_op jit(solution)/shard_map/all_to_all | solution.py:208
  39.7 0.7 fusion.1.edges_ref
  40.4 2.3 %shard_map.190 = (f32[384,512]{1,0:T(8,128)S(1)}, f32[8,72,128]{2,1,0:T(8,128)S(1)}, f32[4,8,72,128]{3,2,1,0:T(8,128)S(1)}) custom-call(s32[3]{0:T(128)S(1)} %fusion.1.edges_ref, f32[8,240,128]{2,1,0:T(8,128)S(1)} %all-to-all-done.came_ref), custom_call_target="tpu_custom_call" | custom-call | tf_op jit(solution)/shard_map/pallas_call | solution.py:138
  42.8 0.7 copy-done.8
  43.5 1.0 copy-done.10
  44.7 2.1 %collective-permute-done = f32[2,8,72,128]{3,2,1,0:T(8,128)} collective-permute-done((f32[2,8,72,128]{3,2,1,0:T(8,128)S(1)}, f32[2,8,72,128]{3,2,1,0:T(8,128)}, u32[]{:S(2)}, u32[]{:S(2)}) %collective-permute-start) | collective-permute-done | bytes 589856 | tf_op jit(solution)/shard_map/ppermute | solution.py:202
  46.7 1.3 bitcast_add_fusion.kept_ref
  48.1 1.6 %collective-permute-start.1 = (f32[8,72,128]{2,1,0:T(8,128)S(1)}, f32[8,72,128]{2,1,0:T(8,128)S(1)}, u32[]{:S(2)}, u32[]{:S(2)}) collective-permute-start(f32[8,72,128]{2,1,0:T(8,128)S(1)} %dynamic-slice_bitcast_fusion.1), channel_id=1, source_target_pairs={{0,2},{1,3},{2,0},{3,1},{4,6},{5,7},{6,4},{7,5},{8,10},{9,11},{10,... | collective-permute-start | bytes 884744 | tf_op jit(solution)/shard_map/ppermute | solution.py:205
  49.6 7.6 %collective-permute-done.1.came_ref = f32[8,72,128]{2,1,0:T(8,128)S(1)} collective-permute-done((f32[8,72,128]{2,1,0:T(8,128)S(1)}, f32[8,72,128]{2,1,0:T(8,128)S(1)}, u32[]{:S(2)}, u32[]{:S(2)}) %collective-permute-start.1) | collective-permute-done | bytes 294944 | tf_op jit(solution)/shard_map/ppermute | solution.py:205
  57.2 2.0 %collective-permute-start.2 = (f32[2,72,128]{2,1,0:T(8,128)S(1)}, f32[2,72,128]{2,1,0:T(8,128)S(1)}, u32[]{:S(2)}, u32[]{:S(2)}) collective-permute-start(f32[2,72,128]{2,1,0:T(8,128)S(1)} %get-tuple-element.52), channel_id=1, source_target_pairs={{0,4},{4,0},{8,12},{12,8},{16,20},{20,16},{24,28},{28,24},{1,5},{5... | collective-permute-start | bytes 221192 | tf_op jit(solution)/shard_map/ppermute | solution.py:409
  59.3 1.5 %collective-permute-start.3 = (f32[2,72,128]{2,1,0:T(8,128)S(1)}, f32[2,72,128]{2,1,0:T(8,128)S(1)}, u32[]{:S(2)}, u32[]{:S(2)}) collective-permute-start(f32[2,72,128]{2,1,0:T(8,128)S(1)} %get-tuple-element.53), channel_id=1, source_target_pairs={{0,8},{4,12},{8,0},{12,4},{16,24},{20,28},{24,16},{28,20},{1,9},{5... | collective-permute-start | bytes 221192 | tf_op jit(solution)/shard_map/ppermute | solution.py:409
  60.8 2.8 %collective-permute-done.2.refs_1_ = f32[2,72,128]{2,1,0:T(8,128)S(1)} collective-permute-done((f32[2,72,128]{2,1,0:T(8,128)S(1)}, f32[2,72,128]{2,1,0:T(8,128)S(1)}, u32[]{:S(2)}, u32[]{:S(2)}) %collective-permute-start.2) | collective-permute-done | bytes 73760 | tf_op jit(solution)/shard_map/ppermute | solution.py:409
  63.6 6.8 %collective-permute-done.3.refs_2_ = f32[2,72,128]{2,1,0:T(8,128)S(1)} collective-permute-done((f32[2,72,128]{2,1,0:T(8,128)S(1)}, f32[2,72,128]{2,1,0:T(8,128)S(1)}, u32[]{:S(2)}, u32[]{:S(2)}) %collective-permute-start.3) | collective-permute-done | bytes 73760 | tf_op jit(solution)/shard_map/ppermute | solution.py:409
  70.4 0.8 collective-permute-done.4.refs_3_
  71.2 1.5 %collective-permute-start.5 = (f32[8,72,128]{2,1,0:T(8,128)S(1)}, f32[8,72,128]{2,1,0:T(8,128)}, u32[]{:S(2)}, u32[]{:S(2)}) collective-permute-start(f32[8,72,128]{2,1,0:T(8,128)S(1)} %copy-done.9), channel_id=1, source_target_pairs={{0,2},{1,3},{2,0},{3,1},{4,6},{5,7},{6,4},{7,5},{8,10},{9,11},{10,... | collective-permute-start | bytes 884744 | tf_op jit(solution)/shard_map/ppermute | solution.py:205
  72.7 2.2 %shard_map.192 = f32[8,144,128]{2,1,0:T(8,128)S(1)} custom-call(s32[1]{0:T(128)} %bitcast.3.group_ref, s32[16]{0:T(128)S(1)} %get-tuple-element.48.table_ref, s32[16]{0:T(128)S(1)} %copy-done.15, f32[48,960]{1,0:T(8,128)S(1)} %bitcast.46, f32[2,72,128]{2,1,0:T(8,128)S(1)} %get-tuple-element.56.refs_0_, f32[2,72,128]{2,1,0:T(8,128)S(1)} %collective-permute-done.2.refs_1_, ...), custom_call_target="tpu_custom_call" | custom-call | tf_op jit(solution)/shard_map/pallas_call | solution.py:138
  74.9 0.8 copy-done.4
  75.7 3.6 %collective-permute-done.5.chip_ref = f32[8,72,128]{2,1,0:T(8,128)} collective-permute-done((f32[8,72,128]{2,1,0:T(8,128)S(1)}, f32[8,72,128]{2,1,0:T(8,128)}, u32[]{:S(2)}, u32[]{:S(2)}) %collective-permute-start.5) | collective-permute-done | bytes 294944 | tf_op jit(solution)/shard_map/ppermute | solution.py:205
  79.4 5.7 %all-to-all-start.2 = ((f32[8,144,128]{2,1,0:T(8,128)}), f32[8,144,128]{2,1,0:T(8,128)S(1)}, u32[]{:S(2)}, u32[]{:S(2)}) async-start(f32[8,144,128]{2,1,0:T(8,128)} %copy-done.4), calls=%async_computation.2 | async-start | bytes 1179648 | tf_op jit(solution)/shard_map/all_to_all | solution.py:208
  85.1 1.0 pad_maximum_fusion
  86.2 2.0 %collective-permute-done.6.pair_ref = f32[2,8,72,128]{3,2,1,0:T(8,128)S(1)} collective-permute-done((f32[2,8,72,128]{3,2,1,0:T(8,128)S(1)}, f32[2,8,72,128]{3,2,1,0:T(8,128)S(1)}, u32[]{:S(2)}, u32[]{:S(2)}) %collective-permute-start.6) | collective-permute-done | bytes 589856 | tf_op jit(solution)/shard_map/ppermute | solution.py:202
  88.2 2.9 %shard_map.193 = (f32[2,384,384]{2,1,0:T(8,128)S(1)}, f32[384,512]{1,0:T(8,128)S(1)}) custom-call(s32[1]{0:T(128)} %bitcast.10.rank_ref, s32[3]{0:T(128)S(1)} %fusion.1.edges_ref, f32[8,72,128]{2,1,0:T(8,128)S(1)} %copy-done.9, f32[8,72,128]{2,1,0:T(8,128)} %collective-permute-done.5.chip_ref, f32[2,8,72,128]{3,2,1,0:T(8,128)S(1)} %collective-permute-done.6.pair_ref, ...), custom_call_target="tpu_custom_call" | custom-call | tf_op jit(solution)/shard_map/pallas_call | solution.py:138
  91.1 4.0 %shard_map.194 = f32[8,336,128]{2,1,0:T(8,128)S(1)} custom-call(s32[3]{0:T(128)S(1)} %fusion.1.edges_ref, f32[8,408,128]{2,1,0:T(8,128)S(1)} %all-to-all-done.1.came_ref, f32[384,512]{1,0:T(8,128)S(1)} %get-tuple-element.63.grad_ref, f32[384,512]{1,0:T(8,128)S(1)} %get-tuple-element.65.hat_ref, f32[2,384,384]{2,1,0:T(8,128)S(1)} %get-tuple-element.66.basis_ref), custom_call_target="tpu_custom_call" | custom-call | tf_op jit(solution)/shard_map/pallas_call | solution.py:138
  95.1 1.1 copy-done
  96.2 3.6 %all-to-all-done.2.came_ref = f32[8,144,128]{2,1,0:T(8,128)S(1)} async-done(((f32[8,144,128]{2,1,0:T(8,128)}), f32[8,144,128]{2,1,0:T(8,128)S(1)}, u32[]{:S(2)}, u32[]{:S(2)}) %all-to-all-start.2) | async-done | bytes 589856 | tf_op jit(solution)/shard_map/all_to_all | solution.py:208
  99.8 0.8 copy-done.2
  100.6 3.8 %all-to-all-start.3 = ((f32[8,336,128]{2,1,0:T(8,128)}), f32[8,336,128]{2,1,0:T(8,128)S(1)}, u32[]{:S(2)}, u32[]{:S(2)}) async-start(f32[8,336,128]{2,1,0:T(8,128)} %copy-done), calls=%async_computation.3 | async-start | bytes 2752512 | tf_op jit(solution)/shard_map/all_to_all | solution.py:208
  105.4 1.6 %shard_map.197 = (f32[2,96,384]{2,1,0:T(8,128)}, f32[384,128]{1,0:T(8,128)S(1)}, f32[384,128]{1,0:T(8,128)S(1)}) custom-call(s32[1]{0:T(128)} %bitcast.10.rank_ref, f32[8,144,128]{2,1,0:T(8,128)S(1)} %copy-done.3), custom_call_target="tpu_custom_call" | custom-call | tf_op jit(solution)/shard_map/pallas_call | solution.py:138
  107.5 1.6 %collective-permute-start.8 = (f32[8,72,128]{2,1,0:T(8,128)S(1)}, f32[8,72,128]{2,1,0:T(8,128)S(1)}, u32[]{:S(2)}, u32[]{:S(2)}) collective-permute-start(f32[8,72,128]{2,1,0:T(8,128)S(1)} %shard_map.196.basis_half_ref), channel_id=1, source_target_pairs={{0,2},{1,3},{2,0},{3,1},{4,6},{5,7},{6,4},{7,5},{8,10},{9,11},{10,... | collective-permute-start | bytes 884744 | tf_op jit(solution)/shard_map/ppermute | solution.py:205
  109.2 1.0 collective-permute-start.10
  110.2 0.7 copy-done.11
  110.9 6.5 %collective-permute-done.8.basis_far_ref = f32[8,72,128]{2,1,0:T(8,128)S(1)} collective-permute-done((f32[8,72,128]{2,1,0:T(8,128)S(1)}, f32[8,72,128]{2,1,0:T(8,128)S(1)}, u32[]{:S(2)}, u32[]{:S(2)}) %collective-permute-start.8) | collective-permute-done | bytes 294944 | tf_op jit(solution)/shard_map/ppermute | solution.py:205
  117.4 5.7 %collective-permute-done.10.gram_far_ref = f32[8,72,128]{2,1,0:T(8,128)S(1)} collective-permute-done((f32[8,72,128]{2,1,0:T(8,128)S(1)}, f32[8,72,128]{2,1,0:T(8,128)S(1)}, u32[]{:S(2)}, u32[]{:S(2)}) %collective-permute-start.10) | collective-permute-done | bytes 294944 | tf_op jit(solution)/shard_map/ppermute | solution.py:205
  123.1 1.0 copy-done.12
  124.0 8.6 %shard_map.199 = (f32[96,384]{1,0:T(8,128)S(1)}, f32[96,384]{1,0:T(8,128)S(1)}, f32[1296,128]{1,0:T(8,128)S(1)}) custom-call(s32[1]{0:T(128)} %bitcast.10.rank_ref, f32[8,72,128]{2,1,0:T(8,128)S(1)} %shard_map.196.basis_half_ref, f32[8,72,128]{2,1,0:T(8,128)S(1)} %collective-permute-done.8.basis_far_ref, f32[8,72,128]{2,1,0:T(8,128)S(1)} %copy-done.12, ...), custom_call_target="tpu_custom_call" | custom-call | tf_op jit(solution)/shard_map/pallas_call | solution.py:138
  133.3 0.7 collective-permute-done.11
  134.0 0.7 maximum_select_fusion
  134.8 1.7 %all-to-all-done.3.came_ref = f32[8,336,128]{2,1,0:T(8,128)S(1)} async-done(((f32[8,336,128]{2,1,0:T(8,128)}), f32[8,336,128]{2,1,0:T(8,128)S(1)}, u32[]{:S(2)}, u32[]{:S(2)}) %all-to-all-start.3) | async-done | bytes 1376288 | tf_op jit(solution)/shard_map/all_to_all | solution.py:208
  136.4 2.1 %shard_map.200 = (f32[1296,128]{1,0:T(8,128)}, f32[1296,128]{1,0:T(8,128)}) custom-call(f32[8,336,128]{2,1,0:T(8,128)S(1)} %all-to-all-done.3.came_ref, f32[1296,128]{1,0:T(8,128)S(1)} %get-tuple-element.78.weight_ref), custom_call_target="tpu_custom_call" | custom-call | tf_op jit(solution)/shard_map/pallas_call | solution.py:138
  (51 shorter events, 2.8 us)
Async XLA Ops:
  1.6 2.7 %copy-start.5 = (f32[48,1,960]{2,0,1:T(8,128)}, f32[48,1,960]{2,0,1:T(8,128)S(1)}, u32[]{:S(2)}) copy-start(f32[48,1,960]{2,0,1:T(8,128)S(1)} %copy.33) | copy-start | bytes 552964
  4.3 7.5 %copy-start.21 = (s32[2,5]{1,0:T(2,128)S(1)}, s32[2,5]{1,0:T(2,128)}, u32[]{:S(2)}) copy-start(s32[2,5]{1,0:T(2,128)} %param.19) | copy-start | bytes 124
  4.3 7.5 %copy-start.1 = (f32[48,1,3456]{2,1,0:T(1,128)S(1)}, f32[48,1,3456]{2,1,0:T(1,128)}, u32[]{:S(2)}) copy-start(f32[48,1,3456]{2,1,0:T(1,128)} %param.13) | copy-start | bytes 1990660
  4.3 31.8 %all-to-all-start = ((f32[8,240,128]{2,1,0:T(8,128)}), f32[8,240,128]{2,1,0:T(8,128)S(1)}, u32[]{:S(2)}, u32[]{:S(2)}) async-start(f32[8,240,128]{2,1,0:T(8,128)} %shard_map.188), calls=%async_computation | async-start | bytes 1966080 | tf_op jit(solution)/shard_map/all_to_all | solution.py:208
  11.8 0.9 copy-start.6
  12.7 1.1 copy-start.13
  13.8 1.1 copy-start.14
  18.3 1.2 copy-start.7
  36.1 43.3 %all-to-all-start.1 = ((f32[8,408,128]{2,1,0:T(8,128)}), f32[8,408,128]{2,1,0:T(8,128)S(1)}, u32[]{:S(2)}, u32[]{:S(2)}) async-start(f32[8,408,128]{2,1,0:T(8,128)} %copy-done.7), calls=%async_computation.1 | async-start | bytes 3342336 | tf_op jit(solution)/shard_map/all_to_all | solution.py:208
  42.7 0.7 copy-start.8
  43.5 1.0 copy-start.10
  44.5 2.2 %collective-permute-start = (f32[2,8,72,128]{3,2,1,0:T(8,128)S(1)}, f32[2,8,72,128]{3,2,1,0:T(8,128)}, u32[]{:S(2)}, u32[]{:S(2)}) collective-permute-start(f32[2,8,72,128]{3,2,1,0:T(8,128)S(1)} %dynamic-slice_bitcast_fusion), channel_id=1, source_target_pairs={{0,1},{1,0},{2,3},{3,2},{4,5},{5,4},{6,7},{7,6},{8,9},{9,8},{10,11... | collective-permute-start | bytes 1769480 | tf_op jit(solution)/shard_map/ppermute | solution.py:202
  44.6 26.5 %copy-start.9 = (f32[8,72,128]{2,1,0:T(8,128)S(1)}, f32[8,72,128]{2,1,0:T(8,128)}, u32[]{:S(2)}) copy-start(f32[8,72,128]{2,1,0:T(8,128)} %copy-done.8) | copy-start | bytes 884740
  44.6 28.0 %copy-start.16 = (f32[48,1,960]{2,1,0:T(1,128)S(1)}, f32[48,1,960]{2,1,0:T(1,128)}, u32[]{:S(2)}) copy-start(f32[48,1,960]{2,1,0:T(1,128)} %param.18) | copy-start | bytes 552964
  48.0 24.7 %copy-start.15 = (s32[16]{0:T(128)S(1)}, s32[16]{0:T(128)}, u32[]{:S(2)}) copy-start(s32[16]{0:T(128)} %constant.73.clone.slot_ref) | copy-start | bytes 196
  48.1 9.1 %collective-permute-start.1 = (f32[8,72,128]{2,1,0:T(8,128)S(1)}, f32[8,72,128]{2,1,0:T(8,128)S(1)}, u32[]{:S(2)}, u32[]{:S(2)}) collective-permute-start(f32[8,72,128]{2,1,0:T(8,128)S(1)} %dynamic-slice_bitcast_fusion.1), channel_id=1, source_target_pairs={{0,2},{1,3},{2,0},{3,1},{4,6},{5,7},{6,4},{7,5},{8,10},{9,11},{10,... | collective-permute-start | bytes 884744 | tf_op jit(solution)/shard_map/ppermute | solution.py:205
  57.2 6.3 %collective-permute-start.2 = (f32[2,72,128]{2,1,0:T(8,128)S(1)}, f32[2,72,128]{2,1,0:T(8,128)S(1)}, u32[]{:S(2)}, u32[]{:S(2)}) collective-permute-start(f32[2,72,128]{2,1,0:T(8,128)S(1)} %get-tuple-element.52), channel_id=1, source_target_pairs={{0,4},{4,0},{8,12},{12,8},{16,20},{20,16},{24,28},{28,24},{1,5},{5... | collective-permute-start | bytes 221192 | tf_op jit(solution)/shard_map/ppermute | solution.py:409
  59.3 11.1 %collective-permute-start.3 = (f32[2,72,128]{2,1,0:T(8,128)S(1)}, f32[2,72,128]{2,1,0:T(8,128)S(1)}, u32[]{:S(2)}, u32[]{:S(2)}) collective-permute-start(f32[2,72,128]{2,1,0:T(8,128)S(1)} %get-tuple-element.53), channel_id=1, source_target_pairs={{0,8},{4,12},{8,0},{12,4},{16,24},{20,28},{24,16},{28,20},{1,9},{5... | collective-permute-start | bytes 221192 | tf_op jit(solution)/shard_map/ppermute | solution.py:409
  60.7 10.5 %collective-permute-start.4 = (f32[2,72,128]{2,1,0:T(8,128)S(1)}, f32[2,72,128]{2,1,0:T(8,128)S(1)}, u32[]{:S(2)}, u32[]{:S(2)}) collective-permute-start(f32[2,72,128]{2,1,0:T(8,128)S(1)} %get-tuple-element.54), channel_id=1, source_target_pairs={{0,12},{4,8},{8,4},{12,0},{16,28},{20,24},{24,20},{28,16},{1,13},{... | collective-permute-start | bytes 221192 | tf_op jit(solution)/shard_map/ppermute | solution.py:409
  71.2 8.2 %collective-permute-start.5 = (f32[8,72,128]{2,1,0:T(8,128)S(1)}, f32[8,72,128]{2,1,0:T(8,128)}, u32[]{:S(2)}, u32[]{:S(2)}) collective-permute-start(f32[8,72,128]{2,1,0:T(8,128)S(1)} %copy-done.9), channel_id=1, source_target_pairs={{0,2},{1,3},{2,0},{3,1},{4,6},{5,7},{6,4},{7,5},{8,10},{9,11},{10,... | collective-permute-start | bytes 884744 | tf_op jit(solution)/shard_map/ppermute | solution.py:205
  74.9 0.8 copy-start.4
  79.4 20.4 %all-to-all-start.2 = ((f32[8,144,128]{2,1,0:T(8,128)}), f32[8,144,128]{2,1,0:T(8,128)S(1)}, u32[]{:S(2)}, u32[]{:S(2)}) async-start(f32[8,144,128]{2,1,0:T(8,128)} %copy-done.4), calls=%async_computation.2 | async-start | bytes 1179648 | tf_op jit(solution)/shard_map/all_to_all | solution.py:208
  86.1 2.1 %collective-permute-start.6 = (f32[2,8,72,128]{3,2,1,0:T(8,128)S(1)}, f32[2,8,72,128]{3,2,1,0:T(8,128)S(1)}, u32[]{:S(2)}, u32[]{:S(2)}) collective-permute-start(f32[2,8,72,128]{3,2,1,0:T(8,128)S(1)} %pad_maximum_fusion), channel_id=1, source_target_pairs={{0,1},{1,0},{2,3},{3,2},{4,5},{5,4},{6,7},{7,6},{8,9},{9,8},{10,11... | collective-permute-start | bytes 1769480 | tf_op jit(solution)/shard_map/ppermute | solution.py:202
  95.1 1.1 copy-start
  99.8 0.8 copy-start.2
  100.6 35.8 %all-to-all-start.3 = ((f32[8,336,128]{2,1,0:T(8,128)}), f32[8,336,128]{2,1,0:T(8,128)S(1)}, u32[]{:S(2)}, u32[]{:S(2)}) async-start(f32[8,336,128]{2,1,0:T(8,128)} %copy-done), calls=%async_computation.3 | async-start | bytes 2752512 | tf_op jit(solution)/shard_map/all_to_all | solution.py:208
  104.4 1.1 copy-start.3
  105.1 2.2 %collective-permute-start.7 = (f32[384,128]{1,0:T(8,128)S(1)}, f32[384,128]{1,0:T(8,128)S(1)}, u32[]{:S(2)}, u32[]{:S(2)}) collective-permute-start(f32[384,128]{1,0:T(8,128)S(1)} %get-tuple-element.69), channel_id=1, source_target_pairs={{0,1},{1,0},{2,3},{3,2},{4,5},{5,4},{6,7},{7,6},{8,9},{9,8},{10,11... | collective-permute-start | bytes 589832 | tf_op jit(solution)/shard_map/ppermute | solution.py:202
  107.0 2.0 %collective-permute-start.9 = (f32[384,128]{1,0:T(8,128)S(1)}, f32[384,128]{1,0:T(8,128)S(1)}, u32[]{:S(2)}, u32[]{:S(2)}) collective-permute-start(f32[384,128]{1,0:T(8,128)S(1)} %get-tuple-element.72), channel_id=1, source_target_pairs={{0,1},{1,0},{2,3},{3,2},{4,5},{5,4},{6,7},{7,6},{8,9},{9,8},{10,11... | collective-permute-start | bytes 589832 | tf_op jit(solution)/shard_map/ppermute | solution.py:202
  107.4 25.2 %copy-start.17 = (f32[360]{0:T(512)S(1)}, f32[360]{0:T(512)}, u32[]{:S(2)}) copy-start(f32[360]{0:T(512)} %param.21) | copy-start | bytes 4324
  107.4 25.2 %copy-start.18 = (f32[360]{0:T(512)S(1)}, f32[360]{0:T(512)}, u32[]{:S(2)}) copy-start(f32[360]{0:T(512)} %param.20) | copy-start | bytes 4324
  107.5 25.2 %copy-start.19 = (f32[360]{0:T(512)S(1)}, f32[360]{0:T(512)}, u32[]{:S(2)}) copy-start(f32[360]{0:T(512)} %param.22) | copy-start | bytes 4324
  107.5 25.2 %copy-start.20 = (f32[360]{0:T(512)S(1)}, f32[360]{0:T(512)}, u32[]{:S(2)}) copy-start(f32[360]{0:T(512)} %param.23) | copy-start | bytes 4324
  107.5 9.9 %collective-permute-start.8 = (f32[8,72,128]{2,1,0:T(8,128)S(1)}, f32[8,72,128]{2,1,0:T(8,128)S(1)}, u32[]{:S(2)}, u32[]{:S(2)}) collective-permute-start(f32[8,72,128]{2,1,0:T(8,128)S(1)} %shard_map.196.basis_half_ref), channel_id=1, source_target_pairs={{0,2},{1,3},{2,0},{3,1},{4,6},{5,7},{6,4},{7,5},{8,10},{9,11},{10,... | collective-permute-start | bytes 884744 | tf_op jit(solution)/shard_map/ppermute | solution.py:205
  109.2 13.9 %collective-permute-start.10 = (f32[8,72,128]{2,1,0:T(8,128)S(1)}, f32[8,72,128]{2,1,0:T(8,128)S(1)}, u32[]{:S(2)}, u32[]{:S(2)}) collective-permute-start(f32[8,72,128]{2,1,0:T(8,128)S(1)} %shard_map.198.gram_half_ref), channel_id=1, source_target_pairs={{0,2},{1,3},{2,0},{3,1},{4,6},{5,7},{6,4},{7,5},{8,10},{9,11},{10,... | collective-permute-start | bytes 884744 | tf_op jit(solution)/shard_map/ppermute | solution.py:205
  110.2 0.7 copy-start.11
  123.1 1.0 copy-start.12
  132.6 1.4 %collective-permute-start.11 = (f32[96,384]{1,0:T(8,128)S(1)}, f32[96,384]{1,0:T(8,128)S(1)}, u32[]{:S(2)}, u32[]{:S(2)}) collective-permute-start(f32[96,384]{1,0:T(8,128)S(1)} %get-tuple-element.74), channel_id=1, source_target_pairs={{0,1},{1,0},{2,3},{3,2},{4,5},{5,4},{6,7},{7,6},{8,9},{9,8},{10,11... | collective-permute-start | bytes 442376 | tf_op jit(solution)/shard_map/ppermute | solution.py:202

commit v3 on v2

--- a/solution.py
+++ b/solution.py
@@ -192,7 +192,8 @@
 
     my_group = lax.axis_index("shard")
     my_rank = lax.axis_index("tensor").astype(jnp.int32)
-    my_edges = jnp.asarray(edges)[my_group]
+    edge_table = jnp.asarray(edges.reshape(-1))
+    group_arg = my_group.astype(jnp.int32).reshape(1)
     rank_arg = my_rank.reshape(1)
     owners = owner_table.reshape(-1)
     core_pairs = [(r, r ^ 1) for r in range(ranks)]
@@ -208,6 +209,9 @@
         return lax.all_to_all(value, "shard", split_axis=0, concat_axis=0, tiled=True)
 
     together = lax.optimization_barrier
+
+    def in_hbm(value):
+        return pltpu.with_memory_space_constraint(value, pltpu.HBM)
 
 
     line_tiles = line // LANES
@@ -259,17 +263,22 @@
     count_scratch = pltpu.SMEM((shards,), jnp.int32)
     stage_scratch = pltpu.VMEM((matrix_total, rows, columns), F32)
 
-    def slot_masks(edges_ref):
+    def slot_masks(group_ref, edges_ref):
         lane = lax.broadcasted_iota(jnp.int32, (1, wide), 1)
-        return [(lane >= edges_ref[k]) & (lane < edges_ref[k + 1]) for k in range(slots)]
-
-
-    def pack_gradient(grad_ref, basis_ref, out_ref, line_ref, dense_ref, sem):
-        fetch = pltpu.make_async_copy(grad_ref, dense_ref, sem)
+        at = group_ref[0] * (slots + 1)
+        return [(lane >= edges_ref[at + k]) & (lane < edges_ref[at + k + 1]) for k in range(slots)]
+
+
+    def pack_gradient(grad_ref, basis_ref, out_ref, line_ref, dense_ref, near_ref, sems):
+        fetch_basis = pltpu.make_async_copy(basis_ref, near_ref, sems.at[0])
+        fetch_basis.start()
+        fetch = pltpu.make_async_copy(grad_ref, dense_ref, sems.at[1])
         fetch.start()
+        fetch_basis.wait()
+        basis = near_ref[:, 0, :]
         for group in range(shards):
             held = [
-                basis_ref[:, matrix * columns : (matrix + 1) * columns]
+                basis[:, matrix * columns : (matrix + 1) * columns]
                 for matrix in slot_matrix[group]
             ]
             held += [jnp.zeros((rows, columns), F32)] * (slots - len(held))
@@ -278,13 +287,18 @@
         send_tiles(dense_ref, line_ref, out_ref, strip_rows)
 
     grad_dense = gradient.reshape(dense)
-    basis_line = left_basis.reshape(rows, matrix_total * columns)
+    basis_hbm = in_hbm(left_basis)
     send_one = call(
         pack_gradient,
         (shards, strip_rows + tile_rows, LANES),
-        (pltpu.with_memory_space_constraint(grad_dense, pltpu.HBM), basis_line),
-        specs=[HBM, None],
-        scratch=[line_scratch, pltpu.VMEM(dense, F32), pltpu.SemaphoreType.DMA(())],
+        (in_hbm(grad_dense), basis_hbm),
+        specs=[HBM, HBM],
+        scratch=[
+            line_scratch,
+            pltpu.VMEM(dense, F32),
+            pltpu.VMEM(left_basis.shape, F32),
+            pltpu.SemaphoreType.DMA((2,)),
+        ],
     )
     came_one = exchange(send_one)
 
@@ -297,7 +311,6 @@
         for group in range(shards)
         for matrix in slot_matrix[group]
     )
-    group_arg = my_group.astype(jnp.int32).reshape(1)
     slot_table = np.full((shards, slots), -1, np.int32)
     for group in range(shards):
         slot_table[group, : len(slot_matrix[group])] = slot_matrix[group]
@@ -318,8 +331,9 @@
         line_ref,
     ):
         fill_owned_table(owner_ref, table_ref, count_ref)
+        basis = basis_ref[:, 0, :]
         for matrix in range(matrix_total):
-            stage_ref[matrix] = basis_ref[:, matrix * columns : (matrix + 1) * columns]
+            stage_ref[matrix] = basis[:, matrix * columns : (matrix + 1) * columns]
         send_owned(stage_ref, table_ref, out_ref, 0)
         send_tiles(second_ref, line_ref, out_ref, owned_rows)
         send_tiles(first_ref, line_ref, out_ref, owned_rows + tile_rows)
@@ -338,7 +352,7 @@
             second_moment.reshape(dense),
             first_moment.reshape(dense),
             grad_dense,
-            basis_line,
+            left_basis,
         ),
         specs=[SMEM, None, None, None, None],
         out_specs=[vmem, vmem, SMEM],
@@ -348,7 +362,9 @@
     came_two = exchange(send_two)
 
 
-    def gram_partials(edges_ref, came_ref, grad_ref, strips_ref, gram_ref, turned_ref):
+    def gram_partials(
+        group_ref, rank_ref, edges_ref, came_ref, grad_ref, strips_ref, kept_ref, core_ref, turned_ref
+    ):
         unpack_columns(came_ref, strip_rows, grad_ref, shards, rows, share)
         for source in range(shards):
             strips_ref[source] = came_ref[source, 0:strip_rows, :]
@@ -359,60 +375,66 @@
             ]
         right = parts_of(turned_ref[...])
         grams = []
-        for mask in slot_masks(edges_ref):
+        for mask in slot_masks(group_ref, edges_ref):
             left = parts_of(jnp.where(mask, grad_ref[...], 0.0))
             grams.append(product(left, right, (1, 1)))
-        for rank in range(ranks):
+        odd = rank_ref[0] % 2 == 1
+        for chip in range(2):
             for group in range(shards):
                 at = slice(group * rows, (group + 1) * rows)
-                held = [g[at, rank * LANES : rank * LANES + columns] for g in grams]
-                store_block(
-                    gram_ref.at[rank],
-                    group,
-                    0,
-                    jnp.concatenate(held, axis=1),
-                    rows,
-                    strip,
-                )
+                low = [g[at, 2 * chip * LANES : 2 * chip * LANES + columns] for g in grams]
+                high = [g[at, (2 * chip + 1) * LANES : (2 * chip + 1) * LANES + columns] for g in grams]
+                low, high = jnp.concatenate(low, axis=1), jnp.concatenate(high, axis=1)
+                mine, other = jnp.where(odd, high, low), jnp.where(odd, low, high)
+                store_block(kept_ref.at[chip], group, 0, mine, rows, strip)
+                store_block(core_ref.at[chip], group, 0, other, rows, strip)
 
     strip_shape = (shards, strip_rows, LANES)
-    grad_full, strips_own, gram_parts = call(
+    grad_full, strips_own, kept, for_core = call(
         gram_partials,
-        [(width, wide), strip_shape, (ranks,) + strip_shape],
-        (my_edges, came_one),
-        specs=[SMEM, None],
+        [(width, wide), strip_shape, (2,) + strip_shape, (2,) + strip_shape],
+        (group_arg, rank_arg, edge_table, came_one),
+        specs=[SMEM, SMEM, SMEM, None],
         scratch=[pltpu.VMEM((ranks * LANES, wide), F32)],
     )
 
-    parts = gram_parts.reshape((2, 2) + strip_shape)
-    my_chip, my_core = my_rank // 2, my_rank % 2
-    for_core = lax.dynamic_index_in_dim(parts, 1 - my_core, 1, False)
-    kept = lax.dynamic_index_in_dim(parts, my_core, 1, False) + over_core(for_core)
-    for_chip = lax.dynamic_index_in_dim(kept, 1 - my_chip, 0, False)
+
+    def add_core(rank_ref, kept_ref, came_ref, mine_ref, far_ref):
+        chip = rank_ref[0] // 2
+        mine_ref[...] = kept_ref[chip] + came_ref[chip]
+        far_ref[...] = kept_ref[1 - chip] + came_ref[1 - chip]
+
+    gram_mine, for_chip = call(
+        add_core,
+        [strip_shape, strip_shape],
+        (rank_arg, kept, over_core(for_core)),
+        specs=[SMEM, None, None],
+    )
     came_chip = over_chip(for_chip)
 
 
-    def sum_strips(group_ref, chip_ref, kept_ref, came_ref, *out_refs):
+    def sum_strips(group_ref, mine_ref, came_ref, *out_refs):
         place = group_ref[0] % half_groups
         for k, out_ref in enumerate(out_refs):
             for j in range(2):
                 at = (place ^ k) + j * half_groups
-                out_ref[j] = kept_ref[chip_ref[0], at] + came_ref[at]
+                out_ref[j] = mine_ref[at] + came_ref[at]
 
     gram_blocks = call(
         sum_strips,
         [(2, strip_rows, LANES)] * half_groups,
-        (group_arg, my_chip.astype(jnp.int32).reshape(1), kept, came_chip),
-        specs=[SMEM, SMEM, None, None],
-    )
+        (group_arg, gram_mine, came_chip),
+        specs=[SMEM, None, None],
+    )
+    *gram_blocks, strips_own = together((*gram_blocks, strips_own))
     gram_blocks = [gram_blocks[0]] + [
         lax.ppermute(gram_blocks[k], "shard", [(s, s ^ k) for s in range(shards)])
         for k in range(1, half_groups)
     ]
 
 
-    *gram_blocks, strips_own = together((*gram_blocks, strips_own))
     strips_chip = over_chip(strips_own)
+    *gram_blocks, strips_chip = together((*gram_blocks, strips_chip))
 
 
     def split_owned(rank_ref, came_ref, *refs):
@@ -464,13 +486,12 @@
 
 
     def new_grams(group_ref, table_ref, slot_ref, gram_ref, *refs):
-        came, (out_ref, stage_ref) = refs[:half_groups], refs[half_groups:]
+        came, (out_ref, stage_ref, near_ref, sem) = refs[:half_groups], refs[half_groups:]
+        fetch = pltpu.make_async_copy(gram_ref, near_ref, sem)
+        fetch.start()
         group = group_ref[0]
         half = group // half_groups
-        for matrix in range(matrix_total):
-            old = 0.95 * gram_ref[:, matrix * columns : (matrix + 1) * columns]
-            stage_ref[0, matrix] = jnp.where(half == 0, old, 0.0)
-            stage_ref[1, matrix] = jnp.where(half == 0, 0.0, old)
+        stage_ref[...] = jnp.zeros_like(stage_ref)
         for k, came_ref in enumerate(came):
             for j in range(2):
                 block = load_block(came_ref, j, 0, rows, strip)
@@ -479,6 +500,11 @@
                     at = jnp.where(matrix >= 0, matrix, matrix_total)
                     part = block[:, m * columns : (m + 1) * columns]
                     stage_ref[j, at] = stage_ref[j, at] + 0.05 * part
+        fetch.wait()
+        old = 0.95 * near_ref[:, 0, :]
+        for matrix in range(matrix_total):
+            own = old[:, matrix * columns : (matrix + 1) * columns]
+            stage_ref[half, matrix] = stage_ref[half, matrix] + own
         for dest in range(shards):
             for j in range(2):
                 held = []
@@ -496,18 +522,24 @@
             group_arg,
             owned_table,
             slot_table,
-            left_gram.reshape(rows, matrix_total * columns),
+            in_hbm(left_gram),
             *gram_blocks,
         ),
-        specs=[SMEM, SMEM, SMEM] + [None] * (1 + half_groups),
-        scratch=[pltpu.VMEM((2, matrix_total + 1, rows, columns), F32)],
-    )
-    came_two, send_four, strips_chip = together((came_two, send_four, strips_chip))
-    came_four = exchange(send_four)
+        specs=[SMEM, SMEM, SMEM, HBM] + [None] * half_groups,
+        scratch=[
+            pltpu.VMEM((2, matrix_total + 1, rows, columns), F32),
+            pltpu.VMEM(left_gram.shape, F32),
+            pltpu.SemaphoreType.DMA(()),
+        ],
+    )
+    send_four = in_hbm(send_four)
+    came_two, send_four = together((came_two, send_four))
+    came_four = in_hbm(exchange(send_four))
     pair = over_core(jnp.stack([strips_own, strips_chip]))
 
 
     def rotate_gradient(
+        group_ref,
         rank_ref,
         edges_ref,
         own_ref,
@@ -538,21 +570,22 @@
                 basis_ref[k, at, :] = jnp.concatenate(ordered, axis=1)
         grad = parts_of(grad_ref[...])
         hat = jnp.zeros((width, wide), F32)
-        for k, mask in enumerate(slot_masks(edges_ref)):
+        for k, mask in enumerate(slot_masks(group_ref, edges_ref)):
             hat = jnp.where(mask, product(parts_of(basis_ref[k].T), grad), hat)
         hat_ref[...] = hat
 
     basis_full, hat_full = call(
         rotate_gradient,
         [(slots, width, width), (width, wide)],
-        (rank_arg, my_edges, strips_own, strips_chip, pair, grad_full),
-        specs=[SMEM, SMEM] + [None] * 4,
+        (group_arg, rank_arg, edge_table, strips_own, strips_chip, pair, grad_full),
+        specs=[SMEM, SMEM, SMEM] + [None] * 4,
     )
 
     basis_half, basis_far = collect(came_two, 0)
 
 
     def directions(
+        group_ref,
         edges_ref,
         came_ref,
         grad_ref,
@@ -565,7 +598,7 @@
         unpack_columns(came_ref, owned_rows, second_ref, shards, rows, share)
         second_ref[...] = 0.95 * second_ref[...] + 0.05 * hat_ref[...] * hat_ref[...]
         unpack_columns(came_ref, owned_rows + tile_rows, moment_ref, shards, rows, share)
-        masks = slot_masks(edges_ref)
+        masks = slot_masks(group_ref, edges_ref)
         moment = parts_of(0.9 * moment_ref[...] + 0.1 * grad_ref[...])
         hat = jnp.zeros((width, wide), F32)
         for k, mask in enumerate(masks):
@@ -581,8 +614,8 @@
     send_five = call(
         directions,
         (shards, 2 * tile_rows, LANES),
-        (my_edges, came_two, grad_full, hat_full, basis_full),
-        specs=[SMEM] + [None] * 4,
+        (group_arg, edge_table, came_two, grad_full, hat_full, basis_full),
+        specs=[SMEM, SMEM] + [None] * 4,
         scratch=[pltpu.VMEM((width, wide), F32)] * 2,
     )
     came_four, send_five = together((came_four, send_five))
@@ -632,7 +665,7 @@
         other_ref[...] = jnp.where(even_core, odd, low)
         fetch.wait()
 
-    weight_dense = pltpu.with_memory_space_constraint(weight.reshape(dense), pltpu.HBM)
+    weight_dense = in_hbm(weight.reshape(dense))
     frame_mine, frame_other, weight_near = call(
         refresh,
         [(columns, width), (columns, width), dense],
@@ -642,7 +675,7 @@
     )
     frame_came = over_core(frame_other)
     pair_out = jnp.where(
-        my_core == 0,
+        my_rank % 2 == 0,
         jnp.stack([frame_mine, frame_came]),
         jnp.stack([frame_came, frame_mine]),
     )

time: 139 us -> 138 us (level)
  local copies, waits for them, and re-layouts: 12.7 us -> 4.46 us
  waiting for transfers between devices: 60.3 us -> 67.7 us
  Pallas kernels: 30.7 us -> 33.9 us
  other arithmetic: 3.64 us -> 1.38 us
    all_to_all x4, waiting for transfers between devices: 21.8 us -> 29.9 us  [exchange(): lax.all_to_all(value, 'shard', split_axis=0, concat_axis=0, tiled=True)]
    unnamed x46 -> x28, local copies, waits for them, and re-layouts: 11.8 us -> 4.37 us
    pallas_call x13 -> x14, Pallas kernels: 30.7 us -> 33.9 us  [call(): pl.pallas_call(kernel, out_shape=shapes, grid=grid, in_specs=[s or vmem f...]
    ppermute x4, waiting for transfers between devices: 23.3 us -> 20.3 us  [over_chip(): return lax.ppermute(value, 'tensor', chip_pairs)]
    ppermute x3, waiting for transfers between devices: 10.4 us -> 12.8 us  [body(): lax.ppermute(gram_blocks[k], 'shard', [(s, s ^ k) for s in range(shards)])]
  transfers between devices with their start and end apart: 16 -> 16, of which waited for: 13 -> 13; matrix products, arithmetic and copies ran while one was open for 3% -> 1% of each run, Pallas kernels for 19% -> 21%
where the time goes in v3:
time: 138 us
  waiting for transfers between devices  67.7 us (49%)
  Pallas kernels  33.9 us (25%)
  starting transfers between devices  29.4 us (21%)
  local copies, waits for them, and re-layouts  4.46 us (3%)
    pallas_call x14, Pallas kernels, call(): pl.pallas_call(kernel, out_shape=shapes, grid=grid, in_specs=[s or vmem f...  33.9 us
    all_to_all x4, waiting for transfers between devices, exchange(): lax.all_to_all(value, 'shard', split_axis=0, concat_axis=0, tiled=True)  29.9 us
    ppermute x4, waiting for transfers between devices, over_chip(): return lax.ppermute(value, 'tensor', chip_pairs)  20.3 us
    all_to_all x4, starting transfers between devices, exchange(): lax.all_to_all(value, 'shard', split_axis=0, concat_axis=0, tiled=True)  19.6 us
    ppermute x3, waiting for transfers between devices, body(): lax.ppermute(gram_blocks[k], 'shard', [(s, s ^ k) for s in range(shards)])  12.8 us
    ppermute x4, starting transfers between devices, over_chip(): return lax.ppermute(value, 'tensor', chip_pairs)  5.54 us
    ppermute x5, waiting for transfers between devices, over_core(): return lax.ppermute(value, 'tensor', core_pairs)  4.7 us
    unnamed x28, local copies, waits for them, and re-layouts  4.37 us
  transfers between devices with their start and end apart: 16, of which 13 were waited for; matrix products, arithmetic and copies ran while one was open for 1% of the time, Pallas kernels for 21%

profile of v3, /device:TPU:0, one launch (start us, length us, event | category | flops | bytes accessed | tf_op | source)
XLA Modules:
  0.0 137.7 jit_solution(8753706446642998861)
XLA Ops:
  0.6 2.6 %shard_map.188 = f32[8,240,128]{2,1,0:T(8,128)} custom-call(f32[1296,128]{1,0:T(8,128)} %bitcast.19, f32[48,1,960]{2,1,0:T(1,128)} %basis_ref.3), custom_call_target="tpu_custom_call" | custom-call | tf_op jit(solution)/shard_map/pallas_call | solution.py:138
  3.3 7.4 %all-to-all-start = ((f32[8,240,128]{2,1,0:T(8,128)}), f32[8,240,128]{2,1,0:T(8,128)S(1)}, u32[]{:S(2)}, u32[]{:S(2)}) async-start(f32[8,240,128]{2,1,0:T(8,128)} %shard_map.188), calls=%async_computation | async-start | bytes 1966080 | tf_op jit(solution)/shard_map/all_to_all | solution.py:209
  10.7 0.1 reshape.47.owner_ref
  10.8 0.9 copy-done.4
  11.7 1.1 copy-done.5
  12.8 1.1 copy-done.6
  13.9 3.9 %shard_map.189 = (f32[8,408,128]{2,1,0:T(8,128)S(1)}, f32[1296,128]{1,0:T(8,128)}, s32[16]{0:T(128)S(1)}) custom-call(s32[10]{0:T(128)S(1)} %reshape.47.owner_ref, f32[1296,128]{1,0:T(8,128)S(1)} %bitcast.23, f32[1296,128]{1,0:T(8,128)S(1)} %bitcast.24, f32[1296,128]{1,0:T(8,128)S(1)} %bitcast.20, f32[48,1,960]{2,1,0:T(1,128)S(1)} %copy-done.4), custom_call_target="tpu_custom_call" | custom-call | tf_op jit(solution)/shard_map/pallas_call | solution.py:138
  17.8 1.2 copy-done.1
  19.0 16.1 %all-to-all-done.came_ref = f32[8,240,128]{2,1,0:T(8,128)S(1)} async-done(((f32[8,240,128]{2,1,0:T(8,128)}), f32[8,240,128]{2,1,0:T(8,128)S(1)}, u32[]{:S(2)}, u32[]{:S(2)}) %all-to-all-start) | async-done | bytes 983072 | tf_op jit(solution)/shard_map/all_to_all | solution.py:209
  35.1 3.7 %all-to-all-start.1 = ((f32[8,408,128]{2,1,0:T(8,128)}), f32[8,408,128]{2,1,0:T(8,128)S(1)}, u32[]{:S(2)}, u32[]{:S(2)}) async-start(f32[8,408,128]{2,1,0:T(8,128)} %copy-done.1), calls=%async_computation.1 | async-start | bytes 3342336 | tf_op jit(solution)/shard_map/all_to_all | solution.py:209
  38.9 2.3 %shard_map.190 = (f32[384,512]{1,0:T(8,128)S(1)}, f32[8,72,128]{2,1,0:T(8,128)S(1)}, f32[2,8,72,128]{3,2,1,0:T(8,128)S(1)}, f32[2,8,72,128]{3,2,1,0:T(8,128)S(1)}) custom-call(s32[1]{0:T(128)} %bitcast.3.group_ref, s32[1]{0:T(128)} %bitcast.4.rank_ref, s32[24]{0:T(128)S(1)} %copy-done.7, f32[8,240,128]{2,1,0:T(8,128)S(1)} %all-to-all-done.came_ref), custom_call_target="tpu_custom_call" | custom-call | tf_op jit(solution)/shard_map/pallas_call | solution.py:138
  41.2 0.1 collective-permute-start
  41.3 2.0 %collective-permute-done.came_ref = f32[2,8,72,128]{3,2,1,0:T(8,128)S(1)} collective-permute-done((f32[2,8,72,128]{3,2,1,0:T(8,128)S(1)}, f32[2,8,72,128]{3,2,1,0:T(8,128)S(1)}, u32[]{:S(2)}, u32[]{:S(2)}) %collective-permute-start) | collective-permute-done | bytes 589856 | tf_op jit(solution)/shard_map/ppermute | solution.py:203
  43.3 0.1 shard_map.191
  43.3 1.6 %collective-permute-start.1 = (f32[8,72,128]{2,1,0:T(8,128)S(1)}, f32[8,72,128]{2,1,0:T(8,128)S(1)}, u32[]{:S(2)}, u32[]{:S(2)}) collective-permute-start(f32[8,72,128]{2,1,0:T(8,128)S(1)} %get-tuple-element.60), channel_id=1, source_target_pairs={{0,2},{1,3},{2,0},{3,1},{4,6},{5,7},{6,4},{7,5},{8,10},{9,11},{10,... | collective-permute-start | bytes 884744 | tf_op jit(solution)/shard_map/ppermute | solution.py:206
  44.9 7.6 %collective-permute-done.1.came_ref = f32[8,72,128]{2,1,0:T(8,128)S(1)} collective-permute-done((f32[8,72,128]{2,1,0:T(8,128)S(1)}, f32[8,72,128]{2,1,0:T(8,128)S(1)}, u32[]{:S(2)}, u32[]{:S(2)}) %collective-permute-start.1) | collective-permute-done | bytes 294944 | tf_op jit(solution)/shard_map/ppermute | solution.py:206
  52.5 1.6 %collective-permute-start.5 = (f32[8,72,128]{2,1,0:T(8,128)S(1)}, f32[8,72,128]{2,1,0:T(8,128)S(1)}, u32[]{:S(2)}, u32[]{:S(2)}) collective-permute-start(f32[8,72,128]{2,1,0:T(8,128)S(1)} %get-tuple-element.70.own_ref), channel_id=1, source_target_pairs={{0,2},{1,3},{2,0},{3,1},{4,6},{5,7},{6,4},{7,5},{8,10},{9,11},{10,... | collective-permute-start | bytes 884744 | tf_op jit(solution)/shard_map/ppermute | solution.py:206
  54.1 2.0 %collective-permute-start.2 = (f32[2,72,128]{2,1,0:T(8,128)S(1)}, f32[2,72,128]{2,1,0:T(8,128)S(1)}, u32[]{:S(2)}, u32[]{:S(2)}) collective-permute-start(f32[2,72,128]{2,1,0:T(8,128)S(1)} %get-tuple-element.67), channel_id=1, source_target_pairs={{0,4},{4,0},{8,12},{12,8},{16,20},{20,16},{24,28},{28,24},{1,5},{5... | collective-permute-start | bytes 221192 | tf_op jit(solution)/shard_map/ppermute | solution.py:431
  56.0 1.5 %collective-permute-start.3 = (f32[2,72,128]{2,1,0:T(8,128)S(1)}, f32[2,72,128]{2,1,0:T(8,128)S(1)}, u32[]{:S(2)}, u32[]{:S(2)}) collective-permute-start(f32[2,72,128]{2,1,0:T(8,128)S(1)} %get-tuple-element.68), channel_id=1, source_target_pairs={{0,8},{4,12},{8,0},{12,4},{16,24},{20,28},{24,16},{28,20},{1,9},{5... | collective-permute-start | bytes 221192 | tf_op jit(solution)/shard_map/ppermute | solution.py:431
  57.5 2.0 %collective-permute-done.2.refs_1_ = f32[2,72,128]{2,1,0:T(8,128)S(1)} collective-permute-done((f32[2,72,128]{2,1,0:T(8,128)S(1)}, f32[2,72,128]{2,1,0:T(8,128)S(1)}, u32[]{:S(2)}, u32[]{:S(2)}) %collective-permute-start.2) | collective-permute-done | bytes 73760 | tf_op jit(solution)/shard_map/ppermute | solution.py:431
  59.5 10.0 %collective-permute-done.3.refs_2_ = f32[2,72,128]{2,1,0:T(8,128)S(1)} collective-permute-done((f32[2,72,128]{2,1,0:T(8,128)S(1)}, f32[2,72,128]{2,1,0:T(8,128)S(1)}, u32[]{:S(2)}, u32[]{:S(2)}) %collective-permute-start.3) | collective-permute-done | bytes 73760 | tf_op jit(solution)/shard_map/ppermute | solution.py:431
  69.5 0.8 collective-permute-done.4.refs_3_
  70.3 2.9 %shard_map.193 = f32[8,144,128]{2,1,0:T(8,128)} custom-call(s32[1]{0:T(128)} %bitcast.3.group_ref, s32[16]{0:T(128)S(1)} %get-tuple-element.55.table_ref, s32[16]{0:T(128)S(1)} %copy-done.8, f32[48,1,960]{2,1,0:T(1,128)} %gram_ref.1, f32[2,72,128]{2,1,0:T(8,128)S(1)} %get-tuple-element.71.refs_0_, f32[2,72,128]{2,1,0:T(8,128)S(1)} %collective-permute-done.2.refs_1_, ...), custom_call_target="tpu_custom_call" | custom-call | tf_op jit(solution)/shard_map/pallas_call | solution.py:138
  73.3 4.8 %all-to-all-done.1.came_ref = f32[8,408,128]{2,1,0:T(8,128)S(1)} async-done(((f32[8,408,128]{2,1,0:T(8,128)}), f32[8,408,128]{2,1,0:T(8,128)S(1)}, u32[]{:S(2)}, u32[]{:S(2)}) %all-to-all-start.1) | async-done | bytes 1671200 | tf_op jit(solution)/shard_map/all_to_all | solution.py:209
  78.1 4.7 %all-to-all-start.2 = ((f32[8,144,128]{2,1,0:T(8,128)}), f32[8,144,128]{2,1,0:T(8,128)}, u32[]{:S(2)}, u32[]{:S(2)}) async-start(f32[8,144,128]{2,1,0:T(8,128)} %shard_map.193), calls=%async_computation.2 | async-start | bytes 1179648 | tf_op jit(solution)/shard_map/all_to_all | solution.py:209
  82.9 0.1 collective-permute-start.6
  82.9 2.0 %collective-permute-done.6.pair_ref = f32[2,8,72,128]{3,2,1,0:T(8,128)S(1)} collective-permute-done((f32[2,8,72,128]{3,2,1,0:T(8,128)S(1)}, f32[2,8,72,128]{3,2,1,0:T(8,128)S(1)}, u32[]{:S(2)}, u32[]{:S(2)}) %collective-permute-start.6) | collective-permute-done | bytes 589856 | tf_op jit(solution)/shard_map/ppermute | solution.py:203
  84.9 2.5 %shard_map.194 = (f32[2,384,384]{2,1,0:T(8,128)S(1)}, f32[384,512]{1,0:T(8,128)S(1)}) custom-call(s32[1]{0:T(128)} %bitcast.3.group_ref, s32[1]{0:T(128)} %bitcast.4.rank_ref, s32[24]{0:T(128)S(1)} %copy-done.7, f32[8,72,128]{2,1,0:T(8,128)S(1)} %copy-done.3, f32[8,72,128]{2,1,0:T(8,128)S(1)} %collective-permute-done.5.chip_ref, ...), custom_call_target="tpu_custom_call" | custom-call | tf_op jit(solution)/shard_map/pallas_call | solution.py:138
  87.4 5.1 %shard_map.195 = f32[8,336,128]{2,1,0:T(8,128)} custom-call(s32[1]{0:T(128)} %bitcast.3.group_ref, s32[24]{0:T(128)S(1)} %copy-done.7, f32[8,408,128]{2,1,0:T(8,128)S(1)} %all-to-all-done.1.came_ref, f32[384,512]{1,0:T(8,128)S(1)} %get-tuple-element.77.grad_ref, f32[384,512]{1,0:T(8,128)S(1)} %get-tuple-element.79.hat_ref, ...), custom_call_target="tpu_custom_call" | custom-call | tf_op jit(solution)/shard_map/pallas_call | solution.py:138
  92.6 6.4 %all-to-all-done.2.came_ref = f32[8,144,128]{2,1,0:T(8,128)} async-done(((f32[8,144,128]{2,1,0:T(8,128)}), f32[8,144,128]{2,1,0:T(8,128)}, u32[]{:S(2)}, u32[]{:S(2)}) %all-to-all-start.2) | async-done | bytes 589856 | tf_op jit(solution)/shard_map/all_to_all | solution.py:209
  99.0 3.8 %all-to-all-start.3 = ((f32[8,336,128]{2,1,0:T(8,128)}), f32[8,336,128]{2,1,0:T(8,128)S(1)}, u32[]{:S(2)}, u32[]{:S(2)}) async-start(f32[8,336,128]{2,1,0:T(8,128)} %shard_map.195), calls=%async_computation.3 | async-start | bytes 2752512 | tf_op jit(solution)/shard_map/all_to_all | solution.py:209
  102.7 0.7 shard_map.196
  103.4 0.1 collective-permute-start.7
  103.5 2.7 %shard_map.198 = (f32[2,96,384]{2,1,0:T(8,128)}, f32[384,128]{1,0:T(8,128)S(1)}, f32[384,128]{1,0:T(8,128)S(1)}) custom-call(s32[1]{0:T(128)} %bitcast.4.rank_ref, f32[8,144,128]{2,1,0:T(8,128)} %all-to-all-done.2.came_ref), custom_call_target="tpu_custom_call" | custom-call | tf_op jit(solution)/shard_map/pallas_call | solution.py:138
  106.2 0.5 collective-permute-start.9
  106.7 0.2 shard_map.197.basis_half_ref
  106.9 1.6 %collective-permute-start.8 = (f32[8,72,128]{2,1,0:T(8,128)S(1)}, f32[8,72,128]{2,1,0:T(8,128)S(1)}, u32[]{:S(2)}, u32[]{:S(2)}) collective-permute-start(f32[8,72,128]{2,1,0:T(8,128)S(1)} %shard_map.197.basis_half_ref), channel_id=1, source_target_pairs={{0,2},{1,3},{2,0},{3,1},{4,6},{5,7},{6,4},{7,5},{8,10},{9,11},{10,... | collective-permute-start | bytes 884744 | tf_op jit(solution)/shard_map/ppermute | solution.py:206
  108.5 0.2 shard_map.199.gram_half_ref
  108.7 0.9 collective-permute-start.10
  109.5 7.3 %collective-permute-done.8.basis_far_ref = f32[8,72,128]{2,1,0:T(8,128)S(1)} collective-permute-done((f32[8,72,128]{2,1,0:T(8,128)S(1)}, f32[8,72,128]{2,1,0:T(8,128)S(1)}, u32[]{:S(2)}, u32[]{:S(2)}) %collective-permute-start.8) | collective-permute-done | bytes 294944 | tf_op jit(solution)/shard_map/ppermute | solution.py:206
  116.8 5.4 %collective-permute-done.10.gram_far_ref = f32[8,72,128]{2,1,0:T(8,128)S(1)} collective-permute-done((f32[8,72,128]{2,1,0:T(8,128)S(1)}, f32[8,72,128]{2,1,0:T(8,128)S(1)}, u32[]{:S(2)}, u32[]{:S(2)}) %collective-permute-start.10) | collective-permute-done | bytes 294944 | tf_op jit(solution)/shard_map/ppermute | solution.py:206
  122.2 8.6 %shard_map.200 = (f32[96,384]{1,0:T(8,128)S(1)}, f32[96,384]{1,0:T(8,128)S(1)}, f32[1296,128]{1,0:T(8,128)S(1)}) custom-call(s32[1]{0:T(128)} %bitcast.4.rank_ref, f32[8,72,128]{2,1,0:T(8,128)S(1)} %shard_map.197.basis_half_ref, f32[8,72,128]{2,1,0:T(8,128)S(1)} %collective-permute-done.8.basis_far_ref, f32[8,72,128]{2,1,0:T(8,128)S(1)} %shard_map.199.gram_half_ref, ...), custom_call_target="tpu_custom_call" | custom-call | tf_op jit(solution)/shard_map/pallas_call | solution.py:138
  130.8 0.1 collective-permute-start.11
  130.9 0.6 multiply_subtract_fusion
  131.5 0.7 collective-permute-done.11
  132.2 0.7 maximum_select_fusion
  133.0 2.6 %all-to-all-done.3.came_ref = f32[8,336,128]{2,1,0:T(8,128)S(1)} async-done(((f32[8,336,128]{2,1,0:T(8,128)}), f32[8,336,128]{2,1,0:T(8,128)S(1)}, u32[]{:S(2)}, u32[]{:S(2)}) %all-to-all-start.3) | async-done | bytes 1376288 | tf_op jit(solution)/shard_map/all_to_all | solution.py:209
  135.6 2.1 %shard_map.201 = (f32[1296,128]{1,0:T(8,128)}, f32[1296,128]{1,0:T(8,128)}) custom-call(f32[8,336,128]{2,1,0:T(8,128)S(1)} %all-to-all-done.3.came_ref, f32[1296,128]{1,0:T(8,128)S(1)} %get-tuple-element.92.weight_ref), custom_call_target="tpu_custom_call" | custom-call | tf_op jit(solution)/shard_map/pallas_call | solution.py:138
  (30 shorter events, 0.2 us)
Async XLA Ops:
  3.3 7.5 %copy-start.13 = (s32[2,5]{1,0:T(2,128)S(1)}, s32[2,5]{1,0:T(2,128)}, u32[]{:S(2)}) copy-start(s32[2,5]{1,0:T(2,128)} %param.19) | copy-start | bytes 124
  3.3 7.5 %copy-start = (f32[48,1,3456]{2,1,0:T(1,128)S(1)}, f32[48,1,3456]{2,1,0:T(1,128)}, u32[]{:S(2)}) copy-start(f32[48,1,3456]{2,1,0:T(1,128)} %param.13) | copy-start | bytes 1990660
  3.3 31.8 %all-to-all-start = ((f32[8,240,128]{2,1,0:T(8,128)}), f32[8,240,128]{2,1,0:T(8,128)S(1)}, u32[]{:S(2)}, u32[]{:S(2)}) async-start(f32[8,240,128]{2,1,0:T(8,128)} %shard_map.188), calls=%async_computation | async-start | bytes 1966080 | tf_op jit(solution)/shard_map/all_to_all | solution.py:209
  10.8 0.9 copy-start.4
  11.7 1.1 copy-start.5
  12.8 1.1 copy-start.6
  17.8 1.2 copy-start.1
  35.1 3.7 %copy-start.7 = (s32[24]{0:T(128)S(1)}, s32[24]{0:T(128)}, u32[]{:S(2)}) copy-start(s32[24]{0:T(128)} %constant.45.clone.edges_ref) | copy-start | bytes 292
  35.1 43.0 %all-to-all-start.1 = ((f32[8,408,128]{2,1,0:T(8,128)}), f32[8,408,128]{2,1,0:T(8,128)S(1)}, u32[]{:S(2)}, u32[]{:S(2)}) async-start(f32[8,408,128]{2,1,0:T(8,128)} %copy-done.1), calls=%async_computation.1 | async-start | bytes 3342336 | tf_op jit(solution)/shard_map/all_to_all | solution.py:209
  38.9 31.5 %copy-start.8 = (s32[16]{0:T(128)S(1)}, s32[16]{0:T(128)}, u32[]{:S(2)}) copy-start(s32[16]{0:T(128)} %constant.46.clone.slot_ref) | copy-start | bytes 196
  41.2 29.1 %copy-start.2 = (f32[8,72,128]{2,1,0:T(8,128)}, f32[8,72,128]{2,1,0:T(8,128)S(1)}, u32[]{:S(2)}) copy-start(f32[8,72,128]{2,1,0:T(8,128)S(1)} %get-tuple-element.70.own_ref) | copy-start | bytes 884740
  41.2 2.1 %collective-permute-start = (f32[2,8,72,128]{3,2,1,0:T(8,128)S(1)}, f32[2,8,72,128]{3,2,1,0:T(8,128)S(1)}, u32[]{:S(2)}, u32[]{:S(2)}) collective-permute-start(f32[2,8,72,128]{3,2,1,0:T(8,128)S(1)} %get-tuple-element.58), channel_id=1, source_target_pairs={{0,1},{1,0},{2,3},{3,2},{4,5},{5,4},{6,7},{7,6},{8,9},{9,8},{10,11... | collective-permute-start | bytes 1769480 | tf_op jit(solution)/shard_map/ppermute | solution.py:203
  43.3 9.1 %collective-permute-start.1 = (f32[8,72,128]{2,1,0:T(8,128)S(1)}, f32[8,72,128]{2,1,0:T(8,128)S(1)}, u32[]{:S(2)}, u32[]{:S(2)}) collective-permute-start(f32[8,72,128]{2,1,0:T(8,128)S(1)} %get-tuple-element.60), channel_id=1, source_target_pairs={{0,2},{1,3},{2,0},{3,1},{4,6},{5,7},{6,4},{7,5},{8,10},{9,11},{10,... | collective-permute-start | bytes 884744 | tf_op jit(solution)/shard_map/ppermute | solution.py:206
  52.5 17.8 %collective-permute-start.5 = (f32[8,72,128]{2,1,0:T(8,128)S(1)}, f32[8,72,128]{2,1,0:T(8,128)S(1)}, u32[]{:S(2)}, u32[]{:S(2)}) collective-permute-start(f32[8,72,128]{2,1,0:T(8,128)S(1)} %get-tuple-element.70.own_ref), channel_id=1, source_target_pairs={{0,2},{1,3},{2,0},{3,1},{4,6},{5,7},{6,4},{7,5},{8,10},{9,11},{10,... | collective-permute-start | bytes 884744 | tf_op jit(solution)/shard_map/ppermute | solution.py:206
  54.1 5.5 %collective-permute-start.2 = (f32[2,72,128]{2,1,0:T(8,128)S(1)}, f32[2,72,128]{2,1,0:T(8,128)S(1)}, u32[]{:S(2)}, u32[]{:S(2)}) collective-permute-start(f32[2,72,128]{2,1,0:T(8,128)S(1)} %get-tuple-element.67), channel_id=1, source_target_pairs={{0,4},{4,0},{8,12},{12,8},{16,20},{20,16},{24,28},{28,24},{1,5},{5... | collective-permute-start | bytes 221192 | tf_op jit(solution)/shard_map/ppermute | solution.py:431
  56.0 13.5 %collective-permute-start.3 = (f32[2,72,128]{2,1,0:T(8,128)S(1)}, f32[2,72,128]{2,1,0:T(8,128)S(1)}, u32[]{:S(2)}, u32[]{:S(2)}) collective-permute-start(f32[2,72,128]{2,1,0:T(8,128)S(1)} %get-tuple-element.68), channel_id=1, source_target_pairs={{0,8},{4,12},{8,0},{12,4},{16,24},{20,28},{24,16},{28,20},{1,9},{5... | collective-permute-start | bytes 221192 | tf_op jit(solution)/shard_map/ppermute | solution.py:431
  57.5 12.8 %collective-permute-start.4 = (f32[2,72,128]{2,1,0:T(8,128)S(1)}, f32[2,72,128]{2,1,0:T(8,128)S(1)}, u32[]{:S(2)}, u32[]{:S(2)}) collective-permute-start(f32[2,72,128]{2,1,0:T(8,128)S(1)} %get-tuple-element.69), channel_id=1, source_target_pairs={{0,12},{4,8},{8,4},{12,0},{16,28},{20,24},{24,20},{28,16},{1,13},{... | collective-permute-start | bytes 221192 | tf_op jit(solution)/shard_map/ppermute | solution.py:431
  73.3 9.5 %copy-start.3 = (f32[8,72,128]{2,1,0:T(8,128)S(1)}, f32[8,72,128]{2,1,0:T(8,128)}, u32[]{:S(2)}) copy-start(f32[8,72,128]{2,1,0:T(8,128)} %copy-done.2) | copy-start | bytes 884740
  78.1 20.9 %all-to-all-start.2 = ((f32[8,144,128]{2,1,0:T(8,128)}), f32[8,144,128]{2,1,0:T(8,128)}, u32[]{:S(2)}, u32[]{:S(2)}) async-start(f32[8,144,128]{2,1,0:T(8,128)} %shard_map.193), calls=%async_computation.2 | async-start | bytes 1179648 | tf_op jit(solution)/shard_map/all_to_all | solution.py:209
  82.9 2.1 %collective-permute-start.6 = (f32[2,8,72,128]{3,2,1,0:T(8,128)S(1)}, f32[2,8,72,128]{3,2,1,0:T(8,128)S(1)}, u32[]{:S(2)}, u32[]{:S(2)}) collective-permute-start(f32[2,8,72,128]{3,2,1,0:T(8,128)S(1)} %pad_maximum_fusion), channel_id=1, source_target_pairs={{0,1},{1,0},{2,3},{3,2},{4,5},{5,4},{6,7},{7,6},{8,9},{9,8},{10,11... | collective-permute-start | bytes 1769480 | tf_op jit(solution)/shard_map/ppermute | solution.py:203
  99.0 36.6 %all-to-all-start.3 = ((f32[8,336,128]{2,1,0:T(8,128)}), f32[8,336,128]{2,1,0:T(8,128)S(1)}, u32[]{:S(2)}, u32[]{:S(2)}) async-start(f32[8,336,128]{2,1,0:T(8,128)} %shard_map.195), calls=%async_computation.3 | async-start | bytes 2752512 | tf_op jit(solution)/shard_map/all_to_all | solution.py:209
  103.4 3.3 %collective-permute-start.7 = (f32[384,128]{1,0:T(8,128)S(1)}, f32[384,128]{1,0:T(8,128)S(1)}, u32[]{:S(2)}, u32[]{:S(2)}) collective-permute-start(f32[384,128]{1,0:T(8,128)S(1)} %get-tuple-element.83), channel_id=1, source_target_pairs={{0,1},{1,0},{2,3},{3,2},{4,5},{5,4},{6,7},{7,6},{8,9},{9,8},{10,11... | collective-permute-start | bytes 589832 | tf_op jit(solution)/shard_map/ppermute | solution.py:203
  106.2 2.3 %collective-permute-start.9 = (f32[384,128]{1,0:T(8,128)S(1)}, f32[384,128]{1,0:T(8,128)S(1)}, u32[]{:S(2)}, u32[]{:S(2)}) collective-permute-start(f32[384,128]{1,0:T(8,128)S(1)} %get-tuple-element.86), channel_id=1, source_target_pairs={{0,1},{1,0},{2,3},{3,2},{4,5},{5,4},{6,7},{7,6},{8,9},{9,8},{10,11... | collective-permute-start | bytes 589832 | tf_op jit(solution)/shard_map/ppermute | solution.py:203
  106.9 24.0 %copy-start.9 = (f32[360]{0:T(512)S(1)}, f32[360]{0:T(512)}, u32[]{:S(2)}) copy-start(f32[360]{0:T(512)} %param.21) | copy-start | bytes 4324
  106.9 24.0 %copy-start.10 = (f32[360]{0:T(512)S(1)}, f32[360]{0:T(512)}, u32[]{:S(2)}) copy-start(f32[360]{0:T(512)} %param.20) | copy-start | bytes 4324
  106.9 24.0 %copy-start.11 = (f32[360]{0:T(512)S(1)}, f32[360]{0:T(512)}, u32[]{:S(2)}) copy-start(f32[360]{0:T(512)} %param.22) | copy-start | bytes 4324
  106.9 24.0 %copy-start.12 = (f32[360]{0:T(512)S(1)}, f32[360]{0:T(512)}, u32[]{:S(2)}) copy-start(f32[360]{0:T(512)} %param.23) | copy-start | bytes 4324
  106.9 9.9 %collective-permute-start.8 = (f32[8,72,128]{2,1,0:T(8,128)S(1)}, f32[8,72,128]{2,1,0:T(8,128)S(1)}, u32[]{:S(2)}, u32[]{:S(2)}) collective-permute-start(f32[8,72,128]{2,1,0:T(8,128)S(1)} %shard_map.197.basis_half_ref), channel_id=1, source_target_pairs={{0,2},{1,3},{2,0},{3,1},{4,6},{5,7},{6,4},{7,5},{8,10},{9,11},{10,... | collective-permute-start | bytes 884744 | tf_op jit(solution)/shard_map/ppermute | solution.py:206
  108.7 13.6 %collective-permute-start.10 = (f32[8,72,128]{2,1,0:T(8,128)S(1)}, f32[8,72,128]{2,1,0:T(8,128)S(1)}, u32[]{:S(2)}, u32[]{:S(2)}) collective-permute-start(f32[8,72,128]{2,1,0:T(8,128)S(1)} %shard_map.199.gram_half_ref), channel_id=1, source_target_pairs={{0,2},{1,3},{2,0},{3,1},{4,6},{5,7},{6,4},{7,5},{8,10},{9,11},{10,... | collective-permute-start | bytes 884744 | tf_op jit(solution)/shard_map/ppermute | solution.py:206
  130.8 1.4 %collective-permute-start.11 = (f32[96,384]{1,0:T(8,128)S(1)}, f32[96,384]{1,0:T(8,128)S(1)}, u32[]{:S(2)}, u32[]{:S(2)}) collective-permute-start(f32[96,384]{1,0:T(8,128)S(1)} %get-tuple-element.88), channel_id=1, source_target_pairs={{0,1},{1,0},{2,3},{3,2},{4,5},{5,4},{6,7},{7,6},{8,9},{9,8},{10,11... | collective-permute-start | bytes 442376 | tf_op jit(solution)/shard_map/ppermute | solution.py:203

commit v4 on v3

--- a/solution.py
+++ b/solution.py
@@ -127,6 +127,20 @@
     dims = (((contract[0],), (contract[1],)), ((), ()))
     dot = functools.partial(lax.dot_general, dimension_numbers=dims, preferred_element_type=F32)
     return dot(left[0], right[0]) + (dot(left[0], right[1]) + dot(left[1], right[0]))
+
+
+def thirds_of(value):
+    high = value.astype(BF16)
+    rest = value - high.astype(F32)
+    middle = rest.astype(BF16)
+    return high, middle, (rest - middle.astype(F32)).astype(BF16)
+
+
+def fine_product(left, right):
+    dims = (((1,), (0,)), ((), ()))
+    dot = functools.partial(lax.dot_general, dimension_numbers=dims, preferred_element_type=F32)
+    small = dot(left[0], right[2]) + dot(left[1], right[1]) + dot(left[2], right[0])
+    return dot(left[0], right[0]) + (dot(left[0], right[1]) + dot(left[1], right[0]) + small)
 
 
 def call(kernel, outs, args, specs=None, out_specs=None, scratch=(), aliases=None, grid=()):
@@ -568,10 +582,10 @@
                     jnp.where(first, odd[1], odd[0]),
                 ]
                 basis_ref[k, at, :] = jnp.concatenate(ordered, axis=1)
-        grad = parts_of(grad_ref[...])
+        grad = thirds_of(grad_ref[...])
         hat = jnp.zeros((width, wide), F32)
         for k, mask in enumerate(slot_masks(group_ref, edges_ref)):
-            hat = jnp.where(mask, product(parts_of(basis_ref[k].T), grad), hat)
+            hat = jnp.where(mask, fine_product(thirds_of(basis_ref[k].T), grad), hat)
         hat_ref[...] = hat
 
     basis_full, hat_full = call(
@@ -599,10 +613,10 @@
         second_ref[...] = 0.95 * second_ref[...] + 0.05 * hat_ref[...] * hat_ref[...]
         unpack_columns(came_ref, owned_rows + tile_rows, moment_ref, shards, rows, share)
         masks = slot_masks(group_ref, edges_ref)
-        moment = parts_of(0.9 * moment_ref[...] + 0.1 * grad_ref[...])
+        moment = thirds_of(0.9 * moment_ref[...] + 0.1 * grad_ref[...])
         hat = jnp.zeros((width, wide), F32)
         for k, mask in enumerate(masks):
-            hat = jnp.where(mask, product(parts_of(basis_ref[k].T), moment), hat)
+            hat = jnp.where(mask, fine_product(thirds_of(basis_ref[k].T), moment), hat)
         step = parts_of(adam_direction(hat, second_ref[...]))
         turned = jnp.zeros((width, wide), F32)
         for k, mask in enumerate(masks):

time: 138 us -> 138 us (level)
  waiting for transfers between devices: 67.7 us -> 65.5 us
  Pallas kernels: 33.9 us -> 36 us
    all_to_all x4, waiting for transfers between devices: 29.9 us -> 27.8 us  [exchange(): lax.all_to_all(value, 'shard', split_axis=0, concat_axis=0, tiled=True)]
    pallas_call x14, Pallas kernels: 33.9 us -> 36 us  [call(): pl.pallas_call(kernel, out_shape=shapes, grid=grid, in_specs=[s or vmem f...]
  transfers between devices with their start and end apart: 16 -> 16, of which waited for: 13 -> 13; matrix products, arithmetic and copies ran while one was open for 1% -> 1% of each run, Pallas kernels for 21% -> 23%
where the time goes in v4:
time: 138 us
  waiting for transfers between devices  65.5 us (47%)
  Pallas kernels  36 us (26%)
  starting transfers between devices  29.4 us (21%)
  local copies, waits for them, and re-layouts  4.46 us (3%)
    pallas_call x14, Pallas kernels, call(): pl.pallas_call(kernel, out_shape=shapes, grid=grid, in_specs=[s or vmem f...  36 us
    all_to_all x4, waiting for transfers between devices, exchange(): lax.all_to_all(value, 'shard', split_axis=0, concat_axis=0, tiled=True)  27.8 us
    ppermute x4, waiting for transfers between devices, over_chip(): return lax.ppermute(value, 'tensor', chip_pairs)  20.3 us
    all_to_all x4, starting transfers between devices, exchange(): lax.all_to_all(value, 'shard', split_axis=0, concat_axis=0, tiled=True)  19.6 us
    ppermute x3, waiting for transfers between devices, body(): lax.ppermute(gram_blocks[k], 'shard', [(s, s ^ k) for s in range(shards)])  12.8 us
    ppermute x4, starting transfers between devices, over_chip(): return lax.ppermute(value, 'tensor', chip_pairs)  5.54 us
    ppermute x5, waiting for transfers between devices, over_core(): return lax.ppermute(value, 'tensor', core_pairs)  4.7 us
    unnamed x28, local copies, waits for them, and re-layouts  4.37 us
  transfers between devices with their start and end apart: 16, of which 13 were waited for; matrix products, arithmetic and copies ran while one was open for 1% of the time, Pallas kernels for 23%

profile of v4, /device:TPU:0, one launch (start us, length us, event | category | flops | bytes accessed | tf_op | source)
XLA Modules:
  0.0 137.7 jit_solution(15579506342027904169)
XLA Ops:
  0.6 2.6 %shard_map.188 = f32[8,240,128]{2,1,0:T(8,128)} custom-call(f32[1296,128]{1,0:T(8,128)} %bitcast.19, f32[48,1,960]{2,1,0:T(1,128)} %basis_ref.3), custom_call_target="tpu_custom_call" | custom-call | tf_op jit(solution)/shard_map/pallas_call | solution.py:152
  3.3 7.4 %all-to-all-start = ((f32[8,240,128]{2,1,0:T(8,128)}), f32[8,240,128]{2,1,0:T(8,128)S(1)}, u32[]{:S(2)}, u32[]{:S(2)}) async-start(f32[8,240,128]{2,1,0:T(8,128)} %shard_map.188), calls=%async_computation | async-start | bytes 1966080 | tf_op jit(solution)/shard_map/all_to_all | solution.py:223
  10.7 0.1 reshape.47.owner_ref
  10.8 0.9 copy-done.4
  11.7 1.1 copy-done.5
  12.8 1.1 copy-done.6
  13.9 3.9 %shard_map.189 = (f32[8,408,128]{2,1,0:T(8,128)S(1)}, f32[1296,128]{1,0:T(8,128)}, s32[16]{0:T(128)S(1)}) custom-call(s32[10]{0:T(128)S(1)} %reshape.47.owner_ref, f32[1296,128]{1,0:T(8,128)S(1)} %bitcast.23, f32[1296,128]{1,0:T(8,128)S(1)} %bitcast.24, f32[1296,128]{1,0:T(8,128)S(1)} %bitcast.20, f32[48,1,960]{2,1,0:T(1,128)S(1)} %copy-done.4), custom_call_target="tpu_custom_call" | custom-call | tf_op jit(solution)/shard_map/pallas_call | solution.py:152
  17.8 1.2 copy-done.1
  19.0 16.1 %all-to-all-done.came_ref = f32[8,240,128]{2,1,0:T(8,128)S(1)} async-done(((f32[8,240,128]{2,1,0:T(8,128)}), f32[8,240,128]{2,1,0:T(8,128)S(1)}, u32[]{:S(2)}, u32[]{:S(2)}) %all-to-all-start) | async-done | bytes 983072 | tf_op jit(solution)/shard_map/all_to_all | solution.py:223
  35.1 3.7 %all-to-all-start.1 = ((f32[8,408,128]{2,1,0:T(8,128)}), f32[8,408,128]{2,1,0:T(8,128)S(1)}, u32[]{:S(2)}, u32[]{:S(2)}) async-start(f32[8,408,128]{2,1,0:T(8,128)} %copy-done.1), calls=%async_computation.1 | async-start | bytes 3342336 | tf_op jit(solution)/shard_map/all_to_all | solution.py:223
  38.9 2.3 %shard_map.190 = (f32[384,512]{1,0:T(8,128)S(1)}, f32[8,72,128]{2,1,0:T(8,128)S(1)}, f32[2,8,72,128]{3,2,1,0:T(8,128)S(1)}, f32[2,8,72,128]{3,2,1,0:T(8,128)S(1)}) custom-call(s32[1]{0:T(128)} %bitcast.3.group_ref, s32[1]{0:T(128)} %bitcast.4.rank_ref, s32[24]{0:T(128)S(1)} %copy-done.7, f32[8,240,128]{2,1,0:T(8,128)S(1)} %all-to-all-done.came_ref), custom_call_target="tpu_custom_call" | custom-call | tf_op jit(solution)/shard_map/pallas_call | solution.py:152
  41.2 0.1 collective-permute-start
  41.3 2.0 %collective-permute-done.came_ref = f32[2,8,72,128]{3,2,1,0:T(8,128)S(1)} collective-permute-done((f32[2,8,72,128]{3,2,1,0:T(8,128)S(1)}, f32[2,8,72,128]{3,2,1,0:T(8,128)S(1)}, u32[]{:S(2)}, u32[]{:S(2)}) %collective-permute-start) | collective-permute-done | bytes 589856 | tf_op jit(solution)/shard_map/ppermute | solution.py:217
  43.3 0.1 shard_map.191
  43.3 1.6 %collective-permute-start.1 = (f32[8,72,128]{2,1,0:T(8,128)S(1)}, f32[8,72,128]{2,1,0:T(8,128)S(1)}, u32[]{:S(2)}, u32[]{:S(2)}) collective-permute-start(f32[8,72,128]{2,1,0:T(8,128)S(1)} %get-tuple-element.60), channel_id=1, source_target_pairs={{0,2},{1,3},{2,0},{3,1},{4,6},{5,7},{6,4},{7,5},{8,10},{9,11},{10,... | collective-permute-start | bytes 884744 | tf_op jit(solution)/shard_map/ppermute | solution.py:220
  44.9 7.6 %collective-permute-done.1.came_ref = f32[8,72,128]{2,1,0:T(8,128)S(1)} collective-permute-done((f32[8,72,128]{2,1,0:T(8,128)S(1)}, f32[8,72,128]{2,1,0:T(8,128)S(1)}, u32[]{:S(2)}, u32[]{:S(2)}) %collective-permute-start.1) | collective-permute-done | bytes 294944 | tf_op jit(solution)/shard_map/ppermute | solution.py:220
  52.5 1.6 %collective-permute-start.5 = (f32[8,72,128]{2,1,0:T(8,128)S(1)}, f32[8,72,128]{2,1,0:T(8,128)S(1)}, u32[]{:S(2)}, u32[]{:S(2)}) collective-permute-start(f32[8,72,128]{2,1,0:T(8,128)S(1)} %get-tuple-element.70.own_ref), channel_id=1, source_target_pairs={{0,2},{1,3},{2,0},{3,1},{4,6},{5,7},{6,4},{7,5},{8,10},{9,11},{10,... | collective-permute-start | bytes 884744 | tf_op jit(solution)/shard_map/ppermute | solution.py:220
  54.1 2.0 %collective-permute-start.2 = (f32[2,72,128]{2,1,0:T(8,128)S(1)}, f32[2,72,128]{2,1,0:T(8,128)S(1)}, u32[]{:S(2)}, u32[]{:S(2)}) collective-permute-start(f32[2,72,128]{2,1,0:T(8,128)S(1)} %get-tuple-element.67), channel_id=1, source_target_pairs={{0,4},{4,0},{8,12},{12,8},{16,20},{20,16},{24,28},{28,24},{1,5},{5... | collective-permute-start | bytes 221192 | tf_op jit(solution)/shard_map/ppermute | solution.py:445
  56.0 1.5 %collective-permute-start.3 = (f32[2,72,128]{2,1,0:T(8,128)S(1)}, f32[2,72,128]{2,1,0:T(8,128)S(1)}, u32[]{:S(2)}, u32[]{:S(2)}) collective-permute-start(f32[2,72,128]{2,1,0:T(8,128)S(1)} %get-tuple-element.68), channel_id=1, source_target_pairs={{0,8},{4,12},{8,0},{12,4},{16,24},{20,28},{24,16},{28,20},{1,9},{5... | collective-permute-start | bytes 221192 | tf_op jit(solution)/shard_map/ppermute | solution.py:445
  57.5 2.0 %collective-permute-done.2.refs_1_ = f32[2,72,128]{2,1,0:T(8,128)S(1)} collective-permute-done((f32[2,72,128]{2,1,0:T(8,128)S(1)}, f32[2,72,128]{2,1,0:T(8,128)S(1)}, u32[]{:S(2)}, u32[]{:S(2)}) %collective-permute-start.2) | collective-permute-done | bytes 73760 | tf_op jit(solution)/shard_map/ppermute | solution.py:445
  59.5 10.0 %collective-permute-done.3.refs_2_ = f32[2,72,128]{2,1,0:T(8,128)S(1)} collective-permute-done((f32[2,72,128]{2,1,0:T(8,128)S(1)}, f32[2,72,128]{2,1,0:T(8,128)S(1)}, u32[]{:S(2)}, u32[]{:S(2)}) %collective-permute-start.3) | collective-permute-done | bytes 73760 | tf_op jit(solution)/shard_map/ppermute | solution.py:445
  69.5 0.8 collective-permute-done.4.refs_3_
  70.3 2.9 %shard_map.193 = f32[8,144,128]{2,1,0:T(8,128)} custom-call(s32[1]{0:T(128)} %bitcast.3.group_ref, s32[16]{0:T(128)S(1)} %get-tuple-element.55.table_ref, s32[16]{0:T(128)S(1)} %copy-done.8, f32[48,1,960]{2,1,0:T(1,128)} %gram_ref.1, f32[2,72,128]{2,1,0:T(8,128)S(1)} %get-tuple-element.71.refs_0_, f32[2,72,128]{2,1,0:T(8,128)S(1)} %collective-permute-done.2.refs_1_, ...), custom_call_target="tpu_custom_call" | custom-call | tf_op jit(solution)/shard_map/pallas_call | solution.py:152
  73.3 4.8 %all-to-all-done.1.came_ref = f32[8,408,128]{2,1,0:T(8,128)S(1)} async-done(((f32[8,408,128]{2,1,0:T(8,128)}), f32[8,408,128]{2,1,0:T(8,128)S(1)}, u32[]{:S(2)}, u32[]{:S(2)}) %all-to-all-start.1) | async-done | bytes 1671200 | tf_op jit(solution)/shard_map/all_to_all | solution.py:223
  78.1 4.7 %all-to-all-start.2 = ((f32[8,144,128]{2,1,0:T(8,128)}), f32[8,144,128]{2,1,0:T(8,128)}, u32[]{:S(2)}, u32[]{:S(2)}) async-start(f32[8,144,128]{2,1,0:T(8,128)} %shard_map.193), calls=%async_computation.2 | async-start | bytes 1179648 | tf_op jit(solution)/shard_map/all_to_all | solution.py:223
  82.9 0.1 collective-permute-start.6
  82.9 2.0 %collective-permute-done.6.pair_ref = f32[2,8,72,128]{3,2,1,0:T(8,128)S(1)} collective-permute-done((f32[2,8,72,128]{3,2,1,0:T(8,128)S(1)}, f32[2,8,72,128]{3,2,1,0:T(8,128)S(1)}, u32[]{:S(2)}, u32[]{:S(2)}) %collective-permute-start.6) | collective-permute-done | bytes 589856 | tf_op jit(solution)/shard_map/ppermute | solution.py:217
  84.9 3.5 %shard_map.194 = (f32[2,384,384]{2,1,0:T(8,128)S(1)}, f32[384,512]{1,0:T(8,128)S(1)}) custom-call(s32[1]{0:T(128)} %bitcast.3.group_ref, s32[1]{0:T(128)} %bitcast.4.rank_ref, s32[24]{0:T(128)S(1)} %copy-done.7, f32[8,72,128]{2,1,0:T(8,128)S(1)} %copy-done.3, f32[8,72,128]{2,1,0:T(8,128)S(1)} %collective-permute-done.5.chip_ref, ...), custom_call_target="tpu_custom_call" | custom-call | tf_op jit(solution)/shard_map/pallas_call | solution.py:152
  88.4 6.3 %shard_map.195 = f32[8,336,128]{2,1,0:T(8,128)} custom-call(s32[1]{0:T(128)} %bitcast.3.group_ref, s32[24]{0:T(128)S(1)} %copy-done.7, f32[8,408,128]{2,1,0:T(8,128)S(1)} %all-to-all-done.1.came_ref, f32[384,512]{1,0:T(8,128)S(1)} %get-tuple-element.77.grad_ref, f32[384,512]{1,0:T(8,128)S(1)} %get-tuple-element.79.hat_ref, ...), custom_call_target="tpu_custom_call" | custom-call | tf_op jit(solution)/shard_map/pallas_call | solution.py:152
  94.7 4.3 %all-to-all-done.2.came_ref = f32[8,144,128]{2,1,0:T(8,128)} async-done(((f32[8,144,128]{2,1,0:T(8,128)}), f32[8,144,128]{2,1,0:T(8,128)}, u32[]{:S(2)}, u32[]{:S(2)}) %all-to-all-start.2) | async-done | bytes 589856 | tf_op jit(solution)/shard_map/all_to_all | solution.py:223
  99.0 3.8 %all-to-all-start.3 = ((f32[8,336,128]{2,1,0:T(8,128)}), f32[8,336,128]{2,1,0:T(8,128)S(1)}, u32[]{:S(2)}, u32[]{:S(2)}) async-start(f32[8,336,128]{2,1,0:T(8,128)} %shard_map.195), calls=%async_computation.3 | async-start | bytes 2752512 | tf_op jit(solution)/shard_map/all_to_all | solution.py:223
  102.7 0.7 shard_map.196
  103.4 0.1 collective-permute-start.7
  103.5 2.7 %shard_map.198 = (f32[2,96,384]{2,1,0:T(8,128)}, f32[384,128]{1,0:T(8,128)S(1)}, f32[384,128]{1,0:T(8,128)S(1)}) custom-call(s32[1]{0:T(128)} %bitcast.4.rank_ref, f32[8,144,128]{2,1,0:T(8,128)} %all-to-all-done.2.came_ref), custom_call_target="tpu_custom_call" | custom-call | tf_op jit(solution)/shard_map/pallas_call | solution.py:152
  106.2 0.5 collective-permute-start.9
  106.7 0.2 shard_map.197.basis_half_ref
  106.9 1.6 %collective-permute-start.8 = (f32[8,72,128]{2,1,0:T(8,128)S(1)}, f32[8,72,128]{2,1,0:T(8,128)S(1)}, u32[]{:S(2)}, u32[]{:S(2)}) collective-permute-start(f32[8,72,128]{2,1,0:T(8,128)S(1)} %shard_map.197.basis_half_ref), channel_id=1, source_target_pairs={{0,2},{1,3},{2,0},{3,1},{4,6},{5,7},{6,4},{7,5},{8,10},{9,11},{10,... | collective-permute-start | bytes 884744 | tf_op jit(solution)/shard_map/ppermute | solution.py:220
  108.5 0.2 shard_map.199.gram_half_ref
  108.7 0.9 collective-permute-start.10
  109.5 7.3 %collective-permute-done.8.basis_far_ref = f32[8,72,128]{2,1,0:T(8,128)S(1)} collective-permute-done((f32[8,72,128]{2,1,0:T(8,128)S(1)}, f32[8,72,128]{2,1,0:T(8,128)S(1)}, u32[]{:S(2)}, u32[]{:S(2)}) %collective-permute-start.8) | collective-permute-done | bytes 294944 | tf_op jit(solution)/shard_map/ppermute | solution.py:220
  116.8 5.4 %collective-permute-done.10.gram_far_ref = f32[8,72,128]{2,1,0:T(8,128)S(1)} collective-permute-done((f32[8,72,128]{2,1,0:T(8,128)S(1)}, f32[8,72,128]{2,1,0:T(8,128)S(1)}, u32[]{:S(2)}, u32[]{:S(2)}) %collective-permute-start.10) | collective-permute-done | bytes 294944 | tf_op jit(solution)/shard_map/ppermute | solution.py:220
  122.2 8.6 %shard_map.200 = (f32[96,384]{1,0:T(8,128)S(1)}, f32[96,384]{1,0:T(8,128)S(1)}, f32[1296,128]{1,0:T(8,128)S(1)}) custom-call(s32[1]{0:T(128)} %bitcast.4.rank_ref, f32[8,72,128]{2,1,0:T(8,128)S(1)} %shard_map.197.basis_half_ref, f32[8,72,128]{2,1,0:T(8,128)S(1)} %collective-permute-done.8.basis_far_ref, f32[8,72,128]{2,1,0:T(8,128)S(1)} %shard_map.199.gram_half_ref, ...), custom_call_target="tpu_custom_call" | custom-call | tf_op jit(solution)/shard_map/pallas_call | solution.py:152
  130.8 0.1 collective-permute-start.11
  130.9 0.6 multiply_subtract_fusion
  131.5 0.7 collective-permute-done.11
  132.2 0.7 maximum_select_fusion
  133.0 2.6 %all-to-all-done.3.came_ref = f32[8,336,128]{2,1,0:T(8,128)S(1)} async-done(((f32[8,336,128]{2,1,0:T(8,128)}), f32[8,336,128]{2,1,0:T(8,128)S(1)}, u32[]{:S(2)}, u32[]{:S(2)}) %all-to-all-start.3) | async-done | bytes 1376288 | tf_op jit(solution)/shard_map/all_to_all | solution.py:223
  135.6 2.1 %shard_map.201 = (f32[1296,128]{1,0:T(8,128)}, f32[1296,128]{1,0:T(8,128)}) custom-call(f32[8,336,128]{2,1,0:T(8,128)S(1)} %all-to-all-done.3.came_ref, f32[1296,128]{1,0:T(8,128)S(1)} %get-tuple-element.92.weight_ref), custom_call_target="tpu_custom_call" | custom-call | tf_op jit(solution)/shard_map/pallas_call | solution.py:152
  (30 shorter events, 0.2 us)
Async XLA Ops:
  3.3 7.5 %copy-start.13 = (s32[2,5]{1,0:T(2,128)S(1)}, s32[2,5]{1,0:T(2,128)}, u32[]{:S(2)}) copy-start(s32[2,5]{1,0:T(2,128)} %param.19) | copy-start | bytes 124
  3.3 7.5 %copy-start = (f32[48,1,3456]{2,1,0:T(1,128)S(1)}, f32[48,1,3456]{2,1,0:T(1,128)}, u32[]{:S(2)}) copy-start(f32[48,1,3456]{2,1,0:T(1,128)} %param.13) | copy-start | bytes 1990660
  3.3 31.8 %all-to-all-start = ((f32[8,240,128]{2,1,0:T(8,128)}), f32[8,240,128]{2,1,0:T(8,128)S(1)}, u32[]{:S(2)}, u32[]{:S(2)}) async-start(f32[8,240,128]{2,1,0:T(8,128)} %shard_map.188), calls=%async_computation | async-start | bytes 1966080 | tf_op jit(solution)/shard_map/all_to_all | solution.py:223
  10.8 0.9 copy-start.4
  11.7 1.1 copy-start.5
  12.8 1.1 copy-start.6
  17.8 1.2 copy-start.1
  35.1 3.7 %copy-start.7 = (s32[24]{0:T(128)S(1)}, s32[24]{0:T(128)}, u32[]{:S(2)}) copy-start(s32[24]{0:T(128)} %constant.45.clone.edges_ref) | copy-start | bytes 292
  35.1 43.0 %all-to-all-start.1 = ((f32[8,408,128]{2,1,0:T(8,128)}), f32[8,408,128]{2,1,0:T(8,128)S(1)}, u32[]{:S(2)}, u32[]{:S(2)}) async-start(f32[8,408,128]{2,1,0:T(8,128)} %copy-done.1), calls=%async_computation.1 | async-start | bytes 3342336 | tf_op jit(solution)/shard_map/all_to_all | solution.py:223
  38.9 31.5 %copy-start.8 = (s32[16]{0:T(128)S(1)}, s32[16]{0:T(128)}, u32[]{:S(2)}) copy-start(s32[16]{0:T(128)} %constant.46.clone.slot_ref) | copy-start | bytes 196
  41.2 29.1 %copy-start.2 = (f32[8,72,128]{2,1,0:T(8,128)}, f32[8,72,128]{2,1,0:T(8,128)S(1)}, u32[]{:S(2)}) copy-start(f32[8,72,128]{2,1,0:T(8,128)S(1)} %get-tuple-element.70.own_ref) | copy-start | bytes 884740
  41.2 2.1 %collective-permute-start = (f32[2,8,72,128]{3,2,1,0:T(8,128)S(1)}, f32[2,8,72,128]{3,2,1,0:T(8,128)S(1)}, u32[]{:S(2)}, u32[]{:S(2)}) collective-permute-start(f32[2,8,72,128]{3,2,1,0:T(8,128)S(1)} %get-tuple-element.58), channel_id=1, source_target_pairs={{0,1},{1,0},{2,3},{3,2},{4,5},{5,4},{6,7},{7,6},{8,9},{9,8},{10,11... | collective-permute-start | bytes 1769480 | tf_op jit(solution)/shard_map/ppermute | solution.py:217
  43.3 9.1 %collective-permute-start.1 = (f32[8,72,128]{2,1,0:T(8,128)S(1)}, f32[8,72,128]{2,1,0:T(8,128)S(1)}, u32[]{:S(2)}, u32[]{:S(2)}) collective-permute-start(f32[8,72,128]{2,1,0:T(8,128)S(1)} %get-tuple-element.60), channel_id=1, source_target_pairs={{0,2},{1,3},{2,0},{3,1},{4,6},{5,7},{6,4},{7,5},{8,10},{9,11},{10,... | collective-permute-start | bytes 884744 | tf_op jit(solution)/shard_map/ppermute | solution.py:220
  52.5 17.8 %collective-permute-start.5 = (f32[8,72,128]{2,1,0:T(8,128)S(1)}, f32[8,72,128]{2,1,0:T(8,128)S(1)}, u32[]{:S(2)}, u32[]{:S(2)}) collective-permute-start(f32[8,72,128]{2,1,0:T(8,128)S(1)} %get-tuple-element.70.own_ref), channel_id=1, source_target_pairs={{0,2},{1,3},{2,0},{3,1},{4,6},{5,7},{6,4},{7,5},{8,10},{9,11},{10,... | collective-permute-start | bytes 884744 | tf_op jit(solution)/shard_map/ppermute | solution.py:220
  54.1 5.5 %collective-permute-start.2 = (f32[2,72,128]{2,1,0:T(8,128)S(1)}, f32[2,72,128]{2,1,0:T(8,128)S(1)}, u32[]{:S(2)}, u32[]{:S(2)}) collective-permute-start(f32[2,72,128]{2,1,0:T(8,128)S(1)} %get-tuple-element.67), channel_id=1, source_target_pairs={{0,4},{4,0},{8,12},{12,8},{16,20},{20,16},{24,28},{28,24},{1,5},{5... | collective-permute-start | bytes 221192 | tf_op jit(solution)/shard_map/ppermute | solution.py:445
  56.0 13.5 %collective-permute-start.3 = (f32[2,72,128]{2,1,0:T(8,128)S(1)}, f32[2,72,128]{2,1,0:T(8,128)S(1)}, u32[]{:S(2)}, u32[]{:S(2)}) collective-permute-start(f32[2,72,128]{2,1,0:T(8,128)S(1)} %get-tuple-element.68), channel_id=1, source_target_pairs={{0,8},{4,12},{8,0},{12,4},{16,24},{20,28},{24,16},{28,20},{1,9},{5... | collective-permute-start | bytes 221192 | tf_op jit(solution)/shard_map/ppermute | solution.py:445
  57.5 12.8 %collective-permute-start.4 = (f32[2,72,128]{2,1,0:T(8,128)S(1)}, f32[2,72,128]{2,1,0:T(8,128)S(1)}, u32[]{:S(2)}, u32[]{:S(2)}) collective-permute-start(f32[2,72,128]{2,1,0:T(8,128)S(1)} %get-tuple-element.69), channel_id=1, source_target_pairs={{0,12},{4,8},{8,4},{12,0},{16,28},{20,24},{24,20},{28,16},{1,13},{... | collective-permute-start | bytes 221192 | tf_op jit(solution)/shard_map/ppermute | solution.py:445
  73.3 9.5 %copy-start.3 = (f32[8,72,128]{2,1,0:T(8,128)S(1)}, f32[8,72,128]{2,1,0:T(8,128)}, u32[]{:S(2)}) copy-start(f32[8,72,128]{2,1,0:T(8,128)} %copy-done.2) | copy-start | bytes 884740
  78.1 20.9 %all-to-all-start.2 = ((f32[8,144,128]{2,1,0:T(8,128)}), f32[8,144,128]{2,1,0:T(8,128)}, u32[]{:S(2)}, u32[]{:S(2)}) async-start(f32[8,144,128]{2,1,0:T(8,128)} %shard_map.193), calls=%async_computation.2 | async-start | bytes 1179648 | tf_op jit(solution)/shard_map/all_to_all | solution.py:223
  82.9 2.1 %collective-permute-start.6 = (f32[2,8,72,128]{3,2,1,0:T(8,128)S(1)}, f32[2,8,72,128]{3,2,1,0:T(8,128)S(1)}, u32[]{:S(2)}, u32[]{:S(2)}) collective-permute-start(f32[2,8,72,128]{3,2,1,0:T(8,128)S(1)} %pad_maximum_fusion), channel_id=1, source_target_pairs={{0,1},{1,0},{2,3},{3,2},{4,5},{5,4},{6,7},{7,6},{8,9},{9,8},{10,11... | collective-permute-start | bytes 1769480 | tf_op jit(solution)/shard_map/ppermute | solution.py:217
  99.0 36.6 %all-to-all-start.3 = ((f32[8,336,128]{2,1,0:T(8,128)}), f32[8,336,128]{2,1,0:T(8,128)S(1)}, u32[]{:S(2)}, u32[]{:S(2)}) async-start(f32[8,336,128]{2,1,0:T(8,128)} %shard_map.195), calls=%async_computation.3 | async-start | bytes 2752512 | tf_op jit(solution)/shard_map/all_to_all | solution.py:223
  103.4 3.3 %collective-permute-start.7 = (f32[384,128]{1,0:T(8,128)S(1)}, f32[384,128]{1,0:T(8,128)S(1)}, u32[]{:S(2)}, u32[]{:S(2)}) collective-permute-start(f32[384,128]{1,0:T(8,128)S(1)} %get-tuple-element.83), channel_id=1, source_target_pairs={{0,1},{1,0},{2,3},{3,2},{4,5},{5,4},{6,7},{7,6},{8,9},{9,8},{10,11... | collective-permute-start | bytes 589832 | tf_op jit(solution)/shard_map/ppermute | solution.py:217
  106.2 2.3 %collective-permute-start.9 = (f32[384,128]{1,0:T(8,128)S(1)}, f32[384,128]{1,0:T(8,128)S(1)}, u32[]{:S(2)}, u32[]{:S(2)}) collective-permute-start(f32[384,128]{1,0:T(8,128)S(1)} %get-tuple-element.86), channel_id=1, source_target_pairs={{0,1},{1,0},{2,3},{3,2},{4,5},{5,4},{6,7},{7,6},{8,9},{9,8},{10,11... | collective-permute-start | bytes 589832 | tf_op jit(solution)/shard_map/ppermute | solution.py:217
  106.9 24.0 %copy-start.9 = (f32[360]{0:T(512)S(1)}, f32[360]{0:T(512)}, u32[]{:S(2)}) copy-start(f32[360]{0:T(512)} %param.21) | copy-start | bytes 4324
  106.9 24.0 %copy-start.10 = (f32[360]{0:T(512)S(1)}, f32[360]{0:T(512)}, u32[]{:S(2)}) copy-start(f32[360]{0:T(512)} %param.20) | copy-start | bytes 4324
  106.9 24.0 %copy-start.11 = (f32[360]{0:T(512)S(1)}, f32[360]{0:T(512)}, u32[]{:S(2)}) copy-start(f32[360]{0:T(512)} %param.22) | copy-start | bytes 4324
  106.9 24.0 %copy-start.12 = (f32[360]{0:T(512)S(1)}, f32[360]{0:T(512)}, u32[]{:S(2)}) copy-start(f32[360]{0:T(512)} %param.23) | copy-start | bytes 4324
  106.9 9.9 %collective-permute-start.8 = (f32[8,72,128]{2,1,0:T(8,128)S(1)}, f32[8,72,128]{2,1,0:T(8,128)S(1)}, u32[]{:S(2)}, u32[]{:S(2)}) collective-permute-start(f32[8,72,128]{2,1,0:T(8,128)S(1)} %shard_map.197.basis_half_ref), channel_id=1, source_target_pairs={{0,2},{1,3},{2,0},{3,1},{4,6},{5,7},{6,4},{7,5},{8,10},{9,11},{10,... | collective-permute-start | bytes 884744 | tf_op jit(solution)/shard_map/ppermute | solution.py:220
  108.7 13.6 %collective-permute-start.10 = (f32[8,72,128]{2,1,0:T(8,128)S(1)}, f32[8,72,128]{2,1,0:T(8,128)S(1)}, u32[]{:S(2)}, u32[]{:S(2)}) collective-permute-start(f32[8,72,128]{2,1,0:T(8,128)S(1)} %shard_map.199.gram_half_ref), channel_id=1, source_target_pairs={{0,2},{1,3},{2,0},{3,1},{4,6},{5,7},{6,4},{7,5},{8,10},{9,11},{10,... | collective-permute-start | bytes 884744 | tf_op jit(solution)/shard_map/ppermute | solution.py:220
  130.8 1.4 %collective-permute-start.11 = (f32[96,384]{1,0:T(8,128)S(1)}, f32[96,384]{1,0:T(8,128)S(1)}, u32[]{:S(2)}, u32[]{:S(2)}) collective-permute-start(f32[96,384]{1,0:T(8,128)S(1)} %get-tuple-element.88), channel_id=1, source_target_pairs={{0,1},{1,0},{2,3},{3,2},{4,5},{5,4},{6,7},{7,6},{8,9},{9,8},{10,11... | collective-permute-start | bytes 442376 | tf_op jit(solution)/shard_map/ppermute | solution.py:217

commit v5 on v4

--- a/solution.py
+++ b/solution.py
@@ -157,7 +157,7 @@
         out_specs=out_specs or [vmem] * len(shapes),
         scratch_shapes=list(scratch),
         input_output_aliases=aliases or {},
-        compiler_params=pltpu.CompilerParams(vmem_limit_bytes=32 * 2**20),
+        compiler_params=pltpu.CompilerParams(vmem_limit_bytes=16 * 2**20),
     )(*args)
     return result[0] if single else result
 
@@ -284,29 +284,42 @@
 
 
     def pack_gradient(grad_ref, basis_ref, out_ref, line_ref, dense_ref, near_ref, sems):
-        fetch_basis = pltpu.make_async_copy(basis_ref, near_ref, sems.at[0])
-        fetch_basis.start()
-        fetch = pltpu.make_async_copy(grad_ref, dense_ref, sems.at[1])
-        fetch.start()
-        fetch_basis.wait()
-        basis = near_ref[:, 0, :]
-        for group in range(shards):
-            held = [
-                basis[:, matrix * columns : (matrix + 1) * columns]
-                for matrix in slot_matrix[group]
-            ]
-            held += [jnp.zeros((rows, columns), F32)] * (slots - len(held))
-            store_block(out_ref, group, 0, jnp.concatenate(held, axis=1), rows, strip)
-        fetch.wait()
-        send_tiles(dense_ref, line_ref, out_ref, strip_rows)
+        step = pl.program_id(0)
+
+        @pl.when(step == 0)
+        def _():
+            fetch_basis = pltpu.make_async_copy(basis_ref, near_ref, sems.at[0])
+            fetch_basis.start()
+            fetch = pltpu.make_async_copy(grad_ref, dense_ref, sems.at[1])
+            fetch.start()
+            fetch_basis.wait()
+            fetch.wait()
+            open_line(dense_ref, line_ref)
+
+        for part in range(2):
+
+            @pl.when(step == part)
+            def _():
+                basis = near_ref[:, 0, :]
+                for place in range(shards // 2):
+                    group = part * (shards // 2) + place
+                    held = [
+                        basis[:, matrix * columns : (matrix + 1) * columns]
+                        for matrix in slot_matrix[group]
+                    ]
+                    held += [jnp.zeros((rows, columns), F32)] * (slots - len(held))
+                    store_block(out_ref, place, 0, jnp.concatenate(held, axis=1), rows, strip)
+                    block = gather_line(line_ref, group)
+                    store_block(out_ref, place, strip_rows, block, rows, share)
 
     grad_dense = gradient.reshape(dense)
-    basis_hbm = in_hbm(left_basis)
     send_one = call(
         pack_gradient,
         (shards, strip_rows + tile_rows, LANES),
-        (in_hbm(grad_dense), basis_hbm),
+        (in_hbm(grad_dense), in_hbm(left_basis)),
         specs=[HBM, HBM],
+        out_specs=[pl.BlockSpec((shards // 2, strip_rows + tile_rows, LANES), lambda i: (i, 0, 0))],
+        grid=(2,),
         scratch=[
             line_scratch,
             pltpu.VMEM(dense, F32),
@@ -448,7 +461,8 @@
 
 
     strips_chip = over_chip(strips_own)
-    *gram_blocks, strips_chip = together((*gram_blocks, strips_chip))
+    *late, strips_chip = together((*gram_blocks[half_groups // 2 :], strips_chip))
+    gram_blocks = gram_blocks[: half_groups // 2] + late
 
 
     def split_owned(rank_ref, came_ref, *refs):
@@ -499,26 +513,38 @@
         return *strips, half, over_chip(half)
 
 
-    def new_grams(group_ref, table_ref, slot_ref, gram_ref, *refs):
-        came, (out_ref, stage_ref, near_ref, sem) = refs[:half_groups], refs[half_groups:]
-        fetch = pltpu.make_async_copy(gram_ref, near_ref, sem)
-        fetch.start()
-        group = group_ref[0]
-        half = group // half_groups
-        stage_ref[...] = jnp.zeros_like(stage_ref)
+    def add_blocks(group_ref, slot_ref, came, first, stage_ref):
         for k, came_ref in enumerate(came):
             for j in range(2):
                 block = load_block(came_ref, j, 0, rows, strip)
                 for m in range(slots):
-                    matrix = slot_ref[(group ^ k) * slots + m]
+                    matrix = slot_ref[(group_ref[0] ^ (first + k)) * slots + m]
                     at = jnp.where(matrix >= 0, matrix, matrix_total)
                     part = block[:, m * columns : (m + 1) * columns]
                     stage_ref[j, at] = stage_ref[j, at] + 0.05 * part
-        fetch.wait()
-        old = 0.95 * near_ref[:, 0, :]
+
+    def early_grams(group_ref, slot_ref, gram_ref, *refs):
+        came, stage_ref = refs[:-1], refs[-1]
+        half = group_ref[0] // half_groups
+        stage_ref[...] = jnp.zeros_like(stage_ref)
+        old = 0.95 * gram_ref[:, 0, :]
         for matrix in range(matrix_total):
-            own = old[:, matrix * columns : (matrix + 1) * columns]
-            stage_ref[half, matrix] = stage_ref[half, matrix] + own
+            stage_ref[half, matrix] = old[:, matrix * columns : (matrix + 1) * columns]
+        add_blocks(group_ref, slot_ref, came, 0, stage_ref)
+
+    early_blocks = half_groups // 2
+    stage_shape = (2, matrix_total + 1, rows, columns)
+    early_stage = call(
+        early_grams,
+        stage_shape,
+        (group_arg, slot_table, left_gram, *gram_blocks[:early_blocks]),
+        specs=[SMEM, SMEM] + [None] * (1 + early_blocks),
+    )
+
+    def new_grams(group_ref, table_ref, slot_ref, *refs):
+        early_ref, *came, out_ref, stage_ref = refs
+        stage_ref[...] = early_ref[...]
+        add_blocks(group_ref, slot_ref, came, early_blocks, stage_ref)
         for dest in range(shards):
             for j in range(2):
                 held = []
@@ -532,19 +558,9 @@
     send_four = call(
         new_grams,
         (shards, 2 * owned_rows, LANES),
-        (
-            group_arg,
-            owned_table,
-            slot_table,
-            in_hbm(left_gram),
-            *gram_blocks,
-        ),
-        specs=[SMEM, SMEM, SMEM, HBM] + [None] * half_groups,
-        scratch=[
-            pltpu.VMEM((2, matrix_total + 1, rows, columns), F32),
-            pltpu.VMEM(left_gram.shape, F32),
-            pltpu.SemaphoreType.DMA(()),
-        ],
+        (group_arg, owned_table, slot_table, early_stage, *gram_blocks[early_blocks:]),
+        specs=[SMEM, SMEM, SMEM] + [None] * (1 + half_groups - early_blocks),
+        scratch=[pltpu.VMEM(stage_shape, F32)],
     )
     send_four = in_hbm(send_four)
     came_two, send_four = together((came_two, send_four))
@@ -696,24 +712,40 @@
     came_five, pair_out, gram_out, first_out = together((came_five, pair_out, gram_out, first_out))
 
 
-    def line_from(came_ref, base, line_ref):
+    steps = 2 if rows % 16 == 0 else 1
+    step_rows = rows // steps
+    step_dense = (step_rows * line_tiles, LANES)
+
+    def line_from(came_ref, base, part, line_ref, ref):
         for group in range(shards):
             block = load_block(came_ref, group, base, rows, share)
+            block = block[part * step_rows : (part + 1) * step_rows]
             offset = 0
             for _, at, length in groups[group]:
                 line_ref[:, at : at + length] = block[:, offset : offset + length]
                 offset += length
+        for j in range(line_tiles):
+            ref[pl.ds(j, step_rows, stride=line_tiles), :] = line_ref[:, j * LANES : (j + 1) * LANES]
 
     def take_back(came_ref, weight_ref, weight_out_ref, second_out_ref, line_ref):
-        line_from(came_ref, 0, line_ref)
-        close_line(line_ref, weight_out_ref)
-        old = weight_ref[...]
-        weight_out_ref[...] = old - 0.01 * (weight_out_ref[...] + 0.1 * old)
-        line_from(came_ref, tile_rows, line_ref)
-        close_line(line_ref, second_out_ref)
-
+        for part in range(steps):
+
+            @pl.when(pl.program_id(0) == part)
+            def _():
+                line_from(came_ref, 0, part, line_ref, weight_out_ref)
+                old = weight_ref[...]
+                weight_out_ref[...] = old - 0.01 * (weight_out_ref[...] + 0.1 * old)
+                line_from(came_ref, tile_rows, part, line_ref, second_out_ref)
+
+    part_spec = pl.BlockSpec(step_dense, lambda i: (i, 0))
     weight_out, second_out = call(
-        take_back, [dense, dense], (came_five, weight_near), scratch=[line_scratch]
+        take_back,
+        [dense, dense],
+        (came_five, weight_near),
+        specs=[None, part_spec],
+        out_specs=[part_spec, part_spec],
+        grid=(steps,),
+        scratch=[pltpu.VMEM((step_rows, line), F32)],
     )
 
     bias_first_new = 0.9 * bias_first + 0.1 * bias_gradient

time: 138 us -> 138 us (level)
    pallas_call x14 -> x15, Pallas kernels: 36 us -> 35.7 us  [call(): pl.pallas_call(kernel, out_shape=shapes, grid=grid, in_specs=[s or vmem f...]
    unnamed x28 -> x30, local copies, waits for them, and re-layouts: 4.37 us -> 4.37 us
where the time goes in v5:
time: 138 us
  waiting for transfers between devices  65.7 us (48%)
  Pallas kernels  35.7 us (26%)
  starting transfers between devices  29.4 us (21%)
  local copies, waits for them, and re-layouts  4.45 us (3%)
    pallas_call x15, Pallas kernels, call(): pl.pallas_call(kernel, out_shape=shapes, grid=grid, in_specs=[s or vmem f...  35.7 us
    all_to_all x4, waiting for transfers between devices, exchange(): lax.all_to_all(value, 'shard', split_axis=0, concat_axis=0, tiled=True)  29 us
    ppermute x4, waiting for transfers between devices, over_chip(): return lax.ppermute(value, 'tensor', chip_pairs)  20.3 us
    all_to_all x4, starting transfers between devices, exchange(): lax.all_to_all(value, 'shard', split_axis=0, concat_axis=0, tiled=True)  19.6 us
    ppermute x3, waiting for transfers between devices, body(): lax.ppermute(gram_blocks[k], 'shard', [(s, s ^ k) for s in range(shards)])  11.8 us
    ppermute x4, starting transfers between devices, over_chip(): return lax.ppermute(value, 'tensor', chip_pairs)  5.54 us
    ppermute x5, waiting for transfers between devices, over_core(): return lax.ppermute(value, 'tensor', core_pairs)  4.7 us
    unnamed x30, local copies, waits for them, and re-layouts  4.37 us
  transfers between devices with their start and end apart: 16, of which 13 were waited for; matrix products, arithmetic and copies ran while one was open for 1% of the time, Pallas kernels for 23%

profile of v5, /device:TPU:0, one launch (start us, length us, event | category | flops | bytes accessed | tf_op | source)
XLA Modules:
  0.0 137.6 jit_solution(3250271351227195496)
XLA Ops:
  0.6 2.7 %shard_map.188 = f32[8,240,128]{2,1,0:T(8,128)} custom-call(f32[1296,128]{1,0:T(8,128)} %bitcast.19, f32[48,1,960]{2,1,0:T(1,128)} %basis_ref.3), custom_call_target="tpu_custom_call" | custom-call | tf_op jit(solution)/shard_map/pallas_call | solution.py:152
  3.3 7.4 %all-to-all-start = ((f32[8,240,128]{2,1,0:T(8,128)}), f32[8,240,128]{2,1,0:T(8,128)S(1)}, u32[]{:S(2)}, u32[]{:S(2)}) async-start(f32[8,240,128]{2,1,0:T(8,128)} %shard_map.188), calls=%async_computation | async-start | bytes 1966080 | tf_op jit(solution)/shard_map/all_to_all | solution.py:223
  10.8 0.1 reshape.47.owner_ref
  10.8 0.9 copy-done.4
  11.8 1.1 copy-done.5
  12.9 1.1 copy-done.6
  14.0 3.9 %shard_map.189 = (f32[8,408,128]{2,1,0:T(8,128)S(1)}, f32[1296,128]{1,0:T(8,128)}, s32[16]{0:T(128)S(1)}) custom-call(s32[10]{0:T(128)S(1)} %reshape.47.owner_ref, f32[1296,128]{1,0:T(8,128)S(1)} %bitcast.23, f32[1296,128]{1,0:T(8,128)S(1)} %bitcast.24, f32[1296,128]{1,0:T(8,128)S(1)} %bitcast.20, f32[48,1,960]{2,1,0:T(1,128)S(1)} %copy-done.4), custom_call_target="tpu_custom_call" | custom-call | tf_op jit(solution)/shard_map/pallas_call | solution.py:152
  17.9 1.2 copy-done.1
  19.1 16.1 %all-to-all-done.came_ref = f32[8,240,128]{2,1,0:T(8,128)S(1)} async-done(((f32[8,240,128]{2,1,0:T(8,128)}), f32[8,240,128]{2,1,0:T(8,128)S(1)}, u32[]{:S(2)}, u32[]{:S(2)}) %all-to-all-start) | async-done | bytes 983072 | tf_op jit(solution)/shard_map/all_to_all | solution.py:223
  35.1 3.7 %all-to-all-start.1 = ((f32[8,408,128]{2,1,0:T(8,128)}), f32[8,408,128]{2,1,0:T(8,128)S(1)}, u32[]{:S(2)}, u32[]{:S(2)}) async-start(f32[8,408,128]{2,1,0:T(8,128)} %copy-done.1), calls=%async_computation.1 | async-start | bytes 3342336 | tf_op jit(solution)/shard_map/all_to_all | solution.py:223
  38.9 2.3 %shard_map.190 = (f32[384,512]{1,0:T(8,128)S(1)}, f32[8,72,128]{2,1,0:T(8,128)S(1)}, f32[2,8,72,128]{3,2,1,0:T(8,128)S(1)}, f32[2,8,72,128]{3,2,1,0:T(8,128)S(1)}) custom-call(s32[1]{0:T(128)} %bitcast.3.group_ref, s32[1]{0:T(128)} %bitcast.4.rank_ref, s32[24]{0:T(128)S(1)} %copy-done.8, f32[8,240,128]{2,1,0:T(8,128)S(1)} %all-to-all-done.came_ref), custom_call_target="tpu_custom_call" | custom-call | tf_op jit(solution)/shard_map/pallas_call | solution.py:152
  41.2 0.1 collective-permute-start
  41.3 2.0 %collective-permute-done.came_ref = f32[2,8,72,128]{3,2,1,0:T(8,128)S(1)} collective-permute-done((f32[2,8,72,128]{3,2,1,0:T(8,128)S(1)}, f32[2,8,72,128]{3,2,1,0:T(8,128)S(1)}, u32[]{:S(2)}, u32[]{:S(2)}) %collective-permute-start) | collective-permute-done | bytes 589856 | tf_op jit(solution)/shard_map/ppermute | solution.py:217
  43.3 0.1 shard_map.191
  43.4 1.6 %collective-permute-start.1 = (f32[8,72,128]{2,1,0:T(8,128)S(1)}, f32[8,72,128]{2,1,0:T(8,128)S(1)}, u32[]{:S(2)}, u32[]{:S(2)}) collective-permute-start(f32[8,72,128]{2,1,0:T(8,128)S(1)} %get-tuple-element.58), channel_id=1, source_target_pairs={{0,2},{1,3},{2,0},{3,1},{4,6},{5,7},{6,4},{7,5},{8,10},{9,11},{10,... | collective-permute-start | bytes 884744 | tf_op jit(solution)/shard_map/ppermute | solution.py:220
  45.0 7.6 %collective-permute-done.1.came_ref = f32[8,72,128]{2,1,0:T(8,128)S(1)} collective-permute-done((f32[8,72,128]{2,1,0:T(8,128)S(1)}, f32[8,72,128]{2,1,0:T(8,128)S(1)}, u32[]{:S(2)}, u32[]{:S(2)}) %collective-permute-start.1) | collective-permute-done | bytes 294944 | tf_op jit(solution)/shard_map/ppermute | solution.py:220
  52.5 1.6 %collective-permute-start.5 = (f32[8,72,128]{2,1,0:T(8,128)S(1)}, f32[8,72,128]{2,1,0:T(8,128)S(1)}, u32[]{:S(2)}, u32[]{:S(2)}) collective-permute-start(f32[8,72,128]{2,1,0:T(8,128)S(1)} %get-tuple-element.68.own_ref), channel_id=1, source_target_pairs={{0,2},{1,3},{2,0},{3,1},{4,6},{5,7},{6,4},{7,5},{8,10},{9,11},{10,... | collective-permute-start | bytes 884744 | tf_op jit(solution)/shard_map/ppermute | solution.py:220
  54.1 2.0 %collective-permute-start.2 = (f32[2,72,128]{2,1,0:T(8,128)S(1)}, f32[2,72,128]{2,1,0:T(8,128)S(1)}, u32[]{:S(2)}, u32[]{:S(2)}) collective-permute-start(f32[2,72,128]{2,1,0:T(8,128)S(1)} %get-tuple-element.65), channel_id=1, source_target_pairs={{0,4},{4,0},{8,12},{12,8},{16,20},{20,16},{24,28},{28,24},{1,5},{5... | collective-permute-start | bytes 221192 | tf_op jit(solution)/shard_map/ppermute | solution.py:458
  56.1 1.5 %collective-permute-start.3 = (f32[2,72,128]{2,1,0:T(8,128)S(1)}, f32[2,72,128]{2,1,0:T(8,128)S(1)}, u32[]{:S(2)}, u32[]{:S(2)}) collective-permute-start(f32[2,72,128]{2,1,0:T(8,128)S(1)} %get-tuple-element.66), channel_id=1, source_target_pairs={{0,8},{4,12},{8,0},{12,4},{16,24},{20,28},{24,16},{28,20},{1,9},{5... | collective-permute-start | bytes 221192 | tf_op jit(solution)/shard_map/ppermute | solution.py:458
  57.6 2.0 %collective-permute-done.2.refs_1_ = f32[2,72,128]{2,1,0:T(8,128)S(1)} collective-permute-done((f32[2,72,128]{2,1,0:T(8,128)S(1)}, f32[2,72,128]{2,1,0:T(8,128)S(1)}, u32[]{:S(2)}, u32[]{:S(2)}) %collective-permute-start.2) | collective-permute-done | bytes 73760 | tf_op jit(solution)/shard_map/ppermute | solution.py:458
  59.6 0.9 shard_map.193.refs_0_
  60.5 9.0 %collective-permute-done.3.refs_1_ = f32[2,72,128]{2,1,0:T(8,128)S(1)} collective-permute-done((f32[2,72,128]{2,1,0:T(8,128)S(1)}, f32[2,72,128]{2,1,0:T(8,128)S(1)}, u32[]{:S(2)}, u32[]{:S(2)}) %collective-permute-start.3) | collective-permute-done | bytes 73760 | tf_op jit(solution)/shard_map/ppermute | solution.py:458
  69.5 0.8 collective-permute-done.4.refs_2_
  70.3 1.8 %shard_map.194 = f32[8,144,128]{2,1,0:T(8,128)} custom-call(s32[1]{0:T(128)} %bitcast.3.group_ref, s32[16]{0:T(128)S(1)} %get-tuple-element.53.table_ref, s32[16]{0:T(128)S(1)} %copy-done.9, f32[2,11,48,96]{3,2,1,0:T(8,128)S(1)} %shard_map.193.refs_0_, f32[2,72,128]{2,1,0:T(8,128)S(1)} %collective-permute-done.3.refs_1_, ...), custom_call_target="tpu_custom_call" | custom-call | tf_op jit(solution)/shard_map/pallas_call | solution.py:152
  72.1 6.0 %all-to-all-done.1.came_ref = f32[8,408,128]{2,1,0:T(8,128)S(1)} async-done(((f32[8,408,128]{2,1,0:T(8,128)}), f32[8,408,128]{2,1,0:T(8,128)S(1)}, u32[]{:S(2)}, u32[]{:S(2)}) %all-to-all-start.1) | async-done | bytes 1671200 | tf_op jit(solution)/shard_map/all_to_all | solution.py:223
  78.1 4.7 %all-to-all-start.2 = ((f32[8,144,128]{2,1,0:T(8,128)}), f32[8,144,128]{2,1,0:T(8,128)}, u32[]{:S(2)}, u32[]{:S(2)}) async-start(f32[8,144,128]{2,1,0:T(8,128)} %shard_map.194), calls=%async_computation.2 | async-start | bytes 1179648 | tf_op jit(solution)/shard_map/all_to_all | solution.py:223
  82.9 0.1 collective-permute-start.6
  83.0 2.0 %collective-permute-done.6.pair_ref = f32[2,8,72,128]{3,2,1,0:T(8,128)S(1)} collective-permute-done((f32[2,8,72,128]{3,2,1,0:T(8,128)S(1)}, f32[2,8,72,128]{3,2,1,0:T(8,128)S(1)}, u32[]{:S(2)}, u32[]{:S(2)}) %collective-permute-start.6) | collective-permute-done | bytes 589856 | tf_op jit(solution)/shard_map/ppermute | solution.py:217
  85.0 3.5 %shard_map.195 = (f32[2,384,384]{2,1,0:T(8,128)S(1)}, f32[384,512]{1,0:T(8,128)S(1)}) custom-call(s32[1]{0:T(128)} %bitcast.3.group_ref, s32[1]{0:T(128)} %bitcast.4.rank_ref, s32[24]{0:T(128)S(1)} %copy-done.8, f32[8,72,128]{2,1,0:T(8,128)S(1)} %copy-done.3, f32[8,72,128]{2,1,0:T(8,128)S(1)} %collective-permute-done.5.chip_ref, ...), custom_call_target="tpu_custom_call" | custom-call | tf_op jit(solution)/shard_map/pallas_call | solution.py:152
  88.5 6.3 %shard_map.196 = f32[8,336,128]{2,1,0:T(8,128)} custom-call(s32[1]{0:T(128)} %bitcast.3.group_ref, s32[24]{0:T(128)S(1)} %copy-done.8, f32[8,408,128]{2,1,0:T(8,128)S(1)} %all-to-all-done.1.came_ref, f32[384,512]{1,0:T(8,128)S(1)} %get-tuple-element.73.grad_ref, f32[384,512]{1,0:T(8,128)S(1)} %get-tuple-element.75.hat_ref, ...), custom_call_target="tpu_custom_call" | custom-call | tf_op jit(solution)/shard_map/pallas_call | solution.py:152
  94.8 4.3 %all-to-all-done.2.came_ref = f32[8,144,128]{2,1,0:T(8,128)} async-done(((f32[8,144,128]{2,1,0:T(8,128)}), f32[8,144,128]{2,1,0:T(8,128)}, u32[]{:S(2)}, u32[]{:S(2)}) %all-to-all-start.2) | async-done | bytes 589856 | tf_op jit(solution)/shard_map/all_to_all | solution.py:223
  99.0 3.8 %all-to-all-start.3 = ((f32[8,336,128]{2,1,0:T(8,128)}), f32[8,336,128]{2,1,0:T(8,128)S(1)}, u32[]{:S(2)}, u32[]{:S(2)}) async-start(f32[8,336,128]{2,1,0:T(8,128)} %shard_map.196), calls=%async_computation.3 | async-start | bytes 2752512 | tf_op jit(solution)/shard_map/all_to_all | solution.py:223
  102.8 0.7 shard_map.197
  103.6 2.7 %shard_map.199 = (f32[2,96,384]{2,1,0:T(8,128)}, f32[384,128]{1,0:T(8,128)S(1)}, f32[384,128]{1,0:T(8,128)S(1)}) custom-call(s32[1]{0:T(128)} %bitcast.4.rank_ref, f32[8,144,128]{2,1,0:T(8,128)} %all-to-all-done.2.came_ref), custom_call_target="tpu_custom_call" | custom-call | tf_op jit(solution)/shard_map/pallas_call | solution.py:152
  106.2 0.5 collective-permute-start.9
  106.7 0.2 shard_map.198.basis_half_ref
  107.0 1.6 %collective-permute-start.8 = (f32[8,72,128]{2,1,0:T(8,128)S(1)}, f32[8,72,128]{2,1,0:T(8,128)S(1)}, u32[]{:S(2)}, u32[]{:S(2)}) collective-permute-start(f32[8,72,128]{2,1,0:T(8,128)S(1)} %shard_map.198.basis_half_ref), channel_id=1, source_target_pairs={{0,2},{1,3},{2,0},{3,1},{4,6},{5,7},{6,4},{7,5},{8,10},{9,11},{10,... | collective-permute-start | bytes 884744 | tf_op jit(solution)/shard_map/ppermute | solution.py:220
  108.5 0.2 shard_map.200.gram_half_ref
  108.7 0.9 collective-permute-start.10
  109.6 7.3 %collective-permute-done.8.basis_far_ref = f32[8,72,128]{2,1,0:T(8,128)S(1)} collective-permute-done((f32[8,72,128]{2,1,0:T(8,128)S(1)}, f32[8,72,128]{2,1,0:T(8,128)S(1)}, u32[]{:S(2)}, u32[]{:S(2)}) %collective-permute-start.8) | collective-permute-done | bytes 294944 | tf_op jit(solution)/shard_map/ppermute | solution.py:220
  116.9 5.4 %collective-permute-done.10.gram_far_ref = f32[8,72,128]{2,1,0:T(8,128)S(1)} collective-permute-done((f32[8,72,128]{2,1,0:T(8,128)S(1)}, f32[8,72,128]{2,1,0:T(8,128)S(1)}, u32[]{:S(2)}, u32[]{:S(2)}) %collective-permute-start.10) | collective-permute-done | bytes 294944 | tf_op jit(solution)/shard_map/ppermute | solution.py:220
  122.3 8.6 %shard_map.201 = (f32[96,384]{1,0:T(8,128)S(1)}, f32[96,384]{1,0:T(8,128)S(1)}, f32[1296,128]{1,0:T(8,128)S(1)}) custom-call(s32[1]{0:T(128)} %bitcast.4.rank_ref, f32[8,72,128]{2,1,0:T(8,128)S(1)} %shard_map.198.basis_half_ref, f32[8,72,128]{2,1,0:T(8,128)S(1)} %collective-permute-done.8.basis_far_ref, f32[8,72,128]{2,1,0:T(8,128)S(1)} %shard_map.200.gram_half_ref, ...), custom_call_target="tpu_custom_call" | custom-call | tf_op jit(solution)/shard_map/pallas_call | solution.py:152
  130.8 0.1 collective-permute-start.11
  130.9 0.6 multiply_subtract_fusion
  131.6 0.7 collective-permute-done.11
  132.3 0.7 maximum_select_fusion
  133.0 2.6 %all-to-all-done.3.came_ref = f32[8,336,128]{2,1,0:T(8,128)S(1)} async-done(((f32[8,336,128]{2,1,0:T(8,128)}), f32[8,336,128]{2,1,0:T(8,128)S(1)}, u32[]{:S(2)}, u32[]{:S(2)}) %all-to-all-start.3) | async-done | bytes 1376288 | tf_op jit(solution)/shard_map/all_to_all | solution.py:223
  135.6 1.9 %shard_map.202 = (f32[1296,128]{1,0:T(8,128)}, f32[1296,128]{1,0:T(8,128)}) custom-call(f32[8,336,128]{2,1,0:T(8,128)S(1)} %all-to-all-done.3.came_ref, f32[1296,128]{1,0:T(8,128)S(1)} %get-tuple-element.88.weight_ref), custom_call_target="tpu_custom_call" | custom-call | tf_op jit(solution)/shard_map/pallas_call | solution.py:152
  (33 shorter events, 0.3 us)
Async XLA Ops:
  3.3 7.5 %copy-start.14 = (s32[2,5]{1,0:T(2,128)S(1)}, s32[2,5]{1,0:T(2,128)}, u32[]{:S(2)}) copy-start(s32[2,5]{1,0:T(2,128)} %param.19) | copy-start | bytes 124
  3.3 7.5 %copy-start = (f32[48,1,3456]{2,1,0:T(1,128)S(1)}, f32[48,1,3456]{2,1,0:T(1,128)}, u32[]{:S(2)}) copy-start(f32[48,1,3456]{2,1,0:T(1,128)} %param.13) | copy-start | bytes 1990660
  3.3 31.8 %all-to-all-start = ((f32[8,240,128]{2,1,0:T(8,128)}), f32[8,240,128]{2,1,0:T(8,128)S(1)}, u32[]{:S(2)}, u32[]{:S(2)}) async-start(f32[8,240,128]{2,1,0:T(8,128)} %shard_map.188), calls=%async_computation | async-start | bytes 1966080 | tf_op jit(solution)/shard_map/all_to_all | solution.py:223
  10.8 0.9 copy-start.4
  11.8 1.1 copy-start.5
  12.9 1.1 copy-start.6
  17.9 1.2 copy-start.1
  35.1 3.7 %copy-start.8 = (s32[24]{0:T(128)S(1)}, s32[24]{0:T(128)}, u32[]{:S(2)}) copy-start(s32[24]{0:T(128)} %constant.45.clone.edges_ref) | copy-start | bytes 292
  35.1 43.0 %all-to-all-start.1 = ((f32[8,408,128]{2,1,0:T(8,128)}), f32[8,408,128]{2,1,0:T(8,128)S(1)}, u32[]{:S(2)}, u32[]{:S(2)}) async-start(f32[8,408,128]{2,1,0:T(8,128)} %copy-done.1), calls=%async_computation.1 | async-start | bytes 3342336 | tf_op jit(solution)/shard_map/all_to_all | solution.py:223
  38.9 20.7 %copy-start.7 = (f32[48,1,960]{2,1,0:T(1,128)S(1)}, f32[48,1,960]{2,1,0:T(1,128)}, u32[]{:S(2)}) copy-start(f32[48,1,960]{2,1,0:T(1,128)} %gram_ref.1) | copy-start | bytes 552964
  38.9 20.7 %copy-start.9 = (s32[16]{0:T(128)S(1)}, s32[16]{0:T(128)}, u32[]{:S(2)}) copy-start(s32[16]{0:T(128)} %constant.46.clone.slot_ref) | copy-start | bytes 196
  41.2 29.1 %copy-start.2 = (f32[8,72,128]{2,1,0:T(8,128)}, f32[8,72,128]{2,1,0:T(8,128)S(1)}, u32[]{:S(2)}) copy-start(f32[8,72,128]{2,1,0:T(8,128)S(1)} %get-tuple-element.68.own_ref) | copy-start | bytes 884740
  41.2 2.1 %collective-permute-start = (f32[2,8,72,128]{3,2,1,0:T(8,128)S(1)}, f32[2,8,72,128]{3,2,1,0:T(8,128)S(1)}, u32[]{:S(2)}, u32[]{:S(2)}) collective-permute-start(f32[2,8,72,128]{3,2,1,0:T(8,128)S(1)} %get-tuple-element.56), channel_id=1, source_target_pairs={{0,1},{1,0},{2,3},{3,2},{4,5},{5,4},{6,7},{7,6},{8,9},{9,8},{10,11... | collective-permute-start | bytes 1769480 | tf_op jit(solution)/shard_map/ppermute | solution.py:217
  43.4 9.1 %collective-permute-start.1 = (f32[8,72,128]{2,1,0:T(8,128)S(1)}, f32[8,72,128]{2,1,0:T(8,128)S(1)}, u32[]{:S(2)}, u32[]{:S(2)}) collective-permute-start(f32[8,72,128]{2,1,0:T(8,128)S(1)} %get-tuple-element.58), channel_id=1, source_target_pairs={{0,2},{1,3},{2,0},{3,1},{4,6},{5,7},{6,4},{7,5},{8,10},{9,11},{10,... | collective-permute-start | bytes 884744 | tf_op jit(solution)/shard_map/ppermute | solution.py:220
  52.5 17.8 %collective-permute-start.5 = (f32[8,72,128]{2,1,0:T(8,128)S(1)}, f32[8,72,128]{2,1,0:T(8,128)S(1)}, u32[]{:S(2)}, u32[]{:S(2)}) collective-permute-start(f32[8,72,128]{2,1,0:T(8,128)S(1)} %get-tuple-element.68.own_ref), channel_id=1, source_target_pairs={{0,2},{1,3},{2,0},{3,1},{4,6},{5,7},{6,4},{7,5},{8,10},{9,11},{10,... | collective-permute-start | bytes 884744 | tf_op jit(solution)/shard_map/ppermute | solution.py:220
  54.1 5.5 %collective-permute-start.2 = (f32[2,72,128]{2,1,0:T(8,128)S(1)}, f32[2,72,128]{2,1,0:T(8,128)S(1)}, u32[]{:S(2)}, u32[]{:S(2)}) collective-permute-start(f32[2,72,128]{2,1,0:T(8,128)S(1)} %get-tuple-element.65), channel_id=1, source_target_pairs={{0,4},{4,0},{8,12},{12,8},{16,20},{20,16},{24,28},{28,24},{1,5},{5... | collective-permute-start | bytes 221192 | tf_op jit(solution)/shard_map/ppermute | solution.py:458
  56.1 13.5 %collective-permute-start.3 = (f32[2,72,128]{2,1,0:T(8,128)S(1)}, f32[2,72,128]{2,1,0:T(8,128)S(1)}, u32[]{:S(2)}, u32[]{:S(2)}) collective-permute-start(f32[2,72,128]{2,1,0:T(8,128)S(1)} %get-tuple-element.66), channel_id=1, source_target_pairs={{0,8},{4,12},{8,0},{12,4},{16,24},{20,28},{24,16},{28,20},{1,9},{5... | collective-permute-start | bytes 221192 | tf_op jit(solution)/shard_map/ppermute | solution.py:458
  57.5 12.8 %collective-permute-start.4 = (f32[2,72,128]{2,1,0:T(8,128)S(1)}, f32[2,72,128]{2,1,0:T(8,128)S(1)}, u32[]{:S(2)}, u32[]{:S(2)}) collective-permute-start(f32[2,72,128]{2,1,0:T(8,128)S(1)} %get-tuple-element.67), channel_id=1, source_target_pairs={{0,12},{4,8},{8,4},{12,0},{16,28},{20,24},{24,20},{28,16},{1,13},{... | collective-permute-start | bytes 221192 | tf_op jit(solution)/shard_map/ppermute | solution.py:458
  72.1 10.7 %copy-start.3 = (f32[8,72,128]{2,1,0:T(8,128)S(1)}, f32[8,72,128]{2,1,0:T(8,128)}, u32[]{:S(2)}) copy-start(f32[8,72,128]{2,1,0:T(8,128)} %copy-done.2) | copy-start | bytes 884740
  78.1 20.9 %all-to-all-start.2 = ((f32[8,144,128]{2,1,0:T(8,128)}), f32[8,144,128]{2,1,0:T(8,128)}, u32[]{:S(2)}, u32[]{:S(2)}) async-start(f32[8,144,128]{2,1,0:T(8,128)} %shard_map.194), calls=%async_computation.2 | async-start | bytes 1179648 | tf_op jit(solution)/shard_map/all_to_all | solution.py:223
  82.9 2.1 %collective-permute-start.6 = (f32[2,8,72,128]{3,2,1,0:T(8,128)S(1)}, f32[2,8,72,128]{3,2,1,0:T(8,128)S(1)}, u32[]{:S(2)}, u32[]{:S(2)}) collective-permute-start(f32[2,8,72,128]{3,2,1,0:T(8,128)S(1)} %pad_maximum_fusion), channel_id=1, source_target_pairs={{0,1},{1,0},{2,3},{3,2},{4,5},{5,4},{6,7},{7,6},{8,9},{9,8},{10,11... | collective-permute-start | bytes 1769480 | tf_op jit(solution)/shard_map/ppermute | solution.py:217
  99.0 36.6 %all-to-all-start.3 = ((f32[8,336,128]{2,1,0:T(8,128)}), f32[8,336,128]{2,1,0:T(8,128)S(1)}, u32[]{:S(2)}, u32[]{:S(2)}) async-start(f32[8,336,128]{2,1,0:T(8,128)} %shard_map.196), calls=%async_computation.3 | async-start | bytes 2752512 | tf_op jit(solution)/shard_map/all_to_all | solution.py:223
  103.5 3.3 %collective-permute-start.7 = (f32[384,128]{1,0:T(8,128)S(1)}, f32[384,128]{1,0:T(8,128)S(1)}, u32[]{:S(2)}, u32[]{:S(2)}) collective-permute-start(f32[384,128]{1,0:T(8,128)S(1)} %get-tuple-element.79), channel_id=1, source_target_pairs={{0,1},{1,0},{2,3},{3,2},{4,5},{5,4},{6,7},{7,6},{8,9},{9,8},{10,11... | collective-permute-start | bytes 589832 | tf_op jit(solution)/shard_map/ppermute | solution.py:217
  106.2 2.3 %collective-permute-start.9 = (f32[384,128]{1,0:T(8,128)S(1)}, f32[384,128]{1,0:T(8,128)S(1)}, u32[]{:S(2)}, u32[]{:S(2)}) collective-permute-start(f32[384,128]{1,0:T(8,128)S(1)} %get-tuple-element.82), channel_id=1, source_target_pairs={{0,1},{1,0},{2,3},{3,2},{4,5},{5,4},{6,7},{7,6},{8,9},{9,8},{10,11... | collective-permute-start | bytes 589832 | tf_op jit(solution)/shard_map/ppermute | solution.py:217
  106.9 24.0 %copy-start.10 = (f32[360]{0:T(512)S(1)}, f32[360]{0:T(512)}, u32[]{:S(2)}) copy-start(f32[360]{0:T(512)} %param.21) | copy-start | bytes 4324
  106.9 24.0 %copy-start.11 = (f32[360]{0:T(512)S(1)}, f32[360]{0:T(512)}, u32[]{:S(2)}) copy-start(f32[360]{0:T(512)} %param.20) | copy-start | bytes 4324
  106.9 24.0 %copy-start.12 = (f32[360]{0:T(512)S(1)}, f32[360]{0:T(512)}, u32[]{:S(2)}) copy-start(f32[360]{0:T(512)} %param.22) | copy-start | bytes 4324
  106.9 24.0 %copy-start.13 = (f32[360]{0:T(512)S(1)}, f32[360]{0:T(512)}, u32[]{:S(2)}) copy-start(f32[360]{0:T(512)} %param.23) | copy-start | bytes 4324
  107.0 9.9 %collective-permute-start.8 = (f32[8,72,128]{2,1,0:T(8,128)S(1)}, f32[8,72,128]{2,1,0:T(8,128)S(1)}, u32[]{:S(2)}, u32[]{:S(2)}) collective-permute-start(f32[8,72,128]{2,1,0:T(8,128)S(1)} %shard_map.198.basis_half_ref), channel_id=1, source_target_pairs={{0,2},{1,3},{2,0},{3,1},{4,6},{5,7},{6,4},{7,5},{8,10},{9,11},{10,... | collective-permute-start | bytes 884744 | tf_op jit(solution)/shard_map/ppermute | solution.py:220
  108.7 13.6 %collective-permute-start.10 = (f32[8,72,128]{2,1,0:T(8,128)S(1)}, f32[8,72,128]{2,1,0:T(8,128)S(1)}, u32[]{:S(2)}, u32[]{:S(2)}) collective-permute-start(f32[8,72,128]{2,1,0:T(8,128)S(1)} %shard_map.200.gram_half_ref), channel_id=1, source_target_pairs={{0,2},{1,3},{2,0},{3,1},{4,6},{5,7},{6,4},{7,5},{8,10},{9,11},{10,... | collective-permute-start | bytes 884744 | tf_op jit(solution)/shard_map/ppermute | solution.py:220
  130.8 1.4 %collective-permute-start.11 = (f32[96,384]{1,0:T(8,128)S(1)}, f32[96,384]{1,0:T(8,128)S(1)}, u32[]{:S(2)}, u32[]{:S(2)}) collective-permute-start(f32[96,384]{1,0:T(8,128)S(1)} %get-tuple-element.84), channel_id=1, source_target_pairs={{0,1},{1,0},{2,3},{3,2},{4,5},{5,4},{6,7},{7,6},{8,9},{9,8},{10,11... | collective-permute-start | bytes 442376 | tf_op jit(solution)/shard_map/ppermute | solution.py:217

commit v6 on v5

--- a/solution.py
+++ b/solution.py
@@ -466,8 +466,8 @@
 
 
     def split_owned(rank_ref, came_ref, *refs):
-        spread = len(refs) == 4
-        mine_ref, other_ref = refs[-3:-1] if spread else refs
+        spread = len(refs) == 3
+        mine_ref, other_ref = refs[-2:]
         odd = rank_ref[0] % 2 == 1
         for block_at in range(shards):
             at = slice(block_at * rows, (block_at + 1) * rows)
@@ -483,10 +483,7 @@
             other_ref[at, 0:columns] = jnp.where(odd, strips[0], strips[1])
             if spread:
                 for m in range(MCAP):
-                    refs[-1][m, at, 0:columns] = strips[m]
-        if spread:
-            for m in range(MCAP):
-                refs[0][m] = refs[-1][m].T[0:columns]
+                    refs[0][m, at, 0:columns] = strips[m]
 
     def join_half(rank_ref, mine_ref, other_ref, half_ref):
         odd = rank_ref[0] % 2 == 1
@@ -499,10 +496,9 @@
     def collect(came, spread):
         *strips, mine, other = call(
             split_owned,
-            [(MCAP, columns, width)] * spread + [(width, LANES), (width, LANES)],
+            [(MCAP, width, LANES)] * spread + [(width, LANES), (width, LANES)],
             (rank_arg, came),
             specs=[SMEM, None],
-            scratch=[pltpu.VMEM((MCAP, width, LANES), F32)] * spread,
         )
         half = call(
             join_half,
@@ -652,7 +648,13 @@
     came_five = exchange(send_five)
 
 
-    gram_out, gram_half, gram_far = collect(came_four, 1)
+    gram_strips, gram_half, gram_far = collect(came_four, 1)
+
+    def turn_strips(strips_ref, out_ref):
+        for m in range(MCAP):
+            out_ref[m] = strips_ref[m].T[0:columns]
+
+    gram_out = call(turn_strips, (MCAP, columns, width), (gram_strips,))
 
     def refresh(
         rank_ref,

time: 138 us -> 138 us (level)
  waiting for transfers between devices: 65.7 us -> 64 us
  local copies, waits for them, and re-layouts: 4.45 us -> 6.12 us
    unnamed x30 -> x34, local copies, waits for them, and re-layouts: 4.37 us -> 6.04 us
    pallas_call x15 -> x16, Pallas kernels: 35.7 us -> 35.7 us  [call(): pl.pallas_call(kernel, out_shape=shapes, grid=grid, in_specs=[s or vmem f...]
  transfers between devices with their start and end apart: 16 -> 16, of which waited for: 13 -> 12; matrix products, arithmetic and copies ran while one was open for 1% -> 1% of each run, Pallas kernels for 23% -> 23%
where the time goes in v6:
time: 138 us
  waiting for transfers between devices  64 us (46%)
  Pallas kernels  35.7 us (26%)
  starting transfers between devices  29.5 us (21%)
  local copies, waits for them, and re-layouts  6.12 us (4%)
    pallas_call x16, Pallas kernels, call(): pl.pallas_call(kernel, out_shape=shapes, grid=grid, in_specs=[s or vmem f...  35.7 us
    all_to_all x4, waiting for transfers between devices, exchange(): lax.all_to_all(value, 'shard', split_axis=0, concat_axis=0, tiled=True)  28 us
    ppermute x4, waiting for transfers between devices, over_chip(): return lax.ppermute(value, 'tensor', chip_pairs)  20.3 us
    all_to_all x4, starting transfers between devices, exchange(): lax.all_to_all(value, 'shard', split_axis=0, concat_axis=0, tiled=True)  19.6 us
    ppermute x3, waiting for transfers between devices, body(): lax.ppermute(gram_blocks[k], 'shard', [(s, s ^ k) for s in range(shards)])  11.8 us
    unnamed x34, local copies, waits for them, and re-layouts  6.04 us
    ppermute x4, starting transfers between devices, over_chip(): return lax.ppermute(value, 'tensor', chip_pairs)  5.54 us
    ppermute x5, waiting for transfers between devices, over_core(): return lax.ppermute(value, 'tensor', core_pairs)  3.99 us
  transfers between devices with their start and end apart: 16, of which 12 were waited for; matrix products, arithmetic and copies ran while one was open for 1% of the time, Pallas kernels for 23%

profile of v6, /device:TPU:0, one launch (start us, length us, event | category | flops | bytes accessed | tf_op | source)
XLA Modules:
  0.0 137.6 jit_solution(6347245014152757366)
XLA Ops:
  0.6 2.7 %shard_map.188 = f32[8,240,128]{2,1,0:T(8,128)} custom-call(f32[1296,128]{1,0:T(8,128)} %bitcast.19, f32[48,1,960]{2,1,0:T(1,128)} %basis_ref.3), custom_call_target="tpu_custom_call" | custom-call | tf_op jit(solution)/shard_map/pallas_call | solution.py:152
  3.3 7.4 %all-to-all-start = ((f32[8,240,128]{2,1,0:T(8,128)}), f32[8,240,128]{2,1,0:T(8,128)S(1)}, u32[]{:S(2)}, u32[]{:S(2)}) async-start(f32[8,240,128]{2,1,0:T(8,128)} %shard_map.188), calls=%async_computation | async-start | bytes 1966080 | tf_op jit(solution)/shard_map/all_to_all | solution.py:223
  10.8 0.1 reshape.47.owner_ref
  10.9 0.9 copy-done.4
  11.8 1.1 copy-done.5
  12.9 1.1 copy-done.6
  14.0 3.9 %shard_map.189 = (f32[8,408,128]{2,1,0:T(8,128)S(1)}, f32[1296,128]{1,0:T(8,128)}, s32[16]{0:T(128)S(1)}) custom-call(s32[10]{0:T(128)S(1)} %reshape.47.owner_ref, f32[1296,128]{1,0:T(8,128)S(1)} %bitcast.23, f32[1296,128]{1,0:T(8,128)S(1)} %bitcast.24, f32[1296,128]{1,0:T(8,128)S(1)} %bitcast.20, f32[48,1,960]{2,1,0:T(1,128)S(1)} %copy-done.4), custom_call_target="tpu_custom_call" | custom-call | tf_op jit(solution)/shard_map/pallas_call | solution.py:152
  17.9 1.2 copy-done.1
  19.1 16.1 %all-to-all-done.came_ref = f32[8,240,128]{2,1,0:T(8,128)S(1)} async-done(((f32[8,240,128]{2,1,0:T(8,128)}), f32[8,240,128]{2,1,0:T(8,128)S(1)}, u32[]{:S(2)}, u32[]{:S(2)}) %all-to-all-start) | async-done | bytes 983072 | tf_op jit(solution)/shard_map/all_to_all | solution.py:223
  35.2 3.7 %all-to-all-start.1 = ((f32[8,408,128]{2,1,0:T(8,128)}), f32[8,408,128]{2,1,0:T(8,128)S(1)}, u32[]{:S(2)}, u32[]{:S(2)}) async-start(f32[8,408,128]{2,1,0:T(8,128)} %copy-done.1), calls=%async_computation.1 | async-start | bytes 3342336 | tf_op jit(solution)/shard_map/all_to_all | solution.py:223
  38.9 2.3 %shard_map.190 = (f32[384,512]{1,0:T(8,128)S(1)}, f32[8,72,128]{2,1,0:T(8,128)S(1)}, f32[2,8,72,128]{3,2,1,0:T(8,128)S(1)}, f32[2,8,72,128]{3,2,1,0:T(8,128)S(1)}) custom-call(s32[1]{0:T(128)} %bitcast.3.group_ref, s32[1]{0:T(128)} %bitcast.4.rank_ref, s32[24]{0:T(128)S(1)} %copy-done.10, f32[8,240,128]{2,1,0:T(8,128)S(1)} %all-to-all-done.came_ref), custom_call_target="tpu_custom_call" | custom-call | tf_op jit(solution)/shard_map/pallas_call | solution.py:152
  41.3 2.0 %collective-permute-done.came_ref = f32[2,8,72,128]{3,2,1,0:T(8,128)S(1)} collective-permute-done((f32[2,8,72,128]{3,2,1,0:T(8,128)S(1)}, f32[2,8,72,128]{3,2,1,0:T(8,128)S(1)}, u32[]{:S(2)}, u32[]{:S(2)}) %collective-permute-start) | collective-permute-done | bytes 589856 | tf_op jit(solution)/shard_map/ppermute | solution.py:217
  43.3 0.1 shard_map.191
  43.4 1.6 %collective-permute-start.1 = (f32[8,72,128]{2,1,0:T(8,128)S(1)}, f32[8,72,128]{2,1,0:T(8,128)S(1)}, u32[]{:S(2)}, u32[]{:S(2)}) collective-permute-start(f32[8,72,128]{2,1,0:T(8,128)S(1)} %get-tuple-element.58), channel_id=1, source_target_pairs={{0,2},{1,3},{2,0},{3,1},{4,6},{5,7},{6,4},{7,5},{8,10},{9,11},{10,... | collective-permute-start | bytes 884744 | tf_op jit(solution)/shard_map/ppermute | solution.py:220
  45.0 7.6 %collective-permute-done.1.came_ref = f32[8,72,128]{2,1,0:T(8,128)S(1)} collective-permute-done((f32[8,72,128]{2,1,0:T(8,128)S(1)}, f32[8,72,128]{2,1,0:T(8,128)S(1)}, u32[]{:S(2)}, u32[]{:S(2)}) %collective-permute-start.1) | collective-permute-done | bytes 294944 | tf_op jit(solution)/shard_map/ppermute | solution.py:220
  52.6 1.6 %collective-permute-start.5 = (f32[8,72,128]{2,1,0:T(8,128)S(1)}, f32[8,72,128]{2,1,0:T(8,128)S(1)}, u32[]{:S(2)}, u32[]{:S(2)}) collective-permute-start(f32[8,72,128]{2,1,0:T(8,128)S(1)} %get-tuple-element.68.own_ref), channel_id=1, source_target_pairs={{0,2},{1,3},{2,0},{3,1},{4,6},{5,7},{6,4},{7,5},{8,10},{9,11},{10,... | collective-permute-start | bytes 884744 | tf_op jit(solution)/shard_map/ppermute | solution.py:220
  54.1 2.0 %collective-permute-start.2 = (f32[2,72,128]{2,1,0:T(8,128)S(1)}, f32[2,72,128]{2,1,0:T(8,128)S(1)}, u32[]{:S(2)}, u32[]{:S(2)}) collective-permute-start(f32[2,72,128]{2,1,0:T(8,128)S(1)} %get-tuple-element.65), channel_id=1, source_target_pairs={{0,4},{4,0},{8,12},{12,8},{16,20},{20,16},{24,28},{28,24},{1,5},{5... | collective-permute-start | bytes 221192 | tf_op jit(solution)/shard_map/ppermute | solution.py:458
  56.1 1.5 %collective-permute-start.3 = (f32[2,72,128]{2,1,0:T(8,128)S(1)}, f32[2,72,128]{2,1,0:T(8,128)S(1)}, u32[]{:S(2)}, u32[]{:S(2)}) collective-permute-start(f32[2,72,128]{2,1,0:T(8,128)S(1)} %get-tuple-element.66), channel_id=1, source_target_pairs={{0,8},{4,12},{8,0},{12,4},{16,24},{20,28},{24,16},{28,20},{1,9},{5... | collective-permute-start | bytes 221192 | tf_op jit(solution)/shard_map/ppermute | solution.py:458
  57.6 2.0 %collective-permute-done.2.refs_1_ = f32[2,72,128]{2,1,0:T(8,128)S(1)} collective-permute-done((f32[2,72,128]{2,1,0:T(8,128)S(1)}, f32[2,72,128]{2,1,0:T(8,128)S(1)}, u32[]{:S(2)}, u32[]{:S(2)}) %collective-permute-start.2) | collective-permute-done | bytes 73760 | tf_op jit(solution)/shard_map/ppermute | solution.py:458
  59.6 0.9 shard_map.193.refs_0_
  60.5 9.0 %collective-permute-done.3.refs_1_ = f32[2,72,128]{2,1,0:T(8,128)S(1)} collective-permute-done((f32[2,72,128]{2,1,0:T(8,128)S(1)}, f32[2,72,128]{2,1,0:T(8,128)S(1)}, u32[]{:S(2)}, u32[]{:S(2)}) %collective-permute-start.3) | collective-permute-done | bytes 73760 | tf_op jit(solution)/shard_map/ppermute | solution.py:458
  69.6 0.8 collective-permute-done.4.refs_2_
  70.4 1.8 %shard_map.194 = f32[8,144,128]{2,1,0:T(8,128)} custom-call(s32[1]{0:T(128)} %bitcast.3.group_ref, s32[16]{0:T(128)S(1)} %get-tuple-element.53.table_ref, s32[16]{0:T(128)S(1)} %copy-done.11, f32[2,11,48,96]{3,2,1,0:T(8,128)S(1)} %shard_map.193.refs_0_, f32[2,72,128]{2,1,0:T(8,128)S(1)} %collective-permute-done.3.refs_1_, ...), custom_call_target="tpu_custom_call" | custom-call | tf_op jit(solution)/shard_map/pallas_call | solution.py:152
  72.1 6.0 %all-to-all-done.1.came_ref = f32[8,408,128]{2,1,0:T(8,128)S(1)} async-done(((f32[8,408,128]{2,1,0:T(8,128)}), f32[8,408,128]{2,1,0:T(8,128)S(1)}, u32[]{:S(2)}, u32[]{:S(2)}) %all-to-all-start.1) | async-done | bytes 1671200 | tf_op jit(solution)/shard_map/all_to_all | solution.py:223
  78.1 4.7 %all-to-all-start.2 = ((f32[8,144,128]{2,1,0:T(8,128)}), f32[8,144,128]{2,1,0:T(8,128)}, u32[]{:S(2)}, u32[]{:S(2)}) async-start(f32[8,144,128]{2,1,0:T(8,128)} %shard_map.194), calls=%async_computation.2 | async-start | bytes 1179648 | tf_op jit(solution)/shard_map/all_to_all | solution.py:223
  83.0 2.0 %collective-permute-done.6.pair_ref = f32[2,8,72,128]{3,2,1,0:T(8,128)S(1)} collective-permute-done((f32[2,8,72,128]{3,2,1,0:T(8,128)S(1)}, f32[2,8,72,128]{3,2,1,0:T(8,128)S(1)}, u32[]{:S(2)}, u32[]{:S(2)}) %collective-permute-start.6) | collective-permute-done | bytes 589856 | tf_op jit(solution)/shard_map/ppermute | solution.py:217
  85.0 3.5 %shard_map.195 = (f32[2,384,384]{2,1,0:T(8,128)S(1)}, f32[384,512]{1,0:T(8,128)S(1)}) custom-call(s32[1]{0:T(128)} %bitcast.3.group_ref, s32[1]{0:T(128)} %bitcast.4.rank_ref, s32[24]{0:T(128)S(1)} %copy-done.10, f32[8,72,128]{2,1,0:T(8,128)S(1)} %copy-done.3, f32[8,72,128]{2,1,0:T(8,128)S(1)} %collective-permute-done.5.chip_ref, ...), custom_call_target="tpu_custom_call" | custom-call | tf_op jit(solution)/shard_map/pallas_call | solution.py:152
  88.5 6.3 %shard_map.196 = f32[8,336,128]{2,1,0:T(8,128)} custom-call(s32[1]{0:T(128)} %bitcast.3.group_ref, s32[24]{0:T(128)S(1)} %copy-done.10, f32[8,408,128]{2,1,0:T(8,128)S(1)} %all-to-all-done.1.came_ref, f32[384,512]{1,0:T(8,128)S(1)} %get-tuple-element.73.grad_ref, f32[384,512]{1,0:T(8,128)S(1)} %get-tuple-element.75.hat_ref, ...), custom_call_target="tpu_custom_call" | custom-call | tf_op jit(solution)/shard_map/pallas_call | solution.py:152
  94.8 4.3 %all-to-all-done.2.came_ref = f32[8,144,128]{2,1,0:T(8,128)} async-done(((f32[8,144,128]{2,1,0:T(8,128)}), f32[8,144,128]{2,1,0:T(8,128)}, u32[]{:S(2)}, u32[]{:S(2)}) %all-to-all-start.2) | async-done | bytes 589856 | tf_op jit(solution)/shard_map/all_to_all | solution.py:223
  99.0 3.8 %all-to-all-start.3 = ((f32[8,336,128]{2,1,0:T(8,128)}), f32[8,336,128]{2,1,0:T(8,128)S(1)}, u32[]{:S(2)}, u32[]{:S(2)}) async-start(f32[8,336,128]{2,1,0:T(8,128)} %shard_map.196), calls=%async_computation.3 | async-start | bytes 2752512 | tf_op jit(solution)/shard_map/all_to_all | solution.py:223
  102.8 0.7 shard_map.197
  103.5 0.1 collective-permute-start.7
  103.6 1.8 %shard_map.199 = (f32[2,384,128]{2,1,0:T(8,128)S(1)}, f32[384,128]{1,0:T(8,128)S(1)}, f32[384,128]{1,0:T(8,128)S(1)}) custom-call(s32[1]{0:T(128)} %bitcast.4.rank_ref, f32[8,144,128]{2,1,0:T(8,128)} %all-to-all-done.2.came_ref), custom_call_target="tpu_custom_call" | custom-call | tf_op jit(solution)/shard_map/pallas_call | solution.py:152
  105.4 0.6 collective-permute-start.9
  105.9 0.2 shard_map.198.basis_half_ref
  106.1 1.6 %collective-permute-start.8 = (f32[8,72,128]{2,1,0:T(8,128)S(1)}, f32[8,72,128]{2,1,0:T(8,128)S(1)}, u32[]{:S(2)}, u32[]{:S(2)}) collective-permute-start(f32[8,72,128]{2,1,0:T(8,128)S(1)} %shard_map.198.basis_half_ref), channel_id=1, source_target_pairs={{0,2},{1,3},{2,0},{3,1},{4,6},{5,7},{6,4},{7,5},{8,10},{9,11},{10,... | collective-permute-start | bytes 884744 | tf_op jit(solution)/shard_map/ppermute | solution.py:220
  107.7 0.2 shard_map.200.gram_half_ref
  107.9 0.9 collective-permute-start.10
  108.7 7.3 %collective-permute-done.8.basis_far_ref = f32[8,72,128]{2,1,0:T(8,128)S(1)} collective-permute-done((f32[8,72,128]{2,1,0:T(8,128)S(1)}, f32[8,72,128]{2,1,0:T(8,128)S(1)}, u32[]{:S(2)}, u32[]{:S(2)}) %collective-permute-start.8) | collective-permute-done | bytes 294944 | tf_op jit(solution)/shard_map/ppermute | solution.py:220
  116.1 5.4 %collective-permute-done.10.gram_far_ref = f32[8,72,128]{2,1,0:T(8,128)S(1)} collective-permute-done((f32[8,72,128]{2,1,0:T(8,128)S(1)}, f32[8,72,128]{2,1,0:T(8,128)S(1)}, u32[]{:S(2)}, u32[]{:S(2)}) %collective-permute-start.10) | collective-permute-done | bytes 294944 | tf_op jit(solution)/shard_map/ppermute | solution.py:220
  121.5 0.7 copy-done.7
  122.2 1.0 copy-done.8
  123.1 8.6 %shard_map.201 = (f32[96,384]{1,0:T(8,128)S(1)}, f32[96,384]{1,0:T(8,128)S(1)}, f32[1296,128]{1,0:T(8,128)S(1)}) custom-call(s32[1]{0:T(128)} %bitcast.4.rank_ref, f32[8,72,128]{2,1,0:T(8,128)S(1)} %shard_map.198.basis_half_ref, f32[8,72,128]{2,1,0:T(8,128)S(1)} %collective-permute-done.8.basis_far_ref, f32[8,72,128]{2,1,0:T(8,128)S(1)} %shard_map.200.gram_half_ref, ...), custom_call_target="tpu_custom_call" | custom-call | tf_op jit(solution)/shard_map/pallas_call | solution.py:152
  131.8 0.6 multiply_subtract_fusion
  132.4 0.9 shard_map.202
  133.3 0.7 maximum_select_fusion
  134.0 1.6 %all-to-all-done.3.came_ref = f32[8,336,128]{2,1,0:T(8,128)S(1)} async-done(((f32[8,336,128]{2,1,0:T(8,128)}), f32[8,336,128]{2,1,0:T(8,128)S(1)}, u32[]{:S(2)}, u32[]{:S(2)}) %all-to-all-start.3) | async-done | bytes 1376288 | tf_op jit(solution)/shard_map/all_to_all | solution.py:223
  135.7 1.9 %shard_map.203 = (f32[1296,128]{1,0:T(8,128)}, f32[1296,128]{1,0:T(8,128)}) custom-call(f32[8,336,128]{2,1,0:T(8,128)S(1)} %all-to-all-done.3.came_ref, f32[1296,128]{1,0:T(8,128)S(1)} %get-tuple-element.88.weight_ref), custom_call_target="tpu_custom_call" | custom-call | tf_op jit(solution)/shard_map/pallas_call | solution.py:152
  (38 shorter events, 0.4 us)
Async XLA Ops:
  3.3 7.5 %copy-start.16 = (s32[2,5]{1,0:T(2,128)S(1)}, s32[2,5]{1,0:T(2,128)}, u32[]{:S(2)}) copy-start(s32[2,5]{1,0:T(2,128)} %param.19) | copy-start | bytes 124
  3.3 7.5 %copy-start = (f32[48,1,3456]{2,1,0:T(1,128)S(1)}, f32[48,1,3456]{2,1,0:T(1,128)}, u32[]{:S(2)}) copy-start(f32[48,1,3456]{2,1,0:T(1,128)} %param.13) | copy-start | bytes 1990660
  3.3 31.8 %all-to-all-start = ((f32[8,240,128]{2,1,0:T(8,128)}), f32[8,240,128]{2,1,0:T(8,128)S(1)}, u32[]{:S(2)}, u32[]{:S(2)}) async-start(f32[8,240,128]{2,1,0:T(8,128)} %shard_map.188), calls=%async_computation | async-start | bytes 1966080 | tf_op jit(solution)/shard_map/all_to_all | solution.py:223
  10.9 0.9 copy-start.4
  11.8 1.1 copy-start.5
  12.9 1.1 copy-start.6
  17.9 1.2 copy-start.1
  35.2 3.7 %copy-start.10 = (s32[24]{0:T(128)S(1)}, s32[24]{0:T(128)}, u32[]{:S(2)}) copy-start(s32[24]{0:T(128)} %constant.45.clone.edges_ref) | copy-start | bytes 292
  35.2 43.0 %all-to-all-start.1 = ((f32[8,408,128]{2,1,0:T(8,128)}), f32[8,408,128]{2,1,0:T(8,128)S(1)}, u32[]{:S(2)}, u32[]{:S(2)}) async-start(f32[8,408,128]{2,1,0:T(8,128)} %copy-done.1), calls=%async_computation.1 | async-start | bytes 3342336 | tf_op jit(solution)/shard_map/all_to_all | solution.py:223
  38.9 20.7 %copy-start.9 = (f32[48,1,960]{2,1,0:T(1,128)S(1)}, f32[48,1,960]{2,1,0:T(1,128)}, u32[]{:S(2)}) copy-start(f32[48,1,960]{2,1,0:T(1,128)} %gram_ref.1) | copy-start | bytes 552964
  38.9 20.7 %copy-start.11 = (s32[16]{0:T(128)S(1)}, s32[16]{0:T(128)}, u32[]{:S(2)}) copy-start(s32[16]{0:T(128)} %constant.46.clone.slot_ref) | copy-start | bytes 196
  41.2 29.1 %copy-start.2 = (f32[8,72,128]{2,1,0:T(8,128)}, f32[8,72,128]{2,1,0:T(8,128)S(1)}, u32[]{:S(2)}) copy-start(f32[8,72,128]{2,1,0:T(8,128)S(1)} %get-tuple-element.68.own_ref) | copy-start | bytes 884740
  41.2 2.1 %collective-permute-start = (f32[2,8,72,128]{3,2,1,0:T(8,128)S(1)}, f32[2,8,72,128]{3,2,1,0:T(8,128)S(1)}, u32[]{:S(2)}, u32[]{:S(2)}) collective-permute-start(f32[2,8,72,128]{3,2,1,0:T(8,128)S(1)} %get-tuple-element.56), channel_id=1, source_target_pairs={{0,1},{1,0},{2,3},{3,2},{4,5},{5,4},{6,7},{7,6},{8,9},{9,8},{10,11... | collective-permute-start | bytes 1769480 | tf_op jit(solution)/shard_map/ppermute | solution.py:217
  43.4 9.1 %collective-permute-start.1 = (f32[8,72,128]{2,1,0:T(8,128)S(1)}, f32[8,72,128]{2,1,0:T(8,128)S(1)}, u32[]{:S(2)}, u32[]{:S(2)}) collective-permute-start(f32[8,72,128]{2,1,0:T(8,128)S(1)} %get-tuple-element.58), channel_id=1, source_target_pairs={{0,2},{1,3},{2,0},{3,1},{4,6},{5,7},{6,4},{7,5},{8,10},{9,11},{10,... | collective-permute-start | bytes 884744 | tf_op jit(solution)/shard_map/ppermute | solution.py:220
  52.6 17.8 %collective-permute-start.5 = (f32[8,72,128]{2,1,0:T(8,128)S(1)}, f32[8,72,128]{2,1,0:T(8,128)S(1)}, u32[]{:S(2)}, u32[]{:S(2)}) collective-permute-start(f32[8,72,128]{2,1,0:T(8,128)S(1)} %get-tuple-element.68.own_ref), channel_id=1, source_target_pairs={{0,2},{1,3},{2,0},{3,1},{4,6},{5,7},{6,4},{7,5},{8,10},{9,11},{10,... | collective-permute-start | bytes 884744 | tf_op jit(solution)/shard_map/ppermute | solution.py:220
  54.1 5.5 %collective-permute-start.2 = (f32[2,72,128]{2,1,0:T(8,128)S(1)}, f32[2,72,128]{2,1,0:T(8,128)S(1)}, u32[]{:S(2)}, u32[]{:S(2)}) collective-permute-start(f32[2,72,128]{2,1,0:T(8,128)S(1)} %get-tuple-element.65), channel_id=1, source_target_pairs={{0,4},{4,0},{8,12},{12,8},{16,20},{20,16},{24,28},{28,24},{1,5},{5... | collective-permute-start | bytes 221192 | tf_op jit(solution)/shard_map/ppermute | solution.py:458
  56.1 13.5 %collective-permute-start.3 = (f32[2,72,128]{2,1,0:T(8,128)S(1)}, f32[2,72,128]{2,1,0:T(8,128)S(1)}, u32[]{:S(2)}, u32[]{:S(2)}) collective-permute-start(f32[2,72,128]{2,1,0:T(8,128)S(1)} %get-tuple-element.66), channel_id=1, source_target_pairs={{0,8},{4,12},{8,0},{12,4},{16,24},{20,28},{24,16},{28,20},{1,9},{5... | collective-permute-start | bytes 221192 | tf_op jit(solution)/shard_map/ppermute | solution.py:458
  57.5 12.8 %collective-permute-start.4 = (f32[2,72,128]{2,1,0:T(8,128)S(1)}, f32[2,72,128]{2,1,0:T(8,128)S(1)}, u32[]{:S(2)}, u32[]{:S(2)}) collective-permute-start(f32[2,72,128]{2,1,0:T(8,128)S(1)} %get-tuple-element.67), channel_id=1, source_target_pairs={{0,12},{4,8},{8,4},{12,0},{16,28},{20,24},{24,20},{28,16},{1,13},{... | collective-permute-start | bytes 221192 | tf_op jit(solution)/shard_map/ppermute | solution.py:458
  72.1 10.7 %copy-start.3 = (f32[8,72,128]{2,1,0:T(8,128)S(1)}, f32[8,72,128]{2,1,0:T(8,128)}, u32[]{:S(2)}) copy-start(f32[8,72,128]{2,1,0:T(8,128)} %copy-done.2) | copy-start | bytes 884740
  78.1 20.9 %all-to-all-start.2 = ((f32[8,144,128]{2,1,0:T(8,128)}), f32[8,144,128]{2,1,0:T(8,128)}, u32[]{:S(2)}, u32[]{:S(2)}) async-start(f32[8,144,128]{2,1,0:T(8,128)} %shard_map.194), calls=%async_computation.2 | async-start | bytes 1179648 | tf_op jit(solution)/shard_map/all_to_all | solution.py:223
  82.9 2.1 %collective-permute-start.6 = (f32[2,8,72,128]{3,2,1,0:T(8,128)S(1)}, f32[2,8,72,128]{3,2,1,0:T(8,128)S(1)}, u32[]{:S(2)}, u32[]{:S(2)}) collective-permute-start(f32[2,8,72,128]{3,2,1,0:T(8,128)S(1)} %pad_maximum_fusion), channel_id=1, source_target_pairs={{0,1},{1,0},{2,3},{3,2},{4,5},{5,4},{6,7},{7,6},{8,9},{9,8},{10,11... | collective-permute-start | bytes 1769480 | tf_op jit(solution)/shard_map/ppermute | solution.py:217
  99.0 36.6 %all-to-all-start.3 = ((f32[8,336,128]{2,1,0:T(8,128)}), f32[8,336,128]{2,1,0:T(8,128)S(1)}, u32[]{:S(2)}, u32[]{:S(2)}) async-start(f32[8,336,128]{2,1,0:T(8,128)} %shard_map.196), calls=%async_computation.3 | async-start | bytes 2752512 | tf_op jit(solution)/shard_map/all_to_all | solution.py:223
  103.5 2.4 %collective-permute-start.7 = (f32[384,128]{1,0:T(8,128)S(1)}, f32[384,128]{1,0:T(8,128)S(1)}, u32[]{:S(2)}, u32[]{:S(2)}) collective-permute-start(f32[384,128]{1,0:T(8,128)S(1)} %get-tuple-element.79), channel_id=1, source_target_pairs={{0,1},{1,0},{2,3},{3,2},{4,5},{5,4},{6,7},{7,6},{8,9},{9,8},{10,11... | collective-permute-start | bytes 589832 | tf_op jit(solution)/shard_map/ppermute | solution.py:217
  105.4 2.4 %collective-permute-start.9 = (f32[384,128]{1,0:T(8,128)S(1)}, f32[384,128]{1,0:T(8,128)S(1)}, u32[]{:S(2)}, u32[]{:S(2)}) collective-permute-start(f32[384,128]{1,0:T(8,128)S(1)} %get-tuple-element.82), channel_id=1, source_target_pairs={{0,1},{1,0},{2,3},{3,2},{4,5},{5,4},{6,7},{7,6},{8,9},{9,8},{10,11... | collective-permute-start | bytes 589832 | tf_op jit(solution)/shard_map/ppermute | solution.py:217
  106.1 25.7 %copy-start.12 = (f32[360]{0:T(512)S(1)}, f32[360]{0:T(512)}, u32[]{:S(2)}) copy-start(f32[360]{0:T(512)} %param.21) | copy-start | bytes 4324
  106.1 25.7 %copy-start.13 = (f32[360]{0:T(512)S(1)}, f32[360]{0:T(512)}, u32[]{:S(2)}) copy-start(f32[360]{0:T(512)} %param.20) | copy-start | bytes 4324
  106.1 25.7 %copy-start.14 = (f32[360]{0:T(512)S(1)}, f32[360]{0:T(512)}, u32[]{:S(2)}) copy-start(f32[360]{0:T(512)} %param.22) | copy-start | bytes 4324
  106.1 25.7 %copy-start.15 = (f32[360]{0:T(512)S(1)}, f32[360]{0:T(512)}, u32[]{:S(2)}) copy-start(f32[360]{0:T(512)} %param.23) | copy-start | bytes 4324
  106.1 9.9 %collective-permute-start.8 = (f32[8,72,128]{2,1,0:T(8,128)S(1)}, f32[8,72,128]{2,1,0:T(8,128)S(1)}, u32[]{:S(2)}, u32[]{:S(2)}) collective-permute-start(f32[8,72,128]{2,1,0:T(8,128)S(1)} %shard_map.198.basis_half_ref), channel_id=1, source_target_pairs={{0,2},{1,3},{2,0},{3,1},{4,6},{5,7},{6,4},{7,5},{8,10},{9,11},{10,... | collective-permute-start | bytes 884744 | tf_op jit(solution)/shard_map/ppermute | solution.py:220
  107.9 13.6 %collective-permute-start.10 = (f32[8,72,128]{2,1,0:T(8,128)S(1)}, f32[8,72,128]{2,1,0:T(8,128)S(1)}, u32[]{:S(2)}, u32[]{:S(2)}) collective-permute-start(f32[8,72,128]{2,1,0:T(8,128)S(1)} %shard_map.200.gram_half_ref), channel_id=1, source_target_pairs={{0,2},{1,3},{2,0},{3,1},{4,6},{5,7},{6,4},{7,5},{8,10},{9,11},{10,... | collective-permute-start | bytes 884744 | tf_op jit(solution)/shard_map/ppermute | solution.py:220
  121.5 0.7 copy-start.7
  122.2 1.0 copy-start.8
  131.7 1.6 %collective-permute-start.11 = (f32[96,384]{1,0:T(8,128)S(1)}, f32[96,384]{1,0:T(8,128)S(1)}, u32[]{:S(2)}, u32[]{:S(2)}) collective-permute-start(f32[96,384]{1,0:T(8,128)S(1)} %get-tuple-element.84), channel_id=1, source_target_pairs={{0,1},{1,0},{2,3},{3,2},{4,5},{5,4},{6,7},{7,6},{8,9},{9,8},{10,11... | collective-permute-start | bytes 442376 | tf_op jit(solution)/shard_map/ppermute | solution.py:217
